TPU v7x, 32 devices: a whole 2x2x4 slice. The times are simulated.
32 devices in a mesh: dp: 8 (over y, x, core), ctx: 4 (over z).
Axes of the slice: x: 2, y: 2, z: 4, core: 2. Of those that a mesh axis runs over, the one named last changes fastest.
Arguments:
- tokens: bfloat16 [4096, 1152], P(('dp', 'ctx')), may hold values from -6 to 6
- cotangent: bfloat16 [4096, 1152], P(('dp', 'ctx')), may hold values from -6 to 6
- lengths: int32 [8, 2], P('dp'), may hold values from 32 to 256, as said below
- w_query: bfloat16 [1152, 1024], P(('dp', 'ctx')), may hold values from -0.1875 to 0.1875
- w_key: bfloat16 [1152, 256], P(('dp', 'ctx')), may hold values from -0.1875 to 0.1875
- w_value: bfloat16 [1152, 256], P(('dp', 'ctx')), may hold values from -0.1875 to 0.1875
- w_out: bfloat16 [1024, 1152], P(('dp', 'ctx')), may hold values from -0.1875 to 0.1875
- w_gate: bfloat16 [1152, 6912], P(('dp', 'ctx')), may hold values from -0.1875 to 0.1875
- w_up: bfloat16 [1152, 6912], P(('dp', 'ctx')), may hold values from -0.1875 to 0.1875
- w_down: bfloat16 [6912, 1152], P(('dp', 'ctx')), may hold values from -0.078125 to 0.078125
- gain_in: bfloat16 [1152], P(('dp', 'ctx')), may hold values from -0.75 to 0.75
- gain_query: bfloat16 [256], P(('dp', 'ctx')), may hold values from -0.75 to 0.75
- gain_key: bfloat16 [256], P(('dp', 'ctx')), may hold values from -0.75 to 0.75
- gain_attn: bfloat16 [1152], P(('dp', 'ctx')), may hold values from -0.75 to 0.75
- gain_pre: bfloat16 [1152], P(('dp', 'ctx')), may hold values from -0.75 to 0.75
- gain_post: bfloat16 [1152], P(('dp', 'ctx')), may hold values from -0.75 to 0.75
Outputs:
- output: bfloat16 [4096, 1152], P(('dp', 'ctx'))
- input_grad: bfloat16 [4096, 1152], P(('dp', 'ctx'))
- grad_query: float32 [1152, 1024], P('dp', 'ctx')
- grad_key: float32 [1152, 256], P('dp', 'ctx')
- grad_value: float32 [1152, 256], P('dp', 'ctx')
- grad_out: float32 [1024, 1152], P('ctx', 'dp')
- grad_gate: float32 [1152, 6912], P('dp', 'ctx')
- grad_up: float32 [1152, 6912], P('dp', 'ctx')
- grad_down: float32 [6912, 1152], P('ctx', 'dp')
- grad_gain_in: float32 [1152], P(('dp', 'ctx'))
- grad_gain_query: float32 [256], P(('dp', 'ctx'))
- grad_gain_key: float32 [256], P(('dp', 'ctx'))
- grad_gain_attn: float32 [1152], P(('dp', 'ctx'))
- grad_gain_pre: float32 [1152], P(('dp', 'ctx'))
- grad_gain_post: float32 [1152], P(('dp', 'ctx'))
Inputs may be any that keep to these rules, and one draw needn't show every extreme that they name: In every row of lengths one sequence, which one drawn from the seed, has length 256.
All inputs are finite; a program needn't handle non-finite values.
Results may differ from a plain program's by a relative error of at most 0.024.
Values may be sent and summed in bfloat16 or wider, within the bound.
No kernel may reach another device: no remote copies, remote signals or barrier semaphores. Data moves between devices by JAX's collectives and lax.ppermute only.
A program may use at most 192 MiB of HBM per device.

v0:
```python
import jax
import jax.numpy as jnp
import numpy as np
from jax import lax
from jax.experimental import pallas as pl
from jax.experimental.pallas import tpu as pltpu
from jax.sharding import PartitionSpec as P

epsilon = 1e-06
rope_base = 1000000.0


def rms_norm(value, weight):
    scale = lax.rsqrt(jnp.mean(value * value, axis=-1, keepdims=True) + epsilon)
    return value * scale * (1.0 + weight)


def rms_back(value, weight, grad):
    scale = lax.rsqrt(jnp.mean(value * value, axis=-1, keepdims=True) + epsilon)
    normed = value * scale
    weighted = grad * (1.0 + weight)
    value_grad = scale * (weighted - normed * jnp.mean(weighted * normed, axis=-1, keepdims=True))
    weight_grad = jnp.sum(grad * normed, axis=tuple(range(value.ndim - 1)))
    return (value_grad, weight_grad)


def rope_tables(positions, width):
    half = width // 2
    freqs = jnp.power(rope_base, -2.0 * jnp.arange(half, dtype=jnp.float32) / width)
    angles = positions[:, None] * freqs[None, :]
    cosine = jnp.concatenate([jnp.cos(angles), jnp.cos(angles)], axis=-1)
    sine = jnp.concatenate([jnp.sin(angles), jnp.sin(angles)], axis=-1)
    return (cosine, sine)


def rotate(value, cosine, sine):
    half = value.shape[-1] // 2
    turned = jnp.concatenate([-value[..., half:], value[..., :half]], axis=-1)
    return value * cosine + turned * sine


def rotate_back(grad, cosine, sine):
    half = grad.shape[-1] // 2
    scaled = grad * sine
    return grad * cosine + jnp.concatenate([scaled[..., half:], -scaled[..., :half]], axis=-1)


def geglu(gate, upper):
    return jax.nn.gelu(gate, approximate=True) * upper


def dot(left, right, left_dim, right_dim):
    return lax.dot_general(
        left, right, (((left_dim,), (right_dim,)), ((), ())), preferred_element_type=jnp.float32
    )


def swap(value, bit):
    size = lax.axis_size("dp")
    return lax.ppermute(value, "dp", [(i, i ^ (1 << bit)) for i in range(size)])


def shift(value, step):
    size = lax.axis_size("ctx")
    return lax.ppermute(value, "ctx", [(i, (i + step) % size) for i in range(size)])


def pick(value, index, axis=0):
    return lax.dynamic_index_in_dim(value, index, axis, keepdims=False)


def plane_bits():
    return list(range(1, lax.axis_size("dp").bit_length() - 1))


def ctx_gather(value):
    return [value] + [shift(value, k) for k in range(1, lax.axis_size("ctx"))]


def ctx_ordered(pieces):
    size = lax.axis_size("ctx")
    stacked = jnp.stack(pieces)
    mine = lax.axis_index("ctx")
    return jnp.stack([pick(stacked, (mine - a + size) % size) for a in range(size)])


def ctx_reduce(pieces):
    total = pieces[0].astype(jnp.float32)
    for k in range(1, len(pieces)):
        total = total + shift(pieces[k].astype(jnp.bfloat16), -k).astype(jnp.float32)
    return total


def ctx_exchange(blocks):
    size = lax.axis_size("ctx")
    mine = lax.axis_index("ctx")
    return [pick(blocks, mine)] + [
        shift(pick(blocks, (mine + k) % size), k) for k in range(1, size)
    ]


def row_parts(rows, count):
    unit = 8 if rows % 8 == 0 else 1
    edges = [unit * (rows // unit * p // count) for p in range(count + 1)]
    return [(edges[p], edges[p + 1]) for p in range(count)]


def dp_gather(value):
    bits = plane_bits()
    plane = lax.axis_index("dp") // 2
    core = lax.axis_index("dp") % 2
    count = 1 << len(bits)
    parts = []
    for p, (low, high) in enumerate(row_parts(value.shape[0], len(bits))):
        current = value[None, low:high]
        masks = [0]
        for bit in bits[p:] + bits[:p]:
            current = jnp.concatenate([current, swap(current, bit)])
            masks = masks + [m ^ (1 << (bit - 1)) for m in masks]
        other = swap(current, 0)
        place = jnp.asarray([masks.index(m) for m in range(count)], jnp.int32)
        rows_of = []
        for a in range(count):
            at = pick(place, plane ^ a)
            first, second = pick(current, at), pick(other, at)
            rows_of.append(
                jnp.stack([lax.select(core == 0, first, second), lax.select(core == 0, second, first)])
            )
        parts.append(jnp.stack(rows_of))
    whole = jnp.concatenate(parts, axis=2)
    return whole.reshape((2 * count,) + value.shape)


def dp_reduce(kept, sent):
    bits = plane_bits()
    plane = lax.axis_index("dp") // 2
    total = (kept + swap(sent.astype(jnp.bfloat16), 0).astype(jnp.float32)).astype(jnp.bfloat16)
    parts = []
    for p, (low, high) in enumerate(row_parts(total.shape[1], len(bits))):
        current = total[:, low:high]
        current = current.reshape((2,) * len(bits) + current.shape[1:])
        left = sorted(bits, reverse=True)
        for bit in bits[p:] + bits[:p]:
            axis = left.index(bit)
            mine = (plane >> (bit - 1)) & 1
            got = swap(pick(current, 1 - mine, axis), bit)
            current = pick(current, mine, axis).astype(jnp.float32) + got.astype(jnp.float32)
            left.remove(bit)
            if left:
                current = current.astype(jnp.bfloat16)
        parts.append(current)
    return jnp.concatenate(parts, axis=0)


def columns_of(value, core):
    dp = lax.axis_size("dp")
    wide = value.reshape(value.shape[0], dp // 2, 2, value.shape[1] // dp)
    return pick(wide, core, 2).reshape(value.shape[0], -1)


def weight_grad(left, right, extra=None):
    core = lax.axis_index("dp") % 2
    dp = lax.axis_size("dp")
    blocks = []
    for side in (core, 1 - core):
        block = dot(columns_of(left, side), right, 0, 0)
        block = block.reshape(dp // 2, left.shape[1] // dp, right.shape[1])
        if extra is not None:
            block = jnp.concatenate([block, pick(extra, side, 1)], axis=1)
        blocks.append(block)
    return dp_reduce(blocks[0], blocks[1])


def plain(
    tokens,
    cotangent,
    lengths,
    w_query,
    w_key,
    w_value,
    w_out,
    w_gate,
    w_up,
    w_down,
    gain_in,
    gain_query,
    gain_key,
    gain_attn,
    gain_pre,
    gain_post,
):
    count, width = tokens.shape
    seq_count = lengths.shape[1]
    stretch = count // (2 * seq_count)
    dp = lax.axis_size("dp")
    ctx = lax.axis_size("ctx")
    mine = lax.axis_index("ctx")
    head_dim = w_key.shape[1]
    heads = w_query.shape[1] // head_dim
    inner = w_gate.shape[1] // ctx
    span = 2 * ctx * stretch
    offsets = jnp.arange(stretch, dtype=jnp.int32)

    def positions_of(index):
        return jnp.concatenate(
            [index * stretch + offsets, (2 * ctx - 1 - index) * stretch + offsets]
        )

    local_pos = positions_of(mine)
    valid = (local_pos[None, :] < lengths[0][:, None]).astype(jnp.float32).reshape(count, 1)
    cosine, sine = rope_tables(jnp.tile(local_pos, seq_count).astype(jnp.float32), head_dim)
    key_pos = jnp.concatenate([positions_of((mine - k + ctx) % ctx) for k in range(ctx)])
    query_pos = jnp.repeat(local_pos, heads)
    allowed = (key_pos[None, None, :] <= query_pos[None, :, None]) & (
        key_pos[None, None, :] < lengths[0][:, None, None]
    )
    inv_root = head_dim ** (-0.5)

    gains = [gain_in, gain_query, gain_key, gain_attn, gain_pre, gain_post]
    sizes = [g.shape[0] for g in gains]
    small = jnp.concatenate(gains)
    qkv_shard = jnp.concatenate([w_query, w_key, w_value], axis=1)
    in_rows, in_cols = qkv_shard.shape
    out_rows = w_out.shape[0]
    top = max(in_rows, out_rows)
    packed_rows = -(-(top + 1) // 8) * 8
    packed = jnp.concatenate(
        [
            jnp.pad(qkv_shard, ((0, top - in_rows), (0, 0))),
            jnp.pad(w_out, ((0, top - out_rows), (0, 0))),
        ],
        axis=1,
    )
    last = jnp.pad(small[None], ((0, packed_rows - top - 1), (0, packed.shape[1] - small.shape[0])))
    packed = jnp.concatenate([packed, last], axis=0)
    near = ctx_ordered(ctx_gather(packed)).reshape(ctx * packed_rows, -1)
    everything = dp_gather(near).reshape(dp * ctx, packed_rows, -1)
    full_qkv = everything[:, :in_rows, :in_cols].reshape(width, in_cols)
    full_out = everything[:, :out_rows, in_cols:].reshape(heads * head_dim, width)
    smalls = everything[:, top, : small.shape[0]]
    norms, start = [], 0
    for size in sizes:
        norms.append(smalls[:, start : start + size].reshape(-1).astype(jnp.float32))
        start += size
    norm_in, norm_query, norm_key, norm_attn, norm_pre, norm_post = norms

    def column_blocks(weight):
        return weight.reshape(weight.shape[0], ctx, inner).transpose(1, 0, 2)

    gate_up = jnp.stack([column_blocks(w_gate), column_blocks(w_up)], axis=1)
    gate_up = ctx_ordered(ctx_exchange(gate_up)).transpose(1, 0, 2, 3)
    gate_up = gate_up.reshape(2, width // dp, inner)
    per = dp // ctx
    down = w_down.T.reshape(dp, width // dp, w_down.shape[0])
    down = lax.all_to_all(down, "dp", split_axis=0, concat_axis=0, tiled=True)
    down = down.reshape(ctx, per, width // dp, w_down.shape[0])
    down = ctx_ordered(ctx_exchange(down))
    down = down.transpose(2, 1, 0, 3).reshape(width // dp, inner)
    full_gate = dp_gather(gate_up[0]).reshape(width, inner)
    full_up = dp_gather(gate_up[1]).reshape(width, inner)
    full_down = dp_gather(down).reshape(width, inner)

    hidden = tokens.astype(jnp.float32)
    normed = rms_norm(hidden, norm_in).astype(jnp.bfloat16)
    qkv_raw = dot(normed, full_qkv, 1, 0)
    query_raw = qkv_raw[:, : heads * head_dim]
    key_raw = qkv_raw[:, heads * head_dim : (heads + 1) * head_dim]
    value_raw = qkv_raw[:, (heads + 1) * head_dim :]
    query_heads = query_raw.reshape(count, heads, head_dim)
    query_bf = rotate(
        rms_norm(query_heads, norm_query), cosine[:, None, :], sine[:, None, :]
    ).astype(jnp.bfloat16)
    query_bf = query_bf.reshape(seq_count, 2 * stretch * heads, head_dim)
    key_bf = rotate(rms_norm(key_raw, norm_key), cosine, sine).astype(jnp.bfloat16)
    both = jnp.concatenate([key_bf, value_raw.astype(jnp.bfloat16)], axis=1)
    both = jnp.stack(
        [p.reshape(seq_count, 2 * stretch, 2 * head_dim) for p in ctx_gather(both)], axis=1
    ).reshape(seq_count, span, 2 * head_dim)
    keys, values = both[..., :head_dim], both[..., head_dim:]
    scores = (
        jnp.einsum("sqd,skd->sqk", query_bf, keys, preferred_element_type=jnp.float32) * inv_root
    )
    masked = jnp.where(allowed, scores, -1e30)
    peak = jnp.max(masked, axis=-1, keepdims=True)
    expo = jnp.exp(masked - peak)
    total = jnp.sum(expo, axis=-1, keepdims=True)
    probs = expo / total
    probs_bf = probs.astype(jnp.bfloat16)
    mixed = jnp.einsum("sqk,skd->sqd", probs_bf, values, preferred_element_type=jnp.float32)
    mixed_bf = mixed.astype(jnp.bfloat16).reshape(count, heads * head_dim)
    attn_raw = dot(mixed_bf, full_out, 1, 0)
    after_attn = hidden + valid * rms_norm(attn_raw, norm_attn)
    normed_two = rms_norm(after_attn, norm_pre).astype(jnp.bfloat16)

    group_two = jnp.concatenate(ctx_gather(normed_two))
    gate = dot(group_two, full_gate, 1, 0)
    upper = dot(group_two, full_up, 1, 0)
    inner_bf = geglu(gate, upper).astype(jnp.bfloat16)
    ffn_part = dot(inner_bf, full_down, 1, 1)
    ffn_raw = ctx_reduce(list(ffn_part.reshape(ctx, count, width)))
    output = (after_attn + valid * rms_norm(ffn_raw, norm_post)).astype(jnp.bfloat16)

    grad_top = cotangent.astype(jnp.float32)
    ffn_grad, grad_gain_post = rms_back(ffn_raw, norm_post, valid * grad_top)
    group_ffn = jnp.concatenate(ctx_gather(ffn_grad.astype(jnp.bfloat16)))
    inner_grad = dot(group_ffn, full_down, 1, 0)
    _, geglu_pull = jax.vjp(geglu, gate, upper)
    gate_grad, upper_grad = geglu_pull(inner_grad)
    gate_grad_bf = gate_grad.astype(jnp.bfloat16)
    upper_grad_bf = upper_grad.astype(jnp.bfloat16)
    two_part = dot(gate_grad_bf, full_gate, 1, 1) + dot(upper_grad_bf, full_up, 1, 1)
    normed_two_grad = ctx_reduce(list(two_part.reshape(ctx, count, width)))
    grad_down = weight_grad(group_ffn, inner_bf).T
    grad_gate = weight_grad(group_two, gate_grad_bf)
    grad_up = weight_grad(group_two, upper_grad_bf)

    through_pre, grad_gain_pre = rms_back(after_attn, norm_pre, normed_two_grad)
    after_grad = grad_top + through_pre
    attn_grad, grad_gain_attn = rms_back(attn_raw, norm_attn, valid * after_grad)
    attn_grad_bf = attn_grad.astype(jnp.bfloat16)
    grad_out = weight_grad(attn_grad_bf, mixed_bf)
    grad_out = sum_of_ctx(grad_out.reshape(grad_out.shape[0], ctx, -1).transpose(1, 0, 2)).T
    mixed_grad_bf = dot(attn_grad_bf, full_out, 1, 1).astype(jnp.bfloat16)
    mixed_grad_bf = mixed_grad_bf.reshape(seq_count, 2 * stretch * heads, head_dim)
    prob_grad = jnp.einsum(
        "sqd,skd->sqk", mixed_grad_bf, values, preferred_element_type=jnp.float32
    )
    row_dot = jnp.sum(probs * prob_grad, axis=-1, keepdims=True)
    score_grad_bf = (probs * (prob_grad - row_dot)).astype(jnp.bfloat16)
    query_grad = (
        jnp.einsum("sqk,skd->sqd", score_grad_bf, keys, preferred_element_type=jnp.float32)
        * inv_root
    )
    keys_grad = (
        jnp.einsum("sqk,sqd->skd", score_grad_bf, query_bf, preferred_element_type=jnp.float32)
        * inv_root
    )
    values_grad = jnp.einsum(
        "sqk,sqd->skd", probs_bf, mixed_grad_bf, preferred_element_type=jnp.float32
    )
    both_grad = jnp.concatenate([keys_grad, values_grad], axis=-1)
    both_grad = both_grad.reshape(seq_count, ctx, 2 * stretch, 2 * head_dim).transpose(1, 0, 2, 3)
    own_grad = ctx_reduce(list(both_grad.reshape(ctx, count, 2 * head_dim)))
    own_keys_grad, own_values_grad = own_grad[:, :head_dim], own_grad[:, head_dim:]
    query_grad = rotate_back(
        query_grad.reshape(count, heads, head_dim), cosine[:, None, :], sine[:, None, :]
    )
    query_raw_grad, grad_gain_query = rms_back(query_heads, norm_query, query_grad)
    query_raw_bf = query_raw_grad.reshape(count, heads * head_dim).astype(jnp.bfloat16)
    key_raw_grad, grad_gain_key = rms_back(
        key_raw, norm_key, rotate_back(own_keys_grad, cosine, sine)
    )
    key_raw_bf = key_raw_grad.astype(jnp.bfloat16)
    value_raw_bf = own_values_grad.astype(jnp.bfloat16)
    raw_bf = jnp.concatenate([query_raw_bf, key_raw_bf, value_raw_bf], axis=1)
    normed_grad = dot(raw_bf, full_qkv, 1, 1)
    through_in, grad_gain_in = rms_back(hidden, norm_in, normed_grad)
    input_grad = (after_grad + through_in).astype(jnp.bfloat16)

    by_ctx = jnp.concatenate(
        [r.reshape(count, ctx, -1) for r in (query_raw_bf, key_raw_bf, value_raw_bf)], axis=2
    )
    each = by_ctx.shape[2]
    gain_grads = jnp.concatenate(
        [
            g.reshape(dp * ctx, -1)
            for g in (
                grad_gain_in,
                grad_gain_query,
                grad_gain_key,
                grad_gain_attn,
                grad_gain_pre,
                grad_gain_post,
            )
        ],
        axis=1,
    )
    small_size = gain_grads.shape[1]
    extra = jnp.pad(gain_grads, ((0, 0), (0, each - small_size))).reshape(
        dp // 2, 2, 1, ctx * each
    )
    extra = jnp.pad(extra, ((0, 0), (0, 0), (0, 7), (0, 0)))
    grad_qkv = weight_grad(normed, by_ctx.reshape(count, ctx * each), extra)
    grad_qkv = sum_of_ctx(grad_qkv.reshape(grad_qkv.shape[0], ctx, each).transpose(1, 0, 2))
    rows = width // dp
    gain_out = grad_qkv[rows, :small_size]
    grad_qkv = grad_qkv[:rows]
    q_cols, k_cols = heads * head_dim // ctx, head_dim // ctx
    outs, start = [], 0
    for size in sizes:
        outs.append(gain_out[start : start + size])
        start += size
    return (
        output,
        input_grad,
        grad_qkv[:, :q_cols],
        grad_qkv[:, q_cols : q_cols + k_cols],
        grad_qkv[:, q_cols + k_cols :],
        grad_out,
        grad_gate,
        grad_up,
        grad_down,
        *outs,
    )


def sum_of_ctx(blocks):
    size = lax.axis_size("ctx")
    mine = lax.axis_index("ctx")
    total = pick(blocks, mine).astype(jnp.float32)
    for k in range(1, size):
        got = shift(pick(blocks, (mine + k) % size).astype(jnp.bfloat16), k)
        total = total + got.astype(jnp.float32)
    return total


mega = 2**20


def place(name):
    return {"vmem": pl.BlockSpec(memory_space=pltpu.VMEM), "smem": pl.BlockSpec(memory_space=pltpu.SMEM), "any": pl.BlockSpec(memory_space=pl.ANY)}[name]


def kernel_call(body, outs, args, where=None, scratch=(), flops=0):
    where = where or {}
    size = sum(a.size * a.dtype.itemsize for a in args)
    size += sum(int(np.prod(s)) * jnp.dtype(t).itemsize for s, t in outs)
    return pl.pallas_call(
        body,
        out_shape=[jax.ShapeDtypeStruct(s, t) for s, t in outs],
        in_specs=[place(where.get(i, "vmem")) for i in range(len(args))],
        out_specs=[place("vmem") for _ in outs],
        scratch_shapes=list(scratch),
        compiler_params=pltpu.CompilerParams(vmem_limit_bytes=58 * mega),
        cost_estimate=pl.CostEstimate(flops=flops, bytes_accessed=size, transcendentals=0),
    )(*args)


def norm_back(value, weight, grad):
    scale = lax.rsqrt(jnp.mean(value * value, axis=-1, keepdims=True) + epsilon)
    normed = value * scale
    weighted = grad * (1.0 + weight)
    value_grad = scale * (weighted - normed * jnp.mean(weighted * normed, axis=-1, keepdims=True))
    return value_grad, jnp.sum(grad * normed, axis=0, keepdims=True)


def put_rows(target, at, pieces, masks, rows):
    for piece, mask in zip(pieces, masks):
        start = pl.multiple_of((at ^ mask) * rows, 16)
        target[pl.ds(start, rows), :] = piece[:rows, :]


def spread(where_ref, parts, masks, rows, lane, size, ctx):
    dp = len(parts)
    shards = jnp.concatenate([p[rows:, lane : lane + 128] for p in parts], axis=0)
    tail = shards.shape[0] // dp
    whole = dp * ctx * size
    column = lax.broadcasted_iota(jnp.int32, (128, whole), 1)
    line = lax.broadcasted_iota(jnp.int32, (128, whole), 0)
    spots = jnp.where(column % size == line, 1.0, 0.0).astype(jnp.bfloat16)
    values = dot(shards, spots, 1, 0)
    column = lax.broadcasted_iota(jnp.int32, (tail, whole), 1) // size
    line = lax.broadcasted_iota(jnp.int32, (tail, whole), 0)
    total = jnp.zeros((tail, whole), jnp.float32)
    for k, mask in enumerate(masks):
        owner = jnp.where(line < ctx, (where_ref[0] ^ mask) * ctx + line, -1)
        total = total + jnp.where(column == owner, values[k * tail : (k + 1) * tail], 0.0)
    return jnp.sum(total, axis=0, keepdims=True)


def pack(w_query, w_key, w_value, gains):
    rows = w_query.shape[0]
    ends = np.cumsum([w_query.shape[1], w_key.shape[1], w_value.shape[1]])
    tall = -(-(rows + 1) // 8) * 8

    def body(query_ref, key_ref, value_ref, *rest):
        shards, out, wide = rest[: len(gains)], rest[-2], rest[-1]
        wide[rows:, :] = jnp.zeros((tall - rows, wide.shape[1]), jnp.float32)
        wide[:rows, : ends[0]] = query_ref[...].astype(jnp.float32)
        wide[:rows, ends[0] : ends[1]] = key_ref[...].astype(jnp.float32)
        wide[:rows, ends[1] :] = value_ref[...].astype(jnp.float32)
        for i, shard in enumerate(shards):
            wide[rows : rows + 1, i * 128 : i * 128 + shard.shape[1]] = shard[...].astype(
                jnp.float32
            )
        out[...] = wide[...].astype(jnp.bfloat16)

    return kernel_call(
        body,
        [((tall, int(ends[2])), jnp.bfloat16)],
        [w_query, w_key, w_value, *[g.reshape(1, -1) for g in gains]],
        scratch=[pltpu.VMEM((tall, int(ends[2])), jnp.float32)],
    )[0]


def tables(where, lengths, count, stretch, ctx, head_dim):
    seqs = lengths.shape[1]
    each, half = count // seqs, head_dim // 2
    span = 2 * ctx * stretch
    freqs = rope_base ** (-2.0 * np.arange(half, dtype=np.float64) / head_dim)
    freqs = jnp.asarray(freqs[None].astype(np.float32))

    def positions(index, owner):
        block, step = index // stretch % 2, index % stretch
        return jnp.where(block == 0, owner, 2 * ctx - 1 - owner) * stretch + step

    def body(where_ref, lengths_ref, freqs_ref, cos_out, sin_out, valid_out, allowed_out):
        mine = where_ref[4]
        rows = lax.broadcasted_iota(jnp.int32, (each, 1), 0)
        local = positions(rows, mine)
        angles = local.astype(jnp.float32) * freqs_ref[...]
        cos, sin = jnp.cos(angles), jnp.sin(angles)
        cols = lax.broadcasted_iota(jnp.int32, (1, span), 1)
        owner = (mine - cols // each + ctx) % ctx
        keys = positions(cols % each, owner)
        for s in range(seqs):
            part = slice(s * each, (s + 1) * each)
            for low, high in ((0, half), (half, head_dim)):
                cos_out[part, low:high] = cos
                sin_out[part, low:high] = sin
            length = lengths_ref[0, s]
            valid_out[part, :] = jnp.where(local < length, 1.0, 0.0)
            allowed_out[s] = jnp.where((keys <= local) & (keys < length), 1.0, 0.0)

    return kernel_call(
        body,
        [
            ((count, head_dim), jnp.float32),
            ((count, head_dim), jnp.float32),
            ((count, 1), jnp.float32),
            ((seqs, each, span), jnp.float32),
        ],
        [where, lengths, freqs],
        {0: "smem", 1: "smem"},
    )


def late_gains(where, pieces, masks, rows, lanes, sizes, ctx, after):
    def body(where_ref, after_ref, *rest):
        parts, outs = rest[: len(pieces)], rest[len(pieces) :]
        for out, lane, size in zip(outs, lanes, sizes):
            out[...] = spread(where_ref, parts, masks, rows, lane, size, ctx)

    return kernel_call(
        body,
        [((1, len(pieces) * ctx * size), jnp.float32) for size in sizes],
        [where, after, *pieces],
        {0: "smem", 1: "any"},
    )


def project(where, tokens, pieces, sizes, cosine, sine, masks, heads, ctx):
    count, width = tokens.shape
    wide = pieces[0].shape[1]
    head_dim = cosine.shape[1]
    total = len(pieces)
    rows = width // total

    def body(where_ref, x_ref, cos_ref, sin_ref, *rest):
        parts = rest[:total]
        normed_ref, query_out, both_out, raw_out, in_ref, query_ref, key_ref, weight = rest[total:]
        for i, ref in enumerate((in_ref, query_ref, key_ref)):
            ref[...] = spread(where_ref, parts, masks, rows, i * 128, sizes[i], ctx)
        put_rows(weight, where_ref[0], parts, masks, rows)
        normed = rms_norm(x_ref[...].astype(jnp.float32), in_ref[...]).astype(jnp.bfloat16)
        normed_ref[...] = normed
        cos, sin = cos_ref[...], sin_ref[...]
        for h in range(heads + 1):
            cols = slice(h * head_dim, (h + 1) * head_dim)
            raw = dot(normed, weight[:, cols], 1, 0)
            raw_out[:, cols] = raw
            gain = query_ref[...] if h < heads else key_ref[...]
            turned = rotate(rms_norm(raw, gain), cos, sin).astype(jnp.bfloat16)
            if h < heads:
                query_out[:, cols] = turned
            else:
                both_out[:, :head_dim] = turned
        both_out[:, head_dim:] = dot(normed, weight[:, (heads + 1) * head_dim :], 1, 0).astype(
            jnp.bfloat16
        )

    return kernel_call(
        body,
        [
            ((count, width), jnp.bfloat16),
            ((count, heads * head_dim), jnp.bfloat16),
            ((count, 2 * head_dim), jnp.bfloat16),
            ((count, (heads + 1) * head_dim), jnp.float32),
            ((1, width), jnp.float32),
            ((1, head_dim), jnp.float32),
            ((1, head_dim), jnp.float32),
        ],
        [where, tokens, cosine, sine, *pieces],
        {0: "smem"},
        [pltpu.VMEM((width, wide), jnp.bfloat16)],
        2 * count * width * wide,
    )


def attend(where, tokens, query, both, allowed, valid, norm_attn, norm_pre, pieces, masks, heads):
    count, width = tokens.shape
    seqs, each, span = allowed.shape
    head_dim = query.shape[1] // heads
    inv_root = head_dim ** (-0.5)
    near, total = len(both), len(pieces)

    def body(where_ref, x_ref, query_ref, allowed_ref, valid_ref, attn_ref, pre_ref, *rest):
        got, parts = rest[:near], rest[near : near + total]
        probs_out, mixed_out, raw_out, after_out, two_out, weight = rest[near + total :]
        put_rows(weight, where_ref[0], parts, masks, parts[0].shape[0])
        for s in range(seqs):
            rows = slice(s * each, (s + 1) * each)
            queries = jnp.concatenate(
                [query_ref[rows, h * head_dim : (h + 1) * head_dim] for h in range(heads)], axis=0
            )
            keys = jnp.concatenate([g[rows, :head_dim] for g in got], axis=0)
            values = jnp.concatenate([g[rows, head_dim:] for g in got], axis=0)
            scores = dot(queries, keys, 1, 1) * inv_root
            keep = jnp.concatenate([allowed_ref[s]] * heads, axis=0)
            scores = jnp.where(keep > 0.0, scores, -1e30)
            expo = jnp.exp(scores - jnp.max(scores, axis=-1, keepdims=True))
            probs = expo / jnp.sum(expo, axis=-1, keepdims=True)
            probs_out[s] = probs
            mixed = dot(probs.astype(jnp.bfloat16), values, 1, 0).astype(jnp.bfloat16)
            for h in range(heads):
                mixed_out[rows, h * head_dim : (h + 1) * head_dim] = mixed[
                    h * each : (h + 1) * each
                ]
        raw = dot(mixed_out[...], weight[...], 1, 0)
        raw_out[...] = raw
        after = x_ref[...].astype(jnp.float32) + valid_ref[...] * rms_norm(raw, attn_ref[...])
        after_out[...] = after
        two_out[...] = rms_norm(after, pre_ref[...]).astype(jnp.bfloat16)

    return kernel_call(
        body,
        [
            ((seqs, heads * each, span), jnp.float32),
            ((count, heads * head_dim), jnp.bfloat16),
            ((count, width), jnp.float32),
            ((count, width), jnp.float32),
            ((count, width), jnp.bfloat16),
        ],
        [where, tokens, query, allowed, valid, norm_attn, norm_pre, *both, *pieces],
        {0: "smem"},
        [pltpu.VMEM((heads * head_dim, width), jnp.bfloat16)],
        2 * count * heads * head_dim * (width + 2 * span),
    )


def column_steps(size, step):
    return [(s, min(size, s + step)) for s in range(0, size, step)]


def halves_of(rows):
    first = -(-rows // 32) * 16
    return first, rows - first


def wide_pieces(parts, far, chunk):
    first, second = halves_of(chunk)
    shapes = [(0, 0, chunk), (2, 0, chunk), (4, 0, chunk), (6, 0, first), (6, first, second)]
    return [(ref, mask, at, rows) for ref, (mask, at, rows) in zip(parts, shapes)] + [
        (ref, mask ^ 1, at, rows) for ref, (mask, at, rows) in zip(far, shapes)
    ]


def load_weights(index, pieces, chunk, target, sems):
    def copies(m):
        result = []
        for i, (ref, mask, at, rows) in enumerate(pieces):
            start = pl.multiple_of((index ^ mask) * chunk + at, 16)
            result.append(
                pltpu.make_async_copy(ref.at[m], target.at[m, pl.ds(start, rows)], sems.at[m, i])
            )
        return result

    return [copies(m) for m in range(target.shape[0])]


def feed_forward(where, pieces, weights):
    count, width = pieces[0].shape
    kinds, chunk, inner = weights[0].shape
    lanes = -(-inner // 128) * 128
    near, spots = len(pieces), len(weights)
    total = near * count
    slope = (2.0 / np.pi) ** 0.5

    def body(where_ref, *rest):
        shards, rest = rest[:spots], rest[spots:]
        parts = rest[:near]
        group_out, act_out, one_out, two_out = rest[near : near + 4]
        sums = rest[near + 4 : near + 4 + near]
        weight, sems = rest[near + 4 + near :]
        shards = wide_pieces(shards[: spots // 2], shards[spots // 2 :], chunk)
        copies = load_weights(where_ref[0], shards, chunk, weight, sems)
        for kind in copies:
            for copy in kind:
                copy.start()
        for k in range(near):
            group_out[k * count : (k + 1) * count, :] = parts[k][...]
        for kind in copies[:2]:
            for copy in kind:
                copy.wait()
        for low, high in column_steps(inner, 256):
            gate = dot(group_out[...], weight[0, :, low:high], 1, 0)
            upper = dot(group_out[...], weight[1, :, low:high], 1, 0)
            bent = jnp.tanh(slope * (gate + 0.044715 * (gate * gate * gate)))
            half = 0.5 * (1.0 + bent)
            gelu = gate * half
            steep = half + 0.5 * gate * (1.0 - bent * bent) * (
                slope * (1.0 + 3.0 * 0.044715 * gate * gate)
            )
            act_out[:, low:high] = (gelu * upper).astype(jnp.bfloat16)
            one_out[:, low:high] = (steep * upper).astype(jnp.bfloat16)
            two_out[:, low:high] = gelu.astype(jnp.bfloat16)
        if lanes > inner:
            act_out[:, inner:] = jnp.zeros((total, lanes - inner), jnp.bfloat16)
        for copy in copies[2]:
            copy.wait()
        for low, high in column_steps(width, 384):
            part = dot(act_out[:, :inner], weight[2, low:high, :], 1, 1)
            for k in range(near):
                sums[k][:, low:high] = part[k * count : (k + 1) * count].astype(sums[k].dtype)

    return kernel_call(
        body,
        [((total, width), jnp.bfloat16)]
        + [((total, lanes), jnp.bfloat16)]
        + [((total, inner), jnp.bfloat16)] * 2
        + [((count, width), jnp.float32)]
        + [((count, width), jnp.bfloat16)] * (near - 1),
        [where, *weights, *pieces],
        {0: "smem", **{1 + i: "any" for i in range(spots)}},
        [
            pltpu.VMEM((kinds, width, inner), jnp.bfloat16),
            pltpu.SemaphoreType.DMA((kinds, spots)),
        ],
        6 * total * width * inner,
    )


def finish(parts, after, cotangent, valid, norm_post):
    count, width = after.shape
    near = len(parts)

    def body(after_ref, cot_ref, valid_ref, post_ref, *rest):
        got = rest[:near]
        output_out, grad_out, gain_out = rest[near:]
        raw = got[0][...]
        for g in got[1:]:
            raw = raw + g[...].astype(jnp.float32)
        ok = valid_ref[...]
        output_out[...] = (after_ref[...] + ok * rms_norm(raw, post_ref[...])).astype(jnp.bfloat16)
        grad, gain = norm_back(raw, post_ref[...], ok * cot_ref[...].astype(jnp.float32))
        grad_out[...] = grad.astype(jnp.bfloat16)
        gain_out[...] = gain

    return kernel_call(
        body,
        [
            ((count, width), jnp.bfloat16),
            ((count, width), jnp.bfloat16),
            ((1, width), jnp.float32),
        ],
        [after, cotangent, valid, norm_post, *parts],
    )


def feed_back(where, pieces, weights, one, two):
    count, width = pieces[0].shape
    kinds, chunk, inner = weights[0].shape
    lanes = -(-inner // 128) * 128
    near, spots = len(pieces), len(weights)
    total = near * count

    def body(where_ref, one_ref, two_ref, *rest):
        shards, rest = rest[:spots], rest[spots:]
        parts = rest[:near]
        group_out, gate_out, upper_out = rest[near : near + 3]
        sums = rest[near + 3 : near + 3 + near]
        weight, sems = rest[near + 3 + near :]
        shards = wide_pieces(shards[: spots // 2], shards[spots // 2 :], chunk)
        copies = load_weights(where_ref[0], shards, chunk, weight, sems)
        for kind in (copies[2], copies[0], copies[1]):
            for copy in kind:
                copy.start()
        for k in range(near):
            group_out[k * count : (k + 1) * count, :] = parts[k][...]
        for copy in copies[2]:
            copy.wait()
        for low, high in column_steps(inner, 256):
            grad = dot(group_out[...], weight[2, :, low:high], 1, 0)
            gate_out[:, low:high] = (grad * one_ref[:, low:high].astype(jnp.float32)).astype(
                jnp.bfloat16
            )
            upper_out[:, low:high] = (grad * two_ref[:, low:high].astype(jnp.float32)).astype(
                jnp.bfloat16
            )
        if lanes > inner:
            gate_out[:, inner:] = jnp.zeros((total, lanes - inner), jnp.bfloat16)
            upper_out[:, inner:] = jnp.zeros((total, lanes - inner), jnp.bfloat16)
        for kind in copies[:2]:
            for copy in kind:
                copy.wait()
        for low, high in column_steps(width, 384):
            part = dot(gate_out[:, :inner], weight[0, low:high, :], 1, 1)
            part = part + dot(upper_out[:, :inner], weight[1, low:high, :], 1, 1)
            for k in range(near):
                sums[k][:, low:high] = part[k * count : (k + 1) * count].astype(sums[k].dtype)

    return kernel_call(
        body,
        [((total, width), jnp.bfloat16)]
        + [((total, lanes), jnp.bfloat16)] * 2
        + [((count, width), jnp.float32)]
        + [((count, width), jnp.bfloat16)] * (near - 1),
        [where, one, two, *weights, *pieces],
        {0: "smem", **{3 + i: "any" for i in range(spots)}},
        [
            pltpu.VMEM((kinds, width, inner), jnp.bfloat16),
            pltpu.SemaphoreType.DMA((kinds, spots)),
        ],
        6 * total * width * inner,
    )


def wide_grads(where, two, two_far, back, back_far, act, act_far, gate, gate_far, upper, upper_far):
    total, width = two.shape
    inner = act.shape[1]
    chunk = width // 8
    first, second = halves_of(chunk)

    def body(where_ref, *rest):
        lefts = [rest[0:2], rest[2:4]]
        rights = [rest[6:8], rest[8:10], rest[4:6]]
        outs = rest[10:14]
        turned, left = rest[14:]
        core, x, y = where_ref[1], where_ref[2], where_ref[3]
        order = []
        for flip in (1, 0):
            order.append([(j * 2 + jnp.bitwise_xor(x, flip), 0, first) for j in range(2)])
        for flip in (1, 0):
            order.append([(jnp.bitwise_xor(y, flip) * 2 + j, first, second) for j in range(2)])
        for index, kinds in ((0, (0, 1)), (1, (2,))):
            for side in range(2):
                turned[:, side * total : (side + 1) * total] = lefts[index][side][...].T
            at = 0
            for block in order:
                for plane, offset, size in block:
                    start = pl.multiple_of((plane * 2 + core) * chunk + offset, 16)
                    left[at : at + size, :] = turned[pl.ds(start, size), :]
                    at += size
            for m in kinds:
                own, far = rights[m]
                for low, high in column_steps(inner, 256):
                    part = dot(left[:, :total], own[:, low:high], 1, 0)
                    part = part + dot(left[:, total:], far[:, low:high], 1, 0)
                    part = part.astype(jnp.bfloat16)
                    at = 0
                    for out, block in zip(outs, order):
                        size = 2 * block[0][2]
                        out[m, :, low:high] = part[at : at + size]
                        at += size

    return kernel_call(
        body,
        [
            ((3, 2 * first, inner), jnp.bfloat16),
            ((3, 2 * first, inner), jnp.bfloat16),
            ((3, 2 * second, inner), jnp.bfloat16),
            ((3, 2 * second, inner), jnp.bfloat16),
        ],
        [where, two, two_far, back, back_far, act, act_far, gate, gate_far, upper, upper_far],
        {0: "smem"},
        [
            pltpu.VMEM((width, 2 * total), jnp.bfloat16),
            pltpu.VMEM((width // 2, 2 * total), jnp.bfloat16),
        ],
        6 * total * width * inner,
    )


def wide_middle(where, kept_a, got_a, kept_b, got_b):
    kinds, twice_a, inner = kept_a.shape
    first, second = twice_a // 2, kept_b.shape[1] // 2

    def body(where_ref, kept_a_ref, got_a_ref, kept_b_ref, got_b_ref, *outs):
        x, y = where_ref[2], where_ref[3]
        for m in range(kinds):
            for flip, out in ((1, outs[0]), (0, outs[1])):
                rows = pl.ds(pl.multiple_of(jnp.bitwise_xor(y, flip) * first, 16), first)
                total = kept_a_ref[m, rows, :].astype(jnp.float32) + got_a_ref[m, rows, :].astype(
                    jnp.float32
                )
                out[m] = total.astype(jnp.bfloat16)
            for flip, out in ((1, outs[2]), (0, outs[3])):
                rows = pl.ds(pl.multiple_of(jnp.bitwise_xor(x, flip) * second, 16), second)
                total = kept_b_ref[m, rows, :].astype(jnp.float32) + got_b_ref[m, rows, :].astype(
                    jnp.float32
                )
                out[m] = total.astype(jnp.bfloat16)

    return kernel_call(
        body,
        [
            ((kinds, first, inner), jnp.bfloat16),
            ((kinds, first, inner), jnp.bfloat16),
            ((kinds, second, inner), jnp.bfloat16),
            ((kinds, second, inner), jnp.bfloat16),
        ],
        [where, kept_a, got_a, kept_b, got_b],
        {0: "smem"},
    )


def wide_last(kept_a, got_a, kept_b, got_b, inner):
    kinds, first, _ = kept_a.shape
    second = kept_b.shape[1]

    def body(kept_a_ref, got_a_ref, kept_b_ref, got_b_ref, *outs):
        for m in range(kinds):
            total = kept_a_ref[m].astype(jnp.float32) + got_a_ref[m].astype(jnp.float32)
            outs[m][:first, :] = total[:, :inner]
            total = kept_b_ref[m].astype(jnp.float32) + got_b_ref[m].astype(jnp.float32)
            outs[m][first:, :] = total[:, :inner]

    return kernel_call(
        body,
        [((first + second, inner), jnp.float32)] * kinds,
        [kept_a, got_a, kept_b, got_b],
    )


def attend_back(
    where,
    parts,
    after,
    cotangent,
    valid,
    attn_raw,
    norm_pre,
    norm_attn,
    norm_query,
    probs,
    query,
    raw,
    both,
    pieces,
    cosine,
    sine,
    masks,
    heads,
):
    count, width = after.shape
    seqs, _, span = probs.shape
    each = count // seqs
    head_dim = norm_query.shape[1]
    inv_root = head_dim ** (-0.5)
    near, total = len(both), len(pieces)

    def body(
        where_ref,
        after_ref,
        cot_ref,
        valid_ref,
        attn_ref,
        pre_ref,
        norm_ref,
        query_gain_ref,
        probs_ref,
        query_ref,
        raw_ref,
        cos_ref,
        sin_ref,
        *rest,
    ):
        sums = rest[:near]
        got = rest[near : 2 * near]
        shards = rest[2 * near : 2 * near + total]
        rest = rest[2 * near + total :]
        dx_out, attn_grad_out, raw_grad_out, pre_out, attn_gain_out, query_gain_out = rest[:6]
        both_outs = rest[6 : 6 + near]
        weight, mixed_grad, query_grad = rest[6 + near :]
        put_rows(weight, where_ref[0], shards, masks, shards[0].shape[0])
        grad = sums[0][...]
        for s in sums[1:]:
            grad = grad + s[...].astype(jnp.float32)
        through, gain = norm_back(after_ref[...], pre_ref[...], grad)
        pre_out[...] = gain
        dx = cot_ref[...].astype(jnp.float32) + through
        dx_out[...] = dx
        attn_grad, gain = norm_back(attn_ref[...], norm_ref[...], valid_ref[...] * dx)
        attn_gain_out[...] = gain
        attn_grad = attn_grad.astype(jnp.bfloat16)
        attn_grad_out[...] = attn_grad
        mixed_grad[...] = dot(attn_grad, weight[...], 1, 1).astype(jnp.bfloat16)
        for s in range(seqs):
            rows = slice(s * each, (s + 1) * each)
            queries = jnp.concatenate(
                [query_ref[rows, h * head_dim : (h + 1) * head_dim] for h in range(heads)], axis=0
            )
            grads = jnp.concatenate(
                [mixed_grad[rows, h * head_dim : (h + 1) * head_dim] for h in range(heads)], axis=0
            )
            keys = jnp.concatenate([g[rows, :head_dim] for g in got], axis=0)
            values = jnp.concatenate([g[rows, head_dim:] for g in got], axis=0)
            probs = probs_ref[s]
            prob_grad = dot(grads, values, 1, 1)
            row = jnp.sum(probs * prob_grad, axis=-1, keepdims=True)
            score_grad = (probs * (prob_grad - row)).astype(jnp.bfloat16)
            back = dot(score_grad, keys, 1, 0) * inv_root
            for h in range(heads):
                query_grad[rows, h * head_dim : (h + 1) * head_dim] = back[
                    h * each : (h + 1) * each
                ]
            keys_grad = dot(score_grad, queries, 0, 0) * inv_root
            values_grad = dot(probs.astype(jnp.bfloat16), grads, 0, 0)
            for k in range(near):
                part = slice(k * each, (k + 1) * each)
                both_outs[k][rows, :head_dim] = keys_grad[part].astype(both_outs[k].dtype)
                both_outs[k][rows, head_dim:] = values_grad[part].astype(both_outs[k].dtype)
        cos, sin = cos_ref[...], sin_ref[...]
        gain_sum = jnp.zeros((1, head_dim), jnp.float32)
        for h in range(heads):
            cols = slice(h * head_dim, (h + 1) * head_dim)
            turned = rotate_back(query_grad[:, cols], cos, sin)
            value_grad, gain = norm_back(raw_ref[:, cols], query_gain_ref[...], turned)
            raw_grad_out[:, cols] = value_grad.astype(jnp.bfloat16)
            gain_sum = gain_sum + gain
        query_gain_out[...] = gain_sum

    return kernel_call(
        body,
        [
            ((count, width), jnp.float32),
            ((count, width), jnp.bfloat16),
            ((count, heads * head_dim), jnp.bfloat16),
            ((1, width), jnp.float32),
            ((1, width), jnp.float32),
            ((1, head_dim), jnp.float32),
            ((count, 2 * head_dim), jnp.float32),
        ]
        + [((count, 2 * head_dim), jnp.bfloat16)] * (near - 1),
        [
            where,
            after,
            cotangent,
            valid,
            attn_raw,
            norm_pre,
            norm_attn,
            norm_query,
            probs,
            query,
            raw,
            cosine,
            sine,
            *parts,
            *both,
            *pieces,
        ],
        {0: "smem"},
        [
            pltpu.VMEM((heads * head_dim, width), jnp.bfloat16),
            pltpu.VMEM((count, heads * head_dim), jnp.bfloat16),
            pltpu.VMEM((count, heads * head_dim), jnp.float32),
        ],
        2 * count * heads * head_dim * (width + 5 * span),
    )


def project_back(
    where,
    parts,
    raw,
    query_grad,
    tokens,
    dx,
    norm_in,
    norm_key,
    cosine,
    sine,
    pieces,
    masks,
    heads,
    ctx,
    gains,
):
    count, width = tokens.shape
    wide = pieces[0].shape[1]
    head_dim = norm_key.shape[1]
    near, total = len(parts), len(pieces)
    step = heads * head_dim // ctx
    count_gains = len(gains)

    def body(
        where_ref, raw_ref, query_ref, x_ref, dx_ref, in_ref, key_ref, cos_ref, sin_ref, *rest
    ):
        sums = rest[:near]
        shards = rest[near : near + total]
        others = rest[near + total : near + total + count_gains]
        input_out, grads_out, gains_out, weight = rest[near + total + count_gains :]
        put_rows(weight, where_ref[0], shards, masks, width // total)
        grad = sums[0][...]
        for s in sums[1:]:
            grad = grad + s[...].astype(jnp.float32)
        turned = rotate_back(grad[:, :head_dim], cos_ref[...], sin_ref[...])
        key_grad, key_gain = norm_back(raw_ref[:, heads * head_dim :], key_ref[...], turned)
        grads_out[:, : heads * head_dim] = query_ref[...]
        grads_out[:, heads * head_dim : (heads + 1) * head_dim] = key_grad.astype(jnp.bfloat16)
        grads_out[:, (heads + 1) * head_dim :] = grad[:, head_dim:].astype(jnp.bfloat16)
        back = dot(grads_out[...], weight[...], 1, 1)
        through, in_gain = norm_back(x_ref[...].astype(jnp.float32), in_ref[...], back)
        input_out[...] = (dx_ref[...] + through).astype(jnp.bfloat16)
        gains_out[...] = jnp.zeros((total, wide), jnp.float32)
        lane = 0
        for gain in (in_gain, others[0][...], key_gain, *[o[...] for o in others[1:]]):
            size = gain.shape[1] // (total * ctx)
            for d in range(total):
                for c in range(ctx):
                    at = c * step + lane
                    gains_out[d : d + 1, at : at + size] = gain[
                        :, (d * ctx + c) * size : (d * ctx + c + 1) * size
                    ]
            lane += size

    return kernel_call(
        body,
        [
            ((count, width), jnp.bfloat16),
            ((count, wide), jnp.bfloat16),
            ((total, wide), jnp.float32),
        ],
        [
            where,
            raw,
            query_grad,
            tokens,
            dx,
            norm_in,
            norm_key,
            cosine,
            sine,
            *parts,
            *pieces,
            *gains,
        ],
        {0: "smem"},
        [pltpu.VMEM((width, wide), jnp.bfloat16)],
        2 * count * width * wide,
    )


def narrow_grads(where, left, left_far, right, right_far, gains=()):
    count, width = left.shape
    wide = right.shape[1]
    chunk = width // 8
    tall = chunk + 16 if gains else chunk

    def body(where_ref, left_ref, far_ref, right_ref, right_far_ref, *rest):
        rows, rest = rest[: len(gains)], rest[len(gains) :]
        outs, (turned, lefts) = rest[:4], rest[4:]
        turned[:, :count] = left_ref[...].T
        turned[:, count:] = far_ref[...].T
        plane, core = where_ref[0] // 2, where_ref[1]
        for m in range(4):
            start = pl.multiple_of((jnp.bitwise_xor(plane, m) * 2 + core) * chunk, 16)
            lefts[m * chunk : (m + 1) * chunk, :] = turned[pl.ds(start, chunk), :]
        for low, high in column_steps(wide, 256):
            part = dot(lefts[:, :count], right_ref[:, low:high], 1, 0)
            part = part + dot(lefts[:, count:], right_far_ref[:, low:high], 1, 0)
            for m in range(4):
                outs[m][:chunk, low:high] = part[m * chunk : (m + 1) * chunk].astype(outs[m].dtype)
        if gains:
            whole = rows[0][...] + rows[1][...]
            index = lax.broadcasted_iota(jnp.int32, whole.shape, 0)
            for m in range(4):
                row = jnp.bitwise_xor(plane, m) * 2 + core
                row = jnp.sum(jnp.where(index == row, whole, 0.0), axis=0, keepdims=True)
                lines = lax.broadcasted_iota(jnp.int32, (16, wide), 0)
                outs[m][chunk:, :] = jnp.where(lines == 0, row, 0.0).astype(outs[m].dtype)

    return kernel_call(
        body,
        [((tall, wide), jnp.float32)] + [((tall, wide), jnp.bfloat16)] * 3,
        [where, left, left_far, right, right_far, *gains],
        {0: "smem"},
        [
            pltpu.VMEM((width, 2 * count), jnp.bfloat16),
            pltpu.VMEM((width // 2, 2 * count), jnp.bfloat16),
        ],
        2 * count * width * wide,
    )


def narrow_middle(where, parts, sizes, ctx):
    chunk, wide = parts[0].shape
    each = wide // ctx

    def body(where_ref, *rest):
        got = rest[: len(parts)]
        outs = rest[len(parts) :]
        mine = where_ref[4]
        total = got[0][...]
        for g in got[1:]:
            total = total + g[...].astype(jnp.float32)
        for c in range(ctx):

            @pl.when(mine == c)
            def _(c=c):
                for k in range(ctx):
                    j = (c + k) % ctx
                    start, at = 0, 0
                    for size in sizes:
                        piece = size // ctx
                        outs[k][:, at : at + piece] = total[
                            :, start + j * piece : start + (j + 1) * piece
                        ].astype(outs[k].dtype)
                        start += size
                        at += piece

    return kernel_call(
        body,
        [((chunk, each), jnp.float32)] + [((chunk, each), jnp.bfloat16)] * (ctx - 1),
        [where, *parts],
        {0: "smem"},
    )


def split_columns(where, gate, up, ctx):
    rows, whole = gate.shape
    inner = whole // ctx

    def body(where_ref, gate_ref, up_ref, *outs):
        mine = where_ref[4]
        for c in range(ctx):

            @pl.when(mine == c)
            def _(c=c):
                for k in range(ctx):
                    j = (c + k) % ctx
                    outs[k][0] = gate_ref[:, j * inner : (j + 1) * inner]
                    outs[k][1] = up_ref[:, j * inner : (j + 1) * inner]

    return kernel_call(
        body, [((2, rows, inner), jnp.bfloat16)] * ctx, [where, gate, up], {0: "smem"}
    )


def join_wide(where, pairs, downs):
    ctx = len(pairs)
    _, rows, inner = pairs[0].shape
    per, chunk, part = downs[0].shape

    def body(where_ref, *rest):
        two, down, out, rows_scr = rest[:ctx], rest[ctx : 2 * ctx], rest[2 * ctx], rest[2 * ctx + 1]
        mine = where_ref[4]
        for c in range(ctx):

            @pl.when(mine == c)
            def _(c=c):
                for m in range(2):
                    for a in range(ctx):
                        rows_scr[a * rows : (a + 1) * rows, :] = two[(c - a) % ctx][m].astype(
                            jnp.float32
                        )
                    out[m] = rows_scr[...].astype(jnp.bfloat16)
                for a in range(ctx):
                    for p in range(per):
                        at = (p * ctx + a) * part
                        rows_scr[:, at : at + part] = down[(c - a) % ctx][p].astype(jnp.float32)
                out[2] = rows_scr[...].astype(jnp.bfloat16)

    return kernel_call(
        body,
        [((3, chunk, inner), jnp.bfloat16)],
        [where, *pairs, *downs],
        {0: "smem"},
        [pltpu.VMEM((chunk, inner), jnp.float32)],
    )[0]


def join_rows(where, pieces, rows):
    ctx = len(pieces)
    tall, wide = pieces[0].shape
    more = 16 if tall > rows else 0

    def body(where_ref, *rest):
        got, out, rows_scr = rest[:ctx], rest[ctx], rest[ctx + 1]
        mine = where_ref[4]
        if more:
            rows_scr[ctx * rows :, :] = jnp.zeros((more, wide), jnp.float32)
        for c in range(ctx):

            @pl.when(mine == c)
            def _(c=c):
                for a in range(ctx):
                    piece = got[(c - a) % ctx]
                    rows_scr[a * rows : (a + 1) * rows, :] = piece[:rows, :].astype(jnp.float32)
                    if more:
                        at = ctx * rows + a
                        rows_scr[at : at + 1, :] = piece[rows : rows + 1, :].astype(jnp.float32)
                out[...] = rows_scr[...].astype(jnp.bfloat16)

    return kernel_call(
        body,
        [((ctx * rows + more, wide), jnp.bfloat16)],
        [where, *pieces],
        {0: "smem"},
        [pltpu.VMEM((ctx * rows + more, wide), jnp.float32)],
    )[0]


def plane_gather(value):
    size = lax.axis_size("dp")

    def across(item, mask):
        return lax.ppermute(item, "dp", [(i, i ^ mask) for i in range(size)])

    near = [value] + [across(value, m) for m in range(2, size, 2)]
    far = [across(item, 1) for item in near]
    return near + far, list(range(0, size, 2)) + list(range(1, size, 2))


def plane_send(parts):
    size = lax.axis_size("dp")
    return [parts[0]] + [
        lax.ppermute(parts[m], "dp", [(i, i ^ (2 * m)) for i in range(size)])
        for m in range(1, len(parts))
    ]


def ctx_send(parts, sign):
    return [parts[0]] + [shift(parts[k], sign * k) for k in range(1, len(parts))]


def fused(
    tokens,
    cotangent,
    lengths,
    w_query,
    w_key,
    w_value,
    w_out,
    w_gate,
    w_up,
    w_down,
    gain_in,
    gain_query,
    gain_key,
    gain_attn,
    gain_pre,
    gain_post,
):
    count, width = tokens.shape
    seq_count = lengths.shape[1]
    stretch = count // (2 * seq_count)
    dp = lax.axis_size("dp")
    ctx = lax.axis_size("ctx")
    mine = lax.axis_index("ctx")
    group = lax.axis_index("dp")
    head_dim = w_key.shape[1]
    heads = w_query.shape[1] // head_dim
    where = jnp.stack([group, group % 2, group // 2 % 2, group // 4, mine]).astype(jnp.int32)

    gains = [gain_in, gain_query, gain_key, gain_attn, gain_pre, gain_post]
    sizes = [g.shape[0] for g in gains]
    packed = pack(w_query, w_key, w_value, gains)
    w_gate, w_up, w_down, packed = lax.optimization_barrier((w_gate, w_up, w_down, packed))
    qkv_chunk = join_rows(where, ctx_gather(packed), w_query.shape[0])
    out_chunk = join_rows(where, ctx_gather(w_out), w_out.shape[0])
    qkv_pieces, masks = plane_gather(qkv_chunk)
    out_pieces, _ = plane_gather(out_chunk)
    per = dp // ctx
    down = w_down.T.reshape(dp, width // dp, w_down.shape[0])
    down = lax.all_to_all(down, "dp", split_axis=0, concat_axis=0, tiled=True)
    down = ctx_exchange(down.reshape(ctx, per, width // dp, w_down.shape[0]))
    pairs = ctx_send(split_columns(where, w_gate, w_up, ctx), 1)
    shard = join_wide(where, pairs, down)
    cosine, sine, valid, allowed = tables(where, lengths, count, stretch, ctx, head_dim)
    shard_x, shard_y = swap(shard, 1), swap(shard, 2)

    normed, query, both, raw, norm_in, norm_query, norm_key = project(
        where, tokens, qkv_pieces, sizes[:3], cosine, sine, masks, heads, ctx
    )
    norm_attn, norm_pre, norm_post = late_gains(
        where, qkv_pieces, masks, width // dp, [384, 512, 640], sizes[3:], ctx, both
    )
    both = ctx_gather(both)
    probs, mixed, attn_raw, after, normed_two = attend(
        where, tokens, query, both, allowed, valid, norm_attn, norm_pre, out_pieces, masks, heads
    )
    shard_x, shard_y, normed_two = lax.optimization_barrier((shard_x, shard_y, normed_two))
    first = halves_of(width // dp)[0]
    weights = [shard, shard_x, shard_y, swap(shard_x[:, :first], 2), swap(shard_y[:, first:], 1)]
    weights = weights + [swap(w, 0) for w in weights]
    group_two, act, one, two, *sums = feed_forward(where, ctx_gather(normed_two), weights)
    output, ffn_grad, gain_post_grad = finish(
        ctx_send(sums, -1), after, cotangent, valid, norm_post
    )
    group_two_far = swap(group_two, 0)
    act_far = swap(act, 0)
    group_ffn, gate_grad, upper_grad, *sums = feed_back(
        where, ctx_gather(ffn_grad), weights, one, two
    )
    sums = ctx_send(sums, -1)
    group_ffn_far, gate_far, upper_far = (
        swap(group_ffn, 0),
        swap(gate_grad, 0),
        swap(upper_grad, 0),
    )
    send_a, kept_a, send_b, kept_b = wide_grads(
        where,
        group_two,
        group_two_far,
        group_ffn,
        group_ffn_far,
        act,
        act_far,
        gate_grad,
        gate_far,
        upper_grad,
        upper_far,
    )
    sums, send_a, send_b = lax.optimization_barrier((sums, send_a, send_b))
    got_a, got_b = swap(send_a, 1), swap(send_b, 2)
    dx, attn_grad, query_grad, gain_pre_grad, gain_attn_grad, gain_query_grad, *parts = attend_back(
        where,
        sums,
        after,
        cotangent,
        valid,
        attn_raw,
        norm_pre,
        norm_attn,
        norm_query,
        probs,
        query,
        raw,
        both,
        out_pieces,
        cosine,
        sine,
        masks,
        heads,
    )
    parts = ctx_send(parts, -1)
    send_a, kept_a, send_b, kept_b = wide_middle(where, kept_a, got_a, kept_b, got_b)
    out_blocks = plane_send(
        narrow_grads(where, attn_grad, swap(attn_grad, 0), mixed, swap(mixed, 0))
    )
    out_blocks = ctx_send(narrow_middle(where, out_blocks, [mixed.shape[1]], ctx), 1)
    parts, send_a, send_b, out_blocks = lax.optimization_barrier(
        (parts, send_a, send_b, out_blocks)
    )
    got_a, got_b = swap(send_a, 2), swap(send_b, 1)
    input_grad, qkv_grads, gain_rows = project_back(
        where,
        parts,
        raw,
        query_grad,
        tokens,
        dx,
        norm_in,
        norm_key,
        cosine,
        sine,
        qkv_pieces,
        masks,
        heads,
        ctx,
        [gain_query_grad, gain_attn_grad, gain_pre_grad, gain_post_grad],
    )
    blocks = plane_send(
        narrow_grads(
            where,
            normed,
            swap(normed, 0),
            qkv_grads,
            swap(qkv_grads, 0),
            [gain_rows, swap(gain_rows, 0)],
        )
    )
    blocks = ctx_send(
        narrow_middle(where, blocks, [heads * head_dim, head_dim, head_dim], ctx), 1
    )
    grad_gate, grad_up, grad_down = wide_last(
        kept_a, got_a, kept_b, got_b, w_gate.shape[1] // ctx
    )

    def total(pieces):
        result = pieces[0].astype(jnp.float32)
        for p in pieces[1:]:
            result = result + p.astype(jnp.float32)
        return result

    grad_out = total(out_blocks).T
    grad_qkv = total(blocks)

    outs, start = [], 0
    for size in sizes:
        outs.append(grad_qkv[width // dp, start : start + size])
        start += size
    grad_qkv = grad_qkv[: width // dp]
    q_cols, k_cols = heads * head_dim // ctx, head_dim // ctx
    return (
        output,
        input_grad,
        grad_qkv[:, :q_cols],
        grad_qkv[:, q_cols : q_cols + k_cols],
        grad_qkv[:, q_cols + k_cols :],
        grad_out,
        grad_gate,
        grad_up,
        grad_down.T,
        *outs,
    )


def on_device(tokens, cotangent, lengths, *params):
    dp, ctx = lax.axis_size("dp"), lax.axis_size("ctx")
    each = tokens.shape[0] // lengths.shape[1]
    fits = dp == 8 and dp % ctx == 0 and tokens.shape[1] // dp % 16 == 0 and each % 16 == 0
    run = fused if fits else plain
    return run(tokens, cotangent, lengths, *params)


def solution(mesh):
    in_specs = (
        P(("dp", "ctx"), None),
        P(("dp", "ctx"), None),
        P("dp", None),
        P(("dp", "ctx"), None),
        P(("dp", "ctx"), None),
        P(("dp", "ctx"), None),
        P(("dp", "ctx"), None),
        P(("dp", "ctx"), None),
        P(("dp", "ctx"), None),
        P(("dp", "ctx"), None),
        P(("dp", "ctx")),
        P(("dp", "ctx")),
        P(("dp", "ctx")),
        P(("dp", "ctx")),
        P(("dp", "ctx")),
        P(("dp", "ctx")),
    )
    out_specs = (
        P(("dp", "ctx"), None),
        P(("dp", "ctx"), None),
        P("dp", "ctx"),
        P("dp", "ctx"),
        P("dp", "ctx"),
        P("ctx", "dp"),
        P("dp", "ctx"),
        P("dp", "ctx"),
        P("ctx", "dp"),
        P(("dp", "ctx")),
        P(("dp", "ctx")),
        P(("dp", "ctx")),
        P(("dp", "ctx")),
        P(("dp", "ctx")),
        P(("dp", "ctx")),
    )
    return jax.shard_map(
        on_device, mesh=mesh, in_specs=in_specs, out_specs=out_specs, check_vma=False
    )
```

profile of v0, /device:TPU:0, one launch (start us, length us, event | category | flops | bytes accessed | tf_op | source)
XLA Modules:
  0.0 436.3 jit_solution(8139835629857531422)
XLA Ops:
  4.4 5.2 %all-to-all-start = ((bf16[8,144,216]{2,1,0:T(8,128)(2,1)}), bf16[8,144,216]{2,1,0:T(8,128)(2,1)S(1)}, u32[]{:S(2)}, u32[]{:S(2)}) async-start(bf16[8,144,216]{2,1,0:T(8,128)(2,1)} %bitcast.12), calls=%async_computation | async-start | bytes 1179648 | tf_op jit(solution)/shard_map/all_to_all | solution.py:1377
  20.9 19.1 %collective-permute-done.14.rest_2_ = bf16[32,1152]{1,0:T(8,128)(2,1)S(1)} collective-permute-done((bf16[32,1152]{1,0:T(8,128)(2,1)S(1)}, bf16[32,1152]{1,0:T(8,128)(2,1)S(1)}, u32[]{:S(2)}, u32[]{:S(2)}) %collective-permute-start.14) | collective-permute-done | bytes 73760 | tf_op jit(solution)/shard_map/ppermute | solution.py:65
  45.1 5.2 %collective-permute-done.1.rest_2_ = bf16[40,1536]{1,0:T(8,128)(2,1)S(1)} collective-permute-done((bf16[40,1536]{1,0:T(8,128)(2,1)S(1)}, bf16[40,1536]{1,0:T(8,128)(2,1)S(1)}, u32[]{:S(2)}, u32[]{:S(2)}) %collective-permute-start.1) | collective-permute-done | bytes 122912 | tf_op jit(solution)/shard_map/ppermute | solution.py:65
  82.7 9.4 %collective-permute-done.4.rest_2_.rest_6_ = bf16[160,1536]{1,0:T(8,128)(2,1)S(1)} collective-permute-done((bf16[160,1536]{1,0:T(8,128)(2,1)}, bf16[160,1536]{1,0:T(8,128)(2,1)S(1)}, u32[]{:S(2)}, u32[]{:S(2)}) %collective-permute-start.4) | collective-permute-done | bytes 491552 | tf_op jit(solution)/shard_map/ppermute | solution.py:1319
  104.6 5.8 %collective-permute-done.10.rest_1_.rest_5_ = bf16[128,512]{1,0:T(8,128)(2,1)S(1)} collective-permute-done((bf16[128,512]{1,0:T(8,128)(2,1)}, bf16[128,512]{1,0:T(8,128)(2,1)S(1)}, u32[]{:S(2)}, u32[]{:S(2)}) %collective-permute-start.10) | collective-permute-done | bytes 131104 | tf_op jit(solution)/shard_map/ppermute | solution.py:65
  130.0 15.1 %collective-permute-done.31.rest_3_ = bf16[3,80,1728]{2,1,0:T(8,128)(2,1)S(1)} collective-permute-done((bf16[3,80,1728]{2,1,0:T(8,128)(2,1)S(1)}, bf16[3,80,1728]{2,1,0:T(8,128)(2,1)S(1)}, u32[]{:S(2)}, u32[]{:S(2)}) %collective-permute-start.31) | collective-permute-done | bytes 829472 | tf_op jit(solution)/shard_map/ppermute | solution.py:60
  146.6 15.3 %collective-permute-done.39.rest_12_ = bf16[128,1152]{1,0:T(8,128)(2,1)S(1)} collective-permute-done((bf16[128,1152]{1,0:T(8,128)(2,1)S(1)}, bf16[128,1152]{1,0:T(8,128)(2,1)S(1)}, u32[]{:S(2)}, u32[]{:S(2)}) %collective-permute-start.39) | collective-permute-done | bytes 294944 | tf_op jit(solution)/shard_map/ppermute | solution.py:65
  163.9 6.5 %collective-permute-done.40.rest_13_ = bf16[128,1152]{1,0:T(8,128)(2,1)S(1)} collective-permute-done((bf16[128,1152]{1,0:T(8,128)(2,1)S(1)}, bf16[128,1152]{1,0:T(8,128)(2,1)S(1)}, u32[]{:S(2)}, u32[]{:S(2)}) %collective-permute-start.40) | collective-permute-done | bytes 294944 | tf_op jit(solution)/shard_map/ppermute | solution.py:65
  173.3 15.3 %shard_map.289 = (bf16[512,1152]{1,0:T(8,128)(2,1)}, bf16[512,1792]{1,0:T(8,128)(2,1)}, bf16[512,1728]{1,0:T(8,128)(2,1)}, bf16[512,1728]{1,0:T(8,128)(2,1)}, f3...) custom-call(s32[5]{0:T(128)} %stack.23.where_ref, ...), custom_call_target="tpu_custom_call" | custom-call | flops 6115295232 | bytes 21151764 | tf_op jit(solution)/shard_map/pallas_call | solution.py:428
  193.6 7.2 %collective-permute-done.41.rest_1_ = bf16[128,1152]{1,0:T(8,128)(2,1)S(1)} collective-permute-done((bf16[128,1152]{1,0:T(8,128)(2,1)}, bf16[128,1152]{1,0:T(8,128)(2,1)S(1)}, u32[]{:S(2)}, u32[]{:S(2)}) %collective-permute-start.41) | collective-permute-done | bytes 294944 | tf_op jit(solution)/shard_map/ppermute | solution.py:65
  200.8 15.0 %collective-permute-done.42.rest_2_ = bf16[128,1152]{1,0:T(8,128)(2,1)S(1)} collective-permute-done((bf16[128,1152]{1,0:T(8,128)(2,1)}, bf16[128,1152]{1,0:T(8,128)(2,1)S(1)}, u32[]{:S(2)}, u32[]{:S(2)}) %collective-permute-start.42) | collective-permute-done | bytes 294944 | tf_op jit(solution)/shard_map/ppermute | solution.py:65
  226.8 4.7 %collective-permute-done.44.rest_11_ = bf16[128,1152]{1,0:T(8,128)(2,1)S(1)} collective-permute-done((bf16[128,1152]{1,0:T(8,128)(2,1)}, bf16[128,1152]{1,0:T(8,128)(2,1)S(1)}, u32[]{:S(2)}, u32[]{:S(2)}) %collective-permute-start.44) | collective-permute-done | bytes 294944 | tf_op jit(solution)/shard_map/ppermute | solution.py:65
  231.6 10.5 %collective-permute-done.45.rest_12_ = bf16[128,1152]{1,0:T(8,128)(2,1)S(1)} collective-permute-done((bf16[128,1152]{1,0:T(8,128)(2,1)}, bf16[128,1152]{1,0:T(8,128)(2,1)S(1)}, u32[]{:S(2)}, u32[]{:S(2)}) %collective-permute-start.45) | collective-permute-done | bytes 294944 | tf_op jit(solution)/shard_map/ppermute | solution.py:65
  242.9 14.4 %shard_map.291 = (bf16[512,1152]{1,0:T(8,128)(2,1)}, bf16[512,1792]{1,0:T(8,128)(2,1)}, bf16[512,1792]{1,0:T(8,128)(2,1)}, f32[128,1152]{1,0:T(8,128)}, bf16[128...) custom-call(s32[5]{0:T(128)} %stack.23.where_ref, ...), custom_call_target="tpu_custom_call" | custom-call | flops 6115295232 | bytes 22986772 | tf_op jit(solution)/shard_map/pallas_call | solution.py:428
  258.4 7.8 %collective-permute-done.50.rest_1_ = bf16[512,1152]{1,0:T(8,128)(2,1)S(1)} collective-permute-done((bf16[512,1152]{1,0:T(8,128)(2,1)S(1)}, bf16[512,1152]{1,0:T(8,128)(2,1)S(1)}, u32[]{:S(2)}, u32[]{:S(2)}) %collective-permute-start.50) | collective-permute-done | bytes 1179680 | tf_op jit(solution)/shard_map/ppermute | solution.py:60
  266.2 9.9 %collective-permute-start.47 = (bf16[128,1152]{1,0:T(8,128)(2,1)}, bf16[128,1152]{1,0:T(8,128)(2,1)S(1)}, u32[]{:S(2)}, u32[]{:S(2)}) collective-permute-start(bf16[128,1152]{1,0:T(8,128)(2,1)} %get-tuple-element.154), channel_id=1, source_target_pairs={{0,3},{1,0},{2,1},{3,2},{4,7},{5,4},{6,5},{7,6},{8,11},{9,8},{10,9... | collective-permute-start | bytes 884744 | tf_op jit(solution)/shard_map/ppermute | solution.py:65
  278.5 15.3 %shard_map.292 = (bf16[3,160,1792]{2,1,0:T(8,128)(2,1)}, bf16[3,160,1792]{2,1,0:T(8,128)(2,1)}, bf16[3,128,1792]{2,1,0:T(8,128)(2,1)}, bf16[3,128,1792]{2,1,0:T(8,128)(2,1)}) custom-call(s32[5]{0:T(128)} %stack.23.where_ref, bf16[512,1152]{1,0:T(8,128)(2,1)} %get-tuple-element.157.rest_0_, bf16[512,1152]{1,0:T(8,128)(2,1)} %copy-done.58, ...), custom_call_target="tpu_custom_call" | custom-call | flops 6341787648 | bytes 21921812 | tf_op jit(solution)/shard_map/pallas_call | solution.py:428
  293.8 7.3 %collective-permute-done.48.rest_2_ = bf16[128,1152]{1,0:T(8,128)(2,1)S(1)} collective-permute-done((bf16[128,1152]{1,0:T(8,128)(2,1)}, bf16[128,1152]{1,0:T(8,128)(2,1)S(1)}, u32[]{:S(2)}, u32[]{:S(2)}) %collective-permute-start.48) | collective-permute-done | bytes 294944 | tf_op jit(solution)/shard_map/ppermute | solution.py:65
  303.2 6.7 %shard_map.293 = (f32[128,1152]{1,0:T(8,128)}, bf16[128,1152]{1,0:T(8,128)(2,1)}, bf16[128,1024]{1,0:T(8,128)(2,1)}, f32[1,1152]{1,0:T(1,128)}, f32[1,1152]{1,0:...) custom-call(s32[5]{0:T(128)} %stack.23.where_ref, ...), custom_call_target="tpu_custom_call" | custom-call | flops 637534208 | bytes 9359892 | tf_op jit(solution)/shard_map/pallas_call | solution.py:428
  320.0 28.2 %collective-permute-done.62.rest_1_ = bf16[144,1024]{1,0:T(8,128)(2,1)S(1)} collective-permute-done((bf16[144,1024]{1,0:T(8,128)(2,1)}, bf16[144,1024]{1,0:T(8,128)(2,1)S(1)}, u32[]{:S(2)}, u32[]{:S(2)}) %collective-permute-start.62) | collective-permute-done | bytes 294944 | tf_op jit(solution)/shard_map/ppermute | solution.py:1329
  362.7 5.1 %shard_map.294 = (bf16[3,80,1792]{2,1,0:T(8,128)(2,1)}, bf16[3,80,1792]{2,1,0:T(8,128)(2,1)}, bf16[3,64,1792]{2,1,0:T(8,128)(2,1)}, bf16[3,64,1792]{2,1,0:T(8,128)(2,1)}) custom-call(s32[5]{0:T(128)} %stack.23.where_ref, bf16[3,160,1792]{2,1,0:T(8,128)(2,1)} %get-tuple-element.176.kept_a_ref, bf16[3,160,1792]{2,1,0:T(8,128)(2,1)} %copy-done.8, ...), custom_call_target="tpu_custom_call" | custom-call | bytes 9289748 | tf_op jit(solution)/shard_map/pallas_call | solution.py:428
  368.5 5.4 %shard_map.297 = (bf16[128,1152]{1,0:T(8,128)(2,1)}, bf16[128,1536]{1,0:T(8,128)(2,1)}, f32[8,1536]{1,0:T(8,128)}) custom-call(s32[5]{0:T(128)} %stack.23.where_ref, f32[128,1280]{1,0:T(8,128)} %get-tuple-element.146.raw_ref, bf16[128,1024]{1,0:T(8,128)(2,1)} %get-tuple-element.168.query_ref, bf16[128,1152]{1,0:T(8,128)(2,1)} %x_ref.5, ...), custom_call_target="tpu_custom_call" | custom-call | flops 452984832 | bytes 7409684 | tf_op jit(solution)/shard_map/pallas_call | solution.py:428
  387.5 9.3 %collective-permute-done.71.rest_1_ = bf16[160,1536]{1,0:T(8,128)(2,1)S(1)} collective-permute-done((bf16[160,1536]{1,0:T(8,128)(2,1)}, bf16[160,1536]{1,0:T(8,128)(2,1)S(1)}, u32[]{:S(2)}, u32[]{:S(2)}) %collective-permute-start.71) | collective-permute-done | bytes 491552 | tf_op jit(solution)/shard_map/ppermute | solution.py:1329
  396.8 19.8 %collective-permute-done.72.rest_2_ = bf16[160,1536]{1,0:T(8,128)(2,1)S(1)} collective-permute-done((bf16[160,1536]{1,0:T(8,128)(2,1)}, bf16[160,1536]{1,0:T(8,128)(2,1)S(1)}, u32[]{:S(2)}, u32[]{:S(2)}) %collective-permute-start.72) | collective-permute-done | bytes 491552 | tf_op jit(solution)/shard_map/ppermute | solution.py:1329
  (330 shorter events, 171.0 us)
Async XLA Ops:
  4.4 55.6 %all-to-all-start = ((bf16[8,144,216]{2,1,0:T(8,128)(2,1)}), bf16[8,144,216]{2,1,0:T(8,128)(2,1)S(1)}, u32[]{:S(2)}, u32[]{:S(2)}) async-start(bf16[8,144,216]{2,1,0:T(8,128)(2,1)} %bitcast.12), calls=%async_computation | async-start | bytes 1179648 | tf_op jit(solution)/shard_map/all_to_all | solution.py:1377
  14.3 41.8 %collective-permute-start.23 = (bf16[2,36,1728]{2,1,0:T(8,128)(2,1)}, bf16[2,36,1728]{2,1,0:T(8,128)(2,1)S(1)}, u32[]{:S(2)}, u32[]{:S(2)}) collective-permute-start(bf16[2,36,1728]{2,1,0:T(8,128)(2,1)} %get-tuple-element.133), channel_id=1, source_target_pairs={{0,1},{1,2},{2,3},{3,0},{4,5},{5,6},{6,7},{7,4},{8,9},{9,10},{10,1... | collective-permute-start | bytes 746504 | tf_op jit(solution)/shard_map/ppermute | solution.py:65
  15.9 24.0 %collective-permute-start.14 = (bf16[32,1152]{1,0:T(8,128)(2,1)S(1)}, bf16[32,1152]{1,0:T(8,128)(2,1)S(1)}, u32[]{:S(2)}, u32[]{:S(2)}) collective-permute-start(bf16[32,1152]{1,0:T(8,128)(2,1)S(1)} %copy-done.49), channel_id=1, source_target_pairs={{0,2},{1,3},{2,0},{3,1},{4,6},{5,7},{6,4},{7,5},{8,10},{9,11},{10,... | collective-permute-start | bytes 221192 | tf_op jit(solution)/shard_map/ppermute | solution.py:65
  19.9 39.8 %collective-permute-start.24 = (bf16[2,36,1728]{2,1,0:T(8,128)(2,1)}, bf16[2,36,1728]{2,1,0:T(8,128)(2,1)S(1)}, u32[]{:S(2)}, u32[]{:S(2)}) collective-permute-start(bf16[2,36,1728]{2,1,0:T(8,128)(2,1)} %get-tuple-element.134), channel_id=1, source_target_pairs={{0,2},{1,3},{2,0},{3,1},{4,6},{5,7},{6,4},{7,5},{8,10},{9,11},{10,... | collective-permute-start | bytes 746504 | tf_op jit(solution)/shard_map/ppermute | solution.py:65
  67.2 24.9 %collective-permute-start.4 = (bf16[160,1536]{1,0:T(8,128)(2,1)}, bf16[160,1536]{1,0:T(8,128)(2,1)S(1)}, u32[]{:S(2)}, u32[]{:S(2)}) collective-permute-start(bf16[160,1536]{1,0:T(8,128)(2,1)} %shard_map.282.rest_0_.rest_4_), channel_id=1, source_target_pairs={{0,16},{4,20},{8,24},{12,28},{16,0},{20,4},{24,8},{28,12},{1,17},{... | collective-permute-start | bytes 1474568 | tf_op jit(solution)/shard_map/ppermute | solution.py:1319
  80.4 41.7 %collective-permute-start.29 = (bf16[3,144,1728]{2,1,0:T(8,128)(2,1)}, bf16[3,144,1728]{2,1,0:T(8,128)(2,1)}, u32[]{:S(2)}, u32[]{:S(2)}) collective-permute-start(bf16[3,144,1728]{2,1,0:T(8,128)(2,1)} %shard_map.288.rest_0_), channel_id=1, source_target_pairs={{0,8},{4,12},{8,0},{12,4},{16,24},{20,28},{24,16},{28,20},{1,9},{5... | collective-permute-start | bytes 4478984 | tf_op jit(solution)/shard_map/ppermute | solution.py:60
  81.3 42.7 %collective-permute-start.30 = (bf16[3,144,1728]{2,1,0:T(8,128)(2,1)}, bf16[3,144,1728]{2,1,0:T(8,128)(2,1)}, u32[]{:S(2)}, u32[]{:S(2)}) collective-permute-start(bf16[3,144,1728]{2,1,0:T(8,128)(2,1)} %shard_map.288.rest_0_), channel_id=1, source_target_pairs={{0,16},{4,20},{8,24},{12,28},{16,0},{20,4},{24,8},{28,12},{1,17},{... | collective-permute-start | bytes 4478984 | tf_op jit(solution)/shard_map/ppermute | solution.py:60
  94.4 34.8 %collective-permute-start.33 = (bf16[3,144,1728]{2,1,0:T(8,128)(2,1)}, bf16[3,144,1728]{2,1,0:T(8,128)(2,1)}, u32[]{:S(2)}, u32[]{:S(2)}) collective-permute-start(bf16[3,144,1728]{2,1,0:T(8,128)(2,1)} %shard_map.288.rest_0_), channel_id=1, source_target_pairs={{0,4},{4,0},{8,12},{12,8},{16,20},{20,16},{24,28},{28,24},{1,5},{5... | collective-permute-start | bytes 4478984 | tf_op jit(solution)/shard_map/ppermute | solution.py:60
  126.2 44.2 %collective-permute-start.34 = (bf16[3,144,1728]{2,1,0:T(8,128)(2,1)}, bf16[3,144,1728]{2,1,0:T(8,128)(2,1)S(1)}, u32[]{:S(2)}, u32[]{:S(2)}) collective-permute-start(bf16[3,144,1728]{2,1,0:T(8,128)(2,1)} %collective-permute-done.29.rest_1_), channel_id=1, source_target_pairs={{0,4},{4,0},{8,12},{12,8},{16,20},{20,16},{24,28},{28,24},{1,5},{5... | collective-permute-start | bytes 4478984 | tf_op jit(solution)/shard_map/ppermute | solution.py:60
  126.2 44.2 %collective-permute-start.35 = (bf16[3,144,1728]{2,1,0:T(8,128)(2,1)}, bf16[3,144,1728]{2,1,0:T(8,128)(2,1)S(1)}, u32[]{:S(2)}, u32[]{:S(2)}) collective-permute-start(bf16[3,144,1728]{2,1,0:T(8,128)(2,1)} %collective-permute-done.30.rest_2_), channel_id=1, source_target_pairs={{0,4},{4,0},{8,12},{12,8},{16,20},{20,16},{24,28},{28,24},{1,5},{5... | collective-permute-start | bytes 4478984 | tf_op jit(solution)/shard_map/ppermute | solution.py:60
  145.1 26.1 %collective-permute-start.36 = (bf16[3,80,1728]{2,1,0:T(8,128)(2,1)S(1)}, bf16[3,80,1728]{2,1,0:T(8,128)(2,1)S(1)}, u32[]{:S(2)}, u32[]{:S(2)}) collective-permute-start(bf16[3,80,1728]{2,1,0:T(8,128)(2,1)S(1)} %collective-permute-done.31.rest_3_), channel_id=1, source_target_pairs={{0,4},{4,0},{8,12},{12,8},{16,20},{20,16},{24,28},{28,24},{1,5},{5... | collective-permute-start | bytes 2488328 | tf_op jit(solution)/shard_map/ppermute | solution.py:60
  145.3 25.1 %collective-permute-start.37 = (bf16[3,64,1728]{2,1,0:T(8,128)(2,1)S(1)}, bf16[3,64,1728]{2,1,0:T(8,128)(2,1)S(1)}, u32[]{:S(2)}, u32[]{:S(2)}) collective-permute-start(bf16[3,64,1728]{2,1,0:T(8,128)(2,1)S(1)} %collective-permute-done.32.rest_4_), channel_id=1, source_target_pairs={{0,4},{4,0},{8,12},{12,8},{16,20},{20,16},{24,28},{28,24},{1,5},{5... | collective-permute-start | bytes 1990664 | tf_op jit(solution)/shard_map/ppermute | solution.py:60
  226.8 49.3 %collective-permute-start.52 = (bf16[512,1792]{1,0:T(8,128)(2,1)S(1)}, bf16[512,1792]{1,0:T(8,128)(2,1)S(1)}, u32[]{:S(2)}, u32[]{:S(2)}) collective-permute-start(bf16[512,1792]{1,0:T(8,128)(2,1)S(1)} %copy-done.53), channel_id=1, source_target_pairs={{0,4},{4,0},{8,12},{12,8},{16,20},{20,16},{24,28},{28,24},{1,5},{5... | collective-permute-start | bytes 5505032 | tf_op jit(solution)/shard_map/ppermute | solution.py:60
  266.2 27.6 %collective-permute-start.47 = (bf16[128,1152]{1,0:T(8,128)(2,1)}, bf16[128,1152]{1,0:T(8,128)(2,1)S(1)}, u32[]{:S(2)}, u32[]{:S(2)}) collective-permute-start(bf16[128,1152]{1,0:T(8,128)(2,1)} %get-tuple-element.154), channel_id=1, source_target_pairs={{0,3},{1,0},{2,1},{3,2},{4,7},{5,4},{6,5},{7,6},{8,11},{9,8},{10,9... | collective-permute-start | bytes 884744 | tf_op jit(solution)/shard_map/ppermute | solution.py:65
  276.2 24.9 %collective-permute-start.48 = (bf16[128,1152]{1,0:T(8,128)(2,1)}, bf16[128,1152]{1,0:T(8,128)(2,1)S(1)}, u32[]{:S(2)}, u32[]{:S(2)}) collective-permute-start(bf16[128,1152]{1,0:T(8,128)(2,1)} %get-tuple-element.155), channel_id=1, source_target_pairs={{0,2},{1,3},{2,0},{3,1},{4,6},{5,7},{6,4},{7,5},{8,10},{9,11},{10,... | collective-permute-start | bytes 884744 | tf_op jit(solution)/shard_map/ppermute | solution.py:65
  301.1 58.6 %collective-permute-start.58 = (bf16[3,160,1792]{2,1,0:T(8,128)(2,1)}, bf16[3,160,1792]{2,1,0:T(8,128)(2,1)S(1)}, u32[]{:S(2)}, u32[]{:S(2)}) collective-permute-start(bf16[3,160,1792]{2,1,0:T(8,128)(2,1)} %get-tuple-element.177), channel_id=1, source_target_pairs={{0,8},{4,12},{8,0},{12,4},{16,24},{20,28},{24,16},{28,20},{1,9},{5... | collective-permute-start | bytes 5160968 | tf_op jit(solution)/shard_map/ppermute | solution.py:60
  302.6 56.7 %collective-permute-start.59 = (bf16[3,128,1792]{2,1,0:T(8,128)(2,1)}, bf16[3,128,1792]{2,1,0:T(8,128)(2,1)S(1)}, u32[]{:S(2)}, u32[]{:S(2)}) collective-permute-start(bf16[3,128,1792]{2,1,0:T(8,128)(2,1)} %get-tuple-element.179), channel_id=1, source_target_pairs={{0,16},{4,20},{8,24},{12,28},{16,0},{20,4},{24,8},{28,12},{1,17},{... | collective-permute-start | bytes 4128776 | tf_op jit(solution)/shard_map/ppermute | solution.py:60
  316.5 31.7 %collective-permute-start.62 = (bf16[144,1024]{1,0:T(8,128)(2,1)}, bf16[144,1024]{1,0:T(8,128)(2,1)S(1)}, u32[]{:S(2)}, u32[]{:S(2)}) collective-permute-start(bf16[144,1024]{1,0:T(8,128)(2,1)} %get-tuple-element.185), channel_id=1, source_target_pairs={{0,8},{4,12},{8,0},{12,4},{16,24},{20,28},{24,16},{28,20},{1,9},{5... | collective-permute-start | bytes 884744 | tf_op jit(solution)/shard_map/ppermute | solution.py:1329
  317.2 31.0 %collective-permute-start.63 = (bf16[144,1024]{1,0:T(8,128)(2,1)}, bf16[144,1024]{1,0:T(8,128)(2,1)S(1)}, u32[]{:S(2)}, u32[]{:S(2)}) collective-permute-start(bf16[144,1024]{1,0:T(8,128)(2,1)} %get-tuple-element.186), channel_id=1, source_target_pairs={{0,16},{4,20},{8,24},{12,28},{16,0},{20,4},{24,8},{28,12},{1,17},{... | collective-permute-start | bytes 884744 | tf_op jit(solution)/shard_map/ppermute | solution.py:1329
  318.5 34.4 %collective-permute-start.64 = (bf16[144,1024]{1,0:T(8,128)(2,1)}, bf16[144,1024]{1,0:T(8,128)(2,1)S(1)}, u32[]{:S(2)}, u32[]{:S(2)}) collective-permute-start(bf16[144,1024]{1,0:T(8,128)(2,1)} %get-tuple-element.187), channel_id=1, source_target_pairs={{0,24},{4,28},{8,16},{12,20},{16,8},{20,12},{24,0},{28,4},{1,25},{... | collective-permute-start | bytes 884744 | tf_op jit(solution)/shard_map/ppermute | solution.py:1329
  374.5 50.6 %collective-permute-start.77 = (bf16[3,80,1792]{2,1,0:T(8,128)(2,1)S(1)}, bf16[3,80,1792]{2,1,0:T(8,128)(2,1)S(1)}, u32[]{:S(2)}, u32[]{:S(2)}) collective-permute-start(bf16[3,80,1792]{2,1,0:T(8,128)(2,1)S(1)} %copy-done.60), channel_id=1, source_target_pairs={{0,16},{4,20},{8,24},{12,28},{16,0},{20,4},{24,8},{28,12},{1,17},{... | collective-permute-start | bytes 2580488 | tf_op jit(solution)/shard_map/ppermute | solution.py:60
  384.0 32.6 %collective-permute-start.72 = (bf16[160,1536]{1,0:T(8,128)(2,1)}, bf16[160,1536]{1,0:T(8,128)(2,1)S(1)}, u32[]{:S(2)}, u32[]{:S(2)}) collective-permute-start(bf16[160,1536]{1,0:T(8,128)(2,1)} %get-tuple-element.206), channel_id=1, source_target_pairs={{0,16},{4,20},{8,24},{12,28},{16,0},{20,4},{24,8},{28,12},{1,17},{... | collective-permute-start | bytes 1474568 | tf_op jit(solution)/shard_map/ppermute | solution.py:1329
  384.6 32.1 %collective-permute-start.73 = (bf16[160,1536]{1,0:T(8,128)(2,1)}, bf16[160,1536]{1,0:T(8,128)(2,1)S(1)}, u32[]{:S(2)}, u32[]{:S(2)}) collective-permute-start(bf16[160,1536]{1,0:T(8,128)(2,1)} %get-tuple-element.207), channel_id=1, source_target_pairs={{0,24},{4,28},{8,16},{12,20},{16,8},{20,12},{24,0},{28,4},{1,25},{... | collective-permute-start | bytes 1474568 | tf_op jit(solution)/shard_map/ppermute | solution.py:1329
  386.0 39.0 %collective-permute-start.78 = (bf16[3,64,1792]{2,1,0:T(8,128)(2,1)S(1)}, bf16[3,64,1792]{2,1,0:T(8,128)(2,1)S(1)}, u32[]{:S(2)}, u32[]{:S(2)}) collective-permute-start(bf16[3,64,1792]{2,1,0:T(8,128)(2,1)S(1)} %copy-done.63), channel_id=1, source_target_pairs={{0,8},{4,12},{8,0},{12,4},{16,24},{20,28},{24,16},{28,20},{1,9},{5... | collective-permute-start | bytes 2064392 | tf_op jit(solution)/shard_map/ppermute | solution.py:60
  (136 other events, 1403.8 us)
where the time goes:
time: 445 us; the launch traced here: 436 us
  waiting for transfers between devices  210 us (47%)
  Pallas kernels  105 us (24%)
  starting transfers between devices  95.4 us (21%)
  local copies, waits for them, and re-layouts  23.2 us (5%)
    ppermute x36, waiting for transfers between devices, shift(): lax.ppermute(value, 'ctx', [(i, (i + step) % size) for i in range(size)])  110 us
    pallas_call x21, Pallas kernels, kernel_call(): pl.pallas_call(body, out_shape=[jax.ShapeDtypeStruct(s, t) for s, t in ou...  105 us
    ppermute x36, starting transfers between devices, shift(): lax.ppermute(value, 'ctx', [(i, (i + step) % size) for i in range(size)])  61.4 us
    ppermute x6, waiting for transfers between devices, plane_send(): lax.ppermute(parts[m], 'dp', [(i, i ^ 2 * m) for i in range(size)])  58.6 us
    ppermute x23, waiting for transfers between devices, swap(): return lax.ppermute(value, 'dp', [(i, i ^ 1 << bit) for i in range(size)])  27.9 us
    unnamed x162, local copies, waits for them, and re-layouts  15.5 us
    ppermute x14, waiting for transfers between devices, across(): return lax.ppermute(item, 'dp', [(i, i ^ mask) for i in range(size)])  13 us
    ppermute x23, starting transfers between devices, swap(): return lax.ppermute(value, 'dp', [(i, i ^ 1 << bit) for i in range(size)])  12.6 us
  transfers between devices with their start and end apart: 80, of which 34 were waited for; matrix products, arithmetic and copies ran while one was open for 1% of the time, Pallas kernels for 18%

commit v1 on v0

--- a/solution.py
+++ b/solution.py
@@ -421,17 +421,15 @@
     return {"vmem": pl.BlockSpec(memory_space=pltpu.VMEM), "smem": pl.BlockSpec(memory_space=pltpu.SMEM), "any": pl.BlockSpec(memory_space=pl.ANY)}[name]
 
 
-def kernel_call(body, outs, args, where=None, scratch=(), flops=0):
+def kernel_call(body, outs, args, where=None, scratch=(), flops=0, size=0):
     where = where or {}
-    size = sum(a.size * a.dtype.itemsize for a in args)
-    size += sum(int(np.prod(s)) * jnp.dtype(t).itemsize for s, t in outs)
     return pl.pallas_call(
         body,
         out_shape=[jax.ShapeDtypeStruct(s, t) for s, t in outs],
         in_specs=[place(where.get(i, "vmem")) for i in range(len(args))],
         out_specs=[place("vmem") for _ in outs],
         scratch_shapes=list(scratch),
-        compiler_params=pltpu.CompilerParams(vmem_limit_bytes=58 * mega),
+        compiler_params=pltpu.CompilerParams(vmem_limit_bytes=121 * mega // 2),
         cost_estimate=pl.CostEstimate(flops=flops, bytes_accessed=size, transcendentals=0),
     )(*args)
 
@@ -444,15 +442,9 @@
     return value_grad, jnp.sum(grad * normed, axis=0, keepdims=True)
 
 
-def put_rows(target, at, pieces, masks, rows):
-    for piece, mask in zip(pieces, masks):
-        start = pl.multiple_of((at ^ mask) * rows, 16)
-        target[pl.ds(start, rows), :] = piece[:rows, :]
-
-
-def spread(where_ref, parts, masks, rows, lane, size, ctx):
-    dp = len(parts)
-    shards = jnp.concatenate([p[rows:, lane : lane + 128] for p in parts], axis=0)
+def spread(index, tails, lane, size, ctx):
+    dp = len(tails)
+    shards = jnp.concatenate([t[:, lane : lane + 128] for t, _ in tails], axis=0)
     tail = shards.shape[0] // dp
     whole = dp * ctx * size
     column = lax.broadcasted_iota(jnp.int32, (128, whole), 1)
@@ -462,34 +454,35 @@
     column = lax.broadcasted_iota(jnp.int32, (tail, whole), 1) // size
     line = lax.broadcasted_iota(jnp.int32, (tail, whole), 0)
     total = jnp.zeros((tail, whole), jnp.float32)
-    for k, mask in enumerate(masks):
-        owner = jnp.where(line < ctx, (where_ref[0] ^ mask) * ctx + line, -1)
+    for k, (_, mask) in enumerate(tails):
+        owner = jnp.where(line < ctx, (index ^ mask) * ctx + line, -1)
         total = total + jnp.where(column == owner, values[k * tail : (k + 1) * tail], 0.0)
     return jnp.sum(total, axis=0, keepdims=True)
 
 
-def pack(w_query, w_key, w_value, gains):
+def pack(w_query, w_key, w_value, w_out, gains):
     rows = w_query.shape[0]
-    ends = np.cumsum([w_query.shape[1], w_key.shape[1], w_value.shape[1]])
-    tall = -(-(rows + 1) // 8) * 8
-
-    def body(query_ref, key_ref, value_ref, *rest):
-        shards, out, wide = rest[: len(gains)], rest[-2], rest[-1]
-        wide[rows:, :] = jnp.zeros((tall - rows, wide.shape[1]), jnp.float32)
-        wide[:rows, : ends[0]] = query_ref[...].astype(jnp.float32)
-        wide[:rows, ends[0] : ends[1]] = key_ref[...].astype(jnp.float32)
-        wide[:rows, ends[1] :] = value_ref[...].astype(jnp.float32)
+    parts = [w_query, w_key, w_value, w_out]
+    ends = [int(e) for e in np.cumsum([0] + [p.shape[1] for p in parts])]
+    tall = -(-max(rows + 1, w_out.shape[0]) // 8) * 8
+
+    def body(*rest):
+        shards, lines = rest[: len(parts)], rest[len(parts) : len(parts) + len(gains)]
+        out, wide = rest[-2], rest[-1]
+        wide[...] = jnp.zeros(wide.shape, jnp.float32)
         for i, shard in enumerate(shards):
-            wide[rows : rows + 1, i * 128 : i * 128 + shard.shape[1]] = shard[...].astype(
+            wide[: shard.shape[0], ends[i] : ends[i + 1]] = shard[...].astype(jnp.float32)
+        for i, line in enumerate(lines):
+            wide[rows : rows + 1, i * 128 : i * 128 + line.shape[1]] = line[...].astype(
                 jnp.float32
             )
         out[...] = wide[...].astype(jnp.bfloat16)
 
     return kernel_call(
         body,
-        [((tall, int(ends[2])), jnp.bfloat16)],
-        [w_query, w_key, w_value, *[g.reshape(1, -1) for g in gains]],
-        scratch=[pltpu.VMEM((tall, int(ends[2])), jnp.float32)],
+        [((tall, ends[-1]), jnp.bfloat16)],
+        [*parts, *[g.reshape(1, -1) for g in gains]],
+        scratch=[pltpu.VMEM((tall, ends[-1]), jnp.float32)],
     )[0]
 
 
@@ -535,36 +528,77 @@
     )
 
 
-def late_gains(where, pieces, masks, rows, lanes, sizes, ctx, after):
-    def body(where_ref, after_ref, *rest):
+def plane_near(value):
+    return [value, swap(value, 1), swap(value, 2)]
+
+
+def cut(near):
+    row = near[0].ndim - 2
+    first = halves_of(near[0].shape[row])[0]
+    low = lax.slice_in_dim(near[1], 0, first, axis=row)
+    high = lax.slice_in_dim(near[2], first, None, axis=row)
+    return [low, high]
+
+
+def diagonal(halves):
+    return [swap(halves[0], 2), swap(halves[1], 1)]
+
+
+def plane_whole(near):
+    pieces = near + diagonal(cut(near))
+    return pieces + [swap(p, 0) for p in pieces]
+
+
+def late_gains(where, pieces, lanes, sizes, ctx, behind):
+    tall = pieces[0].shape[0]
+
+    def body(where_ref, behind_ref, *rest):
         parts, outs = rest[: len(pieces)], rest[len(pieces) :]
+        tails = tails_of(parts, tall)
         for out, lane, size in zip(outs, lanes, sizes):
-            out[...] = spread(where_ref, parts, masks, rows, lane, size, ctx)
+            out[...] = spread(where_ref[0], tails, lane, size, ctx)
 
     return kernel_call(
         body,
-        [((1, len(pieces) * ctx * size), jnp.float32) for size in sizes],
-        [where, after, *pieces],
+        [((1, len(tails_of([np.zeros((tall, 1))] * len(pieces), tall)) * ctx * size), jnp.float32) for size in sizes],
+        [where, behind, *pieces],
         {0: "smem", 1: "any"},
     )
 
 
-def project(where, tokens, pieces, sizes, cosine, sine, masks, heads, ctx):
+def project(where, tokens, pieces, sizes, cosine, sine, heads, ctx):
     count, width = tokens.shape
-    wide = pieces[0].shape[1]
+    tall = pieces[0].shape[0]
     head_dim = cosine.shape[1]
+    wide = (heads + 2) * head_dim
     total = len(pieces)
-    rows = width // total
 
     def body(where_ref, x_ref, cos_ref, sin_ref, *rest):
         parts = rest[:total]
-        normed_ref, query_out, both_out, raw_out, in_ref, query_ref, key_ref, weight = rest[total:]
+        normed_ref, query_out, both_out, raw_out, in_ref, query_ref, key_ref = rest[total : total + 7]
+        weight, ends, sems, end_sems = rest[total + 7 :]
+        copies = load_columns(where_ref[0], parts, tall, tall - 16, 0, weight, sems)
+        tails = [
+            (ref, mask, rows) for ref, mask, at, rows in pieces_of(parts, tall) if at + rows == tall
+        ]
+        end_copies = [
+            pltpu.make_async_copy(
+                ref.at[pl.ds(rows - 16, 16), pl.ds(0, ends.shape[2])], ends.at[i], end_sems.at[i]
+            )
+            for i, (ref, _, rows) in enumerate(tails)
+        ]
+        for copy in end_copies:
+            copy.start()
+        for copy in end_copies:
+            copy.wait()
+        tails = [(ends[i], mask) for i, (_, mask, _) in enumerate(tails)]
         for i, ref in enumerate((in_ref, query_ref, key_ref)):
-            ref[...] = spread(where_ref, parts, masks, rows, i * 128, sizes[i], ctx)
-        put_rows(weight, where_ref[0], parts, masks, rows)
+            ref[...] = spread(where_ref[0], tails, i * 128, sizes[i], ctx)
         normed = rms_norm(x_ref[...].astype(jnp.float32), in_ref[...]).astype(jnp.bfloat16)
         normed_ref[...] = normed
         cos, sin = cos_ref[...], sin_ref[...]
+        for copy in copies:
+            copy.wait()
         for h in range(heads + 1):
             cols = slice(h * head_dim, (h + 1) * head_dim)
             raw = dot(normed, weight[:, cols], 1, 0)
@@ -591,23 +625,30 @@
             ((1, head_dim), jnp.float32),
         ],
         [where, tokens, cosine, sine, *pieces],
-        {0: "smem"},
-        [pltpu.VMEM((width, wide), jnp.bfloat16)],
-        2 * count * width * wide,
-    )
-
-
-def attend(where, tokens, query, both, allowed, valid, norm_attn, norm_pre, pieces, masks, heads):
+        {0: "smem", **{4 + i: "any" for i in range(total)}},
+        [
+            pltpu.VMEM((width, wide), jnp.bfloat16),
+            pltpu.VMEM((8, 16, 384), jnp.bfloat16),
+            pltpu.SemaphoreType.DMA((total,)),
+            pltpu.SemaphoreType.DMA((8,)),
+        ],
+    )
+
+
+def attend(
+    where, tokens, query, both, allowed, valid, norm_attn, norm_pre, pieces, out_rows, heads
+):
     count, width = tokens.shape
     seqs, each, span = allowed.shape
     head_dim = query.shape[1] // heads
     inv_root = head_dim ** (-0.5)
     near, total = len(both), len(pieces)
+    tall, wide = pieces[0].shape
 
     def body(where_ref, x_ref, query_ref, allowed_ref, valid_ref, attn_ref, pre_ref, *rest):
         got, parts = rest[:near], rest[near : near + total]
-        probs_out, mixed_out, raw_out, after_out, two_out, weight = rest[near + total :]
-        put_rows(weight, where_ref[0], parts, masks, parts[0].shape[0])
+        probs_out, mixed_out, raw_out, after_out, two_out, weight, sems = rest[near + total :]
+        copies = load_columns(where_ref[0], parts, tall, out_rows, wide - width, weight, sems)
         for s in range(seqs):
             rows = slice(s * each, (s + 1) * each)
             queries = jnp.concatenate(
@@ -626,6 +667,8 @@
                 mixed_out[rows, h * head_dim : (h + 1) * head_dim] = mixed[
                     h * each : (h + 1) * each
                 ]
+        for copy in copies:
+            copy.wait()
         raw = dot(mixed_out[...], weight[...], 1, 0)
         raw_out[...] = raw
         after = x_ref[...].astype(jnp.float32) + valid_ref[...] * rms_norm(raw, attn_ref[...])
@@ -642,9 +685,11 @@
             ((count, width), jnp.bfloat16),
         ],
         [where, tokens, query, allowed, valid, norm_attn, norm_pre, *both, *pieces],
-        {0: "smem"},
-        [pltpu.VMEM((heads * head_dim, width), jnp.bfloat16)],
-        2 * count * heads * head_dim * (width + 2 * span),
+        {0: "smem", **{7 + near + i: "any" for i in range(total)}},
+        [
+            pltpu.VMEM((heads * head_dim, width), jnp.bfloat16),
+            pltpu.SemaphoreType.DMA((total,)),
+        ],
     )
 
 
@@ -657,7 +702,8 @@
     return first, rows - first
 
 
-def wide_pieces(parts, far, chunk):
+def pieces_of(refs, chunk):
+    parts, far = refs[: len(refs) // 2], refs[len(refs) // 2 :]
     first, second = halves_of(chunk)
     shapes = [(0, 0, chunk), (2, 0, chunk), (4, 0, chunk), (6, 0, first), (6, first, second)]
     return [(ref, mask, at, rows) for ref, (mask, at, rows) in zip(parts, shapes)] + [
@@ -665,10 +711,10 @@
     ]
 
 
-def load_weights(index, pieces, chunk, target, sems):
+def load_weights(index, refs, chunk, target, sems):
     def copies(m):
         result = []
-        for i, (ref, mask, at, rows) in enumerate(pieces):
+        for i, (ref, mask, at, rows) in enumerate(pieces_of(refs, chunk)):
             start = pl.multiple_of((index ^ mask) * chunk + at, 16)
             result.append(
                 pltpu.make_async_copy(ref.at[m], target.at[m, pl.ds(start, rows)], sems.at[m, i])
@@ -678,21 +724,44 @@
     return [copies(m) for m in range(target.shape[0])]
 
 
+def load_columns(index, refs, tall, rows, first, target, sems):
+    copies = []
+    for i, (ref, mask, at, size) in enumerate(pieces_of(refs, tall)):
+        size = min(size, rows - at)
+        if size > 0:
+            start = pl.multiple_of((index ^ mask) * rows + at, 16)
+            copies.append(
+                pltpu.make_async_copy(
+                    ref.at[pl.ds(0, size), pl.ds(first, target.shape[1])],
+                    target.at[pl.ds(start, size)],
+                    sems.at[i],
+                )
+            )
+    for copy in copies:
+        copy.start()
+    return copies
+
+
+def tails_of(refs, tall):
+    return [
+        (ref[rows - 16 : rows], mask) for ref, mask, at, rows in pieces_of(refs, tall) if at + rows == tall
+    ]
+
+
 def feed_forward(where, pieces, weights):
     count, width = pieces[0].shape
     kinds, chunk, inner = weights[0].shape
     lanes = -(-inner // 128) * 128
     near, spots = len(pieces), len(weights)
-    total = near * count
+    total, early = near * count, (near - 1) * count
     slope = (2.0 / np.pi) ** 0.5
 
     def body(where_ref, *rest):
         shards, rest = rest[:spots], rest[spots:]
         parts = rest[:near]
-        group_out, act_out, one_out, two_out = rest[near : near + 4]
-        sums = rest[near + 4 : near + 4 + near]
-        weight, sems = rest[near + 4 + near :]
-        shards = wide_pieces(shards[: spots // 2], shards[spots // 2 :], chunk)
+        group_out, act_out, *slopes = rest[near : near + 6]
+        sums = rest[near + 6 : near + 6 + near]
+        weight, sems = rest[near + 6 + near :]
         copies = load_weights(where_ref[0], shards, chunk, weight, sems)
         for kind in copies:
             for copy in kind:
@@ -712,8 +781,9 @@
                 slope * (1.0 + 3.0 * 0.044715 * gate * gate)
             )
             act_out[:, low:high] = (gelu * upper).astype(jnp.bfloat16)
-            one_out[:, low:high] = (steep * upper).astype(jnp.bfloat16)
-            two_out[:, low:high] = gelu.astype(jnp.bfloat16)
+            for value, outs in ((steep * upper, slopes[:2]), (gelu, slopes[2:])):
+                outs[0][:, low:high] = value[:early].astype(jnp.bfloat16)
+                outs[1][:, low:high] = value[early:].astype(jnp.bfloat16)
         if lanes > inner:
             act_out[:, inner:] = jnp.zeros((total, lanes - inner), jnp.bfloat16)
         for copy in copies[2]:
@@ -727,7 +797,7 @@
         body,
         [((total, width), jnp.bfloat16)]
         + [((total, lanes), jnp.bfloat16)]
-        + [((total, inner), jnp.bfloat16)] * 2
+        + [((early, inner), jnp.bfloat16), ((count, inner), jnp.bfloat16)] * 2
         + [((count, width), jnp.float32)]
         + [((count, width), jnp.bfloat16)] * (near - 1),
         [where, *weights, *pieces],
@@ -736,7 +806,6 @@
             pltpu.VMEM((kinds, width, inner), jnp.bfloat16),
             pltpu.SemaphoreType.DMA((kinds, spots)),
         ],
-        6 * total * width * inner,
     )
 
 
@@ -767,7 +836,7 @@
     )
 
 
-def feed_back(where, pieces, weights, one, two):
+def feed_back(where, pieces, weights, one, two, with_own):
     count, width = pieces[0].shape
     kinds, chunk, inner = weights[0].shape
     lanes = -(-inner // 128) * 128
@@ -777,10 +846,9 @@
     def body(where_ref, one_ref, two_ref, *rest):
         shards, rest = rest[:spots], rest[spots:]
         parts = rest[:near]
-        group_out, gate_out, upper_out = rest[near : near + 3]
-        sums = rest[near + 3 : near + 3 + near]
-        weight, sems = rest[near + 3 + near :]
-        shards = wide_pieces(shards[: spots // 2], shards[spots // 2 :], chunk)
+        group_out, both_out = rest[near : near + 2]
+        sums = rest[near + 2 : near + 2 + near]
+        weight, sems = rest[near + 2 + near :]
         copies = load_weights(where_ref[0], shards, chunk, weight, sems)
         for kind in (copies[2], copies[0], copies[1]):
             for copy in kind:
@@ -791,51 +859,47 @@
             copy.wait()
         for low, high in column_steps(inner, 256):
             grad = dot(group_out[...], weight[2, :, low:high], 1, 0)
-            gate_out[:, low:high] = (grad * one_ref[:, low:high].astype(jnp.float32)).astype(
-                jnp.bfloat16
-            )
-            upper_out[:, low:high] = (grad * two_ref[:, low:high].astype(jnp.float32)).astype(
-                jnp.bfloat16
-            )
+            for i, ref in enumerate((one_ref, two_ref)):
+                both_out[i, :, low:high] = (grad * ref[:, low:high].astype(jnp.float32)).astype(
+                    jnp.bfloat16
+                )
         if lanes > inner:
-            gate_out[:, inner:] = jnp.zeros((total, lanes - inner), jnp.bfloat16)
-            upper_out[:, inner:] = jnp.zeros((total, lanes - inner), jnp.bfloat16)
+            both_out[:, :, inner:] = jnp.zeros((2, total, lanes - inner), jnp.bfloat16)
         for kind in copies[:2]:
             for copy in kind:
                 copy.wait()
         for low, high in column_steps(width, 384):
-            part = dot(gate_out[:, :inner], weight[0, low:high, :], 1, 1)
-            part = part + dot(upper_out[:, :inner], weight[1, low:high, :], 1, 1)
+            part = dot(both_out[0, :, :inner], weight[0, low:high, :], 1, 1)
+            part = part + dot(both_out[1, :, :inner], weight[1, low:high, :], 1, 1)
             for k in range(near):
                 sums[k][:, low:high] = part[k * count : (k + 1) * count].astype(sums[k].dtype)
 
     return kernel_call(
         body,
         [((total, width), jnp.bfloat16)]
-        + [((total, lanes), jnp.bfloat16)] * 2
-        + [((count, width), jnp.float32)]
-        + [((count, width), jnp.bfloat16)] * (near - 1),
+        + [((2, total, lanes), jnp.bfloat16)]
+        + [((count, width), jnp.float32 if with_own and k == 0 else jnp.bfloat16) for k in range(near)],
         [where, one, two, *weights, *pieces],
         {0: "smem", **{3 + i: "any" for i in range(spots)}},
         [
             pltpu.VMEM((kinds, width, inner), jnp.bfloat16),
             pltpu.SemaphoreType.DMA((kinds, spots)),
         ],
-        6 * total * width * inner,
-    )
-
-
-def wide_grads(where, two, two_far, back, back_far, act, act_far, gate, gate_far, upper, upper_far):
+    )
+
+
+def wide_grads(where, two, two_far, back, back_far, act, act_far, both, both_far):
     total, width = two.shape
     inner = act.shape[1]
     chunk = width // 8
     first, second = halves_of(chunk)
 
+    cuts = [(0, back[0].shape[0]), (back[0].shape[0], total)]
+
     def body(where_ref, *rest):
-        lefts = [rest[0:2], rest[2:4]]
-        rights = [rest[6:8], rest[8:10], rest[4:6]]
-        outs = rest[10:14]
-        turned, left = rest[14:]
+        twos, backs, acts, boths = rest[0:2], rest[2:6], rest[6:8], rest[8:12]
+        outs = rest[12:16]
+        turned, left = rest[16:]
         core, x, y = where_ref[1], where_ref[2], where_ref[3]
         order = []
         for flip in (1, 0):
@@ -844,7 +908,13 @@
             order.append([(jnp.bitwise_xor(y, flip) * 2 + j, first, second) for j in range(2)])
         for index, kinds in ((0, (0, 1)), (1, (2,))):
             for side in range(2):
-                turned[:, side * total : (side + 1) * total] = lefts[index][side][...].T
+                if index == 0:
+                    turned[:, side * total : (side + 1) * total] = twos[side][...].T
+                else:
+                    for i, (start, end) in enumerate(cuts):
+                        turned[:, side * total + start : side * total + end] = backs[
+                            2 * side + i
+                        ][...].T
             at = 0
             for block in order:
                 for plane, offset, size in block:
@@ -852,10 +922,13 @@
                     left[at : at + size, :] = turned[pl.ds(start, size), :]
                     at += size
             for m in kinds:
-                own, far = rights[m]
                 for low, high in column_steps(inner, 256):
-                    part = dot(left[:, :total], own[:, low:high], 1, 0)
-                    part = part + dot(left[:, total:], far[:, low:high], 1, 0)
+                    if m == 2:
+                        rights = [acts[0][:, low:high], acts[1][:, low:high]]
+                    else:
+                        rights = [b[m, :, low:high] for b in boths]
+                    right = jnp.concatenate(rights, axis=0)
+                    part = dot(left[...], right, 1, 0)
                     part = part.astype(jnp.bfloat16)
                     at = 0
                     for out, block in zip(outs, order):
@@ -871,13 +944,12 @@
             ((3, 2 * second, inner), jnp.bfloat16),
             ((3, 2 * second, inner), jnp.bfloat16),
         ],
-        [where, two, two_far, back, back_far, act, act_far, gate, gate_far, upper, upper_far],
+        [where, two, two_far, *back, *back_far, act, act_far, *both, *both_far],
         {0: "smem"},
         [
             pltpu.VMEM((width, 2 * total), jnp.bfloat16),
             pltpu.VMEM((width // 2, 2 * total), jnp.bfloat16),
         ],
-        6 * total * width * inner,
     )
 
 
@@ -947,9 +1019,9 @@
     raw,
     both,
     pieces,
+    out_rows,
     cosine,
     sine,
-    masks,
     heads,
 ):
     count, width = after.shape
@@ -957,7 +1029,8 @@
     each = count // seqs
     head_dim = norm_query.shape[1]
     inv_root = head_dim ** (-0.5)
-    near, total = len(both), len(pieces)
+    near, spots = len(both), len(pieces)
+    tall, wide = pieces[0].shape
 
     def body(
         where_ref,
@@ -975,14 +1048,14 @@
         sin_ref,
         *rest,
     ):
+        shards, rest = rest[:spots], rest[spots:]
         sums = rest[:near]
         got = rest[near : 2 * near]
-        shards = rest[2 * near : 2 * near + total]
-        rest = rest[2 * near + total :]
+        rest = rest[2 * near :]
         dx_out, attn_grad_out, raw_grad_out, pre_out, attn_gain_out, query_gain_out = rest[:6]
         both_outs = rest[6 : 6 + near]
-        weight, mixed_grad, query_grad = rest[6 + near :]
-        put_rows(weight, where_ref[0], shards, masks, shards[0].shape[0])
+        mixed_grad, query_grad, weight, sems = rest[6 + near :]
+        copies = load_columns(where_ref[0], shards, tall, out_rows, wide - width, weight, sems)
         grad = sums[0][...]
         for s in sums[1:]:
             grad = grad + s[...].astype(jnp.float32)
@@ -994,6 +1067,8 @@
         attn_gain_out[...] = gain
         attn_grad = attn_grad.astype(jnp.bfloat16)
         attn_grad_out[...] = attn_grad
+        for copy in copies:
+            copy.wait()
         mixed_grad[...] = dot(attn_grad, weight[...], 1, 1).astype(jnp.bfloat16)
         for s in range(seqs):
             rows = slice(s * each, (s + 1) * each)
@@ -1056,17 +1131,17 @@
             raw,
             cosine,
             sine,
+            *pieces,
             *parts,
             *both,
-            *pieces,
         ],
-        {0: "smem"},
-        [
-            pltpu.VMEM((heads * head_dim, width), jnp.bfloat16),
+        {0: "smem", **{13 + i: "any" for i in range(spots)}},
+        [
             pltpu.VMEM((count, heads * head_dim), jnp.bfloat16),
             pltpu.VMEM((count, heads * head_dim), jnp.float32),
+            pltpu.VMEM((heads * head_dim, width), jnp.bfloat16),
+            pltpu.SemaphoreType.DMA((spots,)),
         ],
-        2 * count * heads * head_dim * (width + 5 * span),
     )
 
 
@@ -1082,26 +1157,31 @@
     cosine,
     sine,
     pieces,
-    masks,
     heads,
     ctx,
     gains,
 ):
     count, width = tokens.shape
-    wide = pieces[0].shape[1]
+    tall_piece = pieces[0].shape[0]
     head_dim = norm_key.shape[1]
-    near, total = len(parts), len(pieces)
-    step = heads * head_dim // ctx
+    wide = (heads + 2) * head_dim
+    near, spots, total = len(parts), len(pieces), 8
+    each = wide // ctx
     count_gains = len(gains)
+    tall = count + 16
 
     def body(
         where_ref, raw_ref, query_ref, x_ref, dx_ref, in_ref, key_ref, cos_ref, sin_ref, *rest
     ):
         sums = rest[:near]
-        shards = rest[near : near + total]
-        others = rest[near + total : near + total + count_gains]
-        input_out, grads_out, gains_out, weight = rest[near + total + count_gains :]
-        put_rows(weight, where_ref[0], shards, masks, width // total)
+        shards = rest[near : near + spots]
+        others = rest[near + spots : near + spots + count_gains]
+        input_out = rest[near + spots + count_gains]
+        outs = rest[near + spots + count_gains + 1 : near + spots + count_gains + 1 + ctx]
+        weight, grads_out, gains_out, sems = rest[near + spots + count_gains + 1 + ctx :]
+        copies = load_columns(
+            where_ref[0], shards, tall_piece, tall_piece - 16, 0, weight, sems
+        )
         grad = sums[0][...]
         for s in sums[1:]:
             grad = grad + s[...].astype(jnp.float32)
@@ -1110,28 +1190,43 @@
         grads_out[:, : heads * head_dim] = query_ref[...]
         grads_out[:, heads * head_dim : (heads + 1) * head_dim] = key_grad.astype(jnp.bfloat16)
         grads_out[:, (heads + 1) * head_dim :] = grad[:, head_dim:].astype(jnp.bfloat16)
+        for copy in copies:
+            copy.wait()
         back = dot(grads_out[...], weight[...], 1, 1)
         through, in_gain = norm_back(x_ref[...].astype(jnp.float32), in_ref[...], back)
         input_out[...] = (dx_ref[...] + through).astype(jnp.bfloat16)
-        gains_out[...] = jnp.zeros((total, wide), jnp.float32)
+        gains_out[...] = jnp.zeros((16, wide), jnp.float32)
         lane = 0
         for gain in (in_gain, others[0][...], key_gain, *[o[...] for o in others[1:]]):
             size = gain.shape[1] // (total * ctx)
             for d in range(total):
                 for c in range(ctx):
-                    at = c * step + lane
+                    at = c * each + lane
                     gains_out[d : d + 1, at : at + size] = gain[
                         :, (d * ctx + c) * size : (d * ctx + c + 1) * size
                     ]
             lane += size
+        spans = [(0, heads * head_dim), (heads * head_dim, head_dim), ((heads + 1) * head_dim, head_dim)]
+        mine = where_ref[4]
+        for c in range(ctx):
+
+            @pl.when(mine == c)
+            def _(c=c):
+                for k in range(ctx):
+                    j, at = (c + k) % ctx, 0
+                    for first, size in spans:
+                        step = size // ctx
+                        outs[k][:count, at : at + step] = grads_out[
+                            :, first + j * step : first + (j + 1) * step
+                        ]
+                        at += step
+                    outs[k][count:, :] = gains_out[:, j * each : (j + 1) * each].astype(
+                        jnp.bfloat16
+                    )
 
     return kernel_call(
         body,
-        [
-            ((count, width), jnp.bfloat16),
-            ((count, wide), jnp.bfloat16),
-            ((total, wide), jnp.float32),
-        ],
+        [((count, width), jnp.bfloat16)] + [((tall, each), jnp.bfloat16)] * ctx,
         [
             where,
             raw,
@@ -1146,51 +1241,57 @@
             *pieces,
             *gains,
         ],
-        {0: "smem"},
-        [pltpu.VMEM((width, wide), jnp.bfloat16)],
-        2 * count * width * wide,
-    )
-
-
-def narrow_grads(where, left, left_far, right, right_far, gains=()):
-    count, width = left.shape
-    wide = right.shape[1]
-    chunk = width // 8
-    tall = chunk + 16 if gains else chunk
-
-    def body(where_ref, left_ref, far_ref, right_ref, right_far_ref, *rest):
-        rows, rest = rest[: len(gains)], rest[len(gains) :]
-        outs, (turned, lefts) = rest[:4], rest[4:]
-        turned[:, :count] = left_ref[...].T
-        turned[:, count:] = far_ref[...].T
+        {0: "smem", **{9 + near + i: "any" for i in range(spots)}},
+        [
+            pltpu.VMEM((width, wide), jnp.bfloat16),
+            pltpu.VMEM((count, wide), jnp.bfloat16),
+            pltpu.VMEM((16, wide), jnp.float32),
+            pltpu.SemaphoreType.DMA((spots,)),
+        ],
+    )
+
+
+def narrow_grads(where, lefts, rights, with_gains):
+    count, width = lefts[0].shape
+    wide = rights[0].shape[1]
+    chunk, near = width // 8, len(lefts)
+    total = near * count
+    tall = chunk + 16 if with_gains else chunk
+
+    def body(where_ref, *rest):
+        left_refs, right_refs, outs = rest[:near], rest[near : 2 * near], rest[2 * near : -3]
+        turned, lines, values = rest[-3:]
+        for i in range(near):
+            turned[:, i * count : (i + 1) * count] = left_refs[i][...].T
+            values[i * count : (i + 1) * count, :] = right_refs[i][:count, :]
         plane, core = where_ref[0] // 2, where_ref[1]
         for m in range(4):
             start = pl.multiple_of((jnp.bitwise_xor(plane, m) * 2 + core) * chunk, 16)
-            lefts[m * chunk : (m + 1) * chunk, :] = turned[pl.ds(start, chunk), :]
+            lines[m * chunk : (m + 1) * chunk, :] = turned[pl.ds(start, chunk), :]
         for low, high in column_steps(wide, 256):
-            part = dot(lefts[:, :count], right_ref[:, low:high], 1, 0)
-            part = part + dot(lefts[:, count:], right_far_ref[:, low:high], 1, 0)
+            part = dot(lines[...], values[:, low:high], 1, 0)
             for m in range(4):
                 outs[m][:chunk, low:high] = part[m * chunk : (m + 1) * chunk].astype(outs[m].dtype)
-        if gains:
-            whole = rows[0][...] + rows[1][...]
+        if with_gains:
+            whole = right_refs[0][count:, :].astype(jnp.float32)
+            for r in right_refs[1:]:
+                whole = whole + r[count:, :].astype(jnp.float32)
             index = lax.broadcasted_iota(jnp.int32, whole.shape, 0)
             for m in range(4):
                 row = jnp.bitwise_xor(plane, m) * 2 + core
                 row = jnp.sum(jnp.where(index == row, whole, 0.0), axis=0, keepdims=True)
-                lines = lax.broadcasted_iota(jnp.int32, (16, wide), 0)
-                outs[m][chunk:, :] = jnp.where(lines == 0, row, 0.0).astype(outs[m].dtype)
+                outs[m][chunk:, :] = jnp.where(index == 0, row, 0.0).astype(outs[m].dtype)
 
     return kernel_call(
         body,
         [((tall, wide), jnp.float32)] + [((tall, wide), jnp.bfloat16)] * 3,
-        [where, left, left_far, right, right_far, *gains],
+        [where, *lefts, *rights],
         {0: "smem"},
         [
-            pltpu.VMEM((width, 2 * count), jnp.bfloat16),
-            pltpu.VMEM((width // 2, 2 * count), jnp.bfloat16),
+            pltpu.VMEM((width, total), jnp.bfloat16),
+            pltpu.VMEM((width // 2, total), jnp.bfloat16),
+            pltpu.VMEM((total, wide), jnp.bfloat16),
         ],
-        2 * count * width * wide,
     )
 
 
@@ -1228,11 +1329,14 @@
     )
 
 
-def split_columns(where, gate, up, ctx):
+def split_wide(where, gate, up, down, ctx):
     rows, whole = gate.shape
     inner = whole // ctx
-
-    def body(where_ref, gate_ref, up_ref, *outs):
+    groups, chunk, part = down.shape
+    per, steps = groups // ctx, chunk // rows
+
+    def body(where_ref, gate_ref, up_ref, down_ref, *rest):
+        outs, wide = rest[:ctx], rest[ctx]
         mine = where_ref[4]
         for c in range(ctx):
 
@@ -1242,19 +1346,29 @@
                     j = (c + k) % ctx
                     outs[k][0] = gate_ref[:, j * inner : (j + 1) * inner]
                     outs[k][1] = up_ref[:, j * inner : (j + 1) * inner]
+                    for b in range(groups):
+                        first = b % steps * rows
+                        wide[:, b * part : (b + 1) * part] = down_ref[
+                            j * per + b // steps, first : first + rows, :
+                        ].astype(jnp.float32)
+                    outs[k][2] = wide[...].astype(jnp.bfloat16)
 
     return kernel_call(
-        body, [((2, rows, inner), jnp.bfloat16)] * ctx, [where, gate, up], {0: "smem"}
-    )
-
-
-def join_wide(where, pairs, downs):
-    ctx = len(pairs)
-    _, rows, inner = pairs[0].shape
-    per, chunk, part = downs[0].shape
+        body,
+        [((3, rows, inner), jnp.bfloat16)] * ctx,
+        [where, gate, up, down],
+        {0: "smem"},
+        [pltpu.VMEM((rows, inner), jnp.float32)],
+    )
+
+
+def join_wide(where, pieces, part):
+    ctx = len(pieces)
+    _, rows, inner = pieces[0].shape
+    chunk, groups = ctx * rows, inner // part
 
     def body(where_ref, *rest):
-        two, down, out, rows_scr = rest[:ctx], rest[ctx : 2 * ctx], rest[2 * ctx], rest[2 * ctx + 1]
+        got, out, wide = rest[:ctx], rest[ctx], rest[ctx + 1]
         mine = where_ref[4]
         for c in range(ctx):
 
@@ -1262,65 +1376,62 @@
             def _(c=c):
                 for m in range(2):
                     for a in range(ctx):
-                        rows_scr[a * rows : (a + 1) * rows, :] = two[(c - a) % ctx][m].astype(
+                        wide[a * rows : (a + 1) * rows, :] = got[(c - a) % ctx][m].astype(
                             jnp.float32
                         )
-                    out[m] = rows_scr[...].astype(jnp.bfloat16)
+                    out[m] = wide[...].astype(jnp.bfloat16)
                 for a in range(ctx):
-                    for p in range(per):
-                        at = (p * ctx + a) * part
-                        rows_scr[:, at : at + part] = down[(c - a) % ctx][p].astype(jnp.float32)
-                out[2] = rows_scr[...].astype(jnp.bfloat16)
+                    piece = got[(c - a) % ctx][2].astype(jnp.float32)
+                    for b in range(groups):
+                        first = b % ctx * rows
+                        at = (b // ctx * ctx + a) * part
+                        wide[first : first + rows, at : at + part] = piece[
+                            :, b * part : (b + 1) * part
+                        ]
+                out[2] = wide[...].astype(jnp.bfloat16)
 
     return kernel_call(
         body,
         [((3, chunk, inner), jnp.bfloat16)],
-        [where, *pairs, *downs],
+        [where, *pieces],
         {0: "smem"},
         [pltpu.VMEM((chunk, inner), jnp.float32)],
     )[0]
 
 
-def join_rows(where, pieces, rows):
+def join_rows(where, pieces, rows, split, out_rows):
     ctx = len(pieces)
-    tall, wide = pieces[0].shape
-    more = 16 if tall > rows else 0
+    _, wide = pieces[0].shape
+    tall = ctx * rows + 16
 
     def body(where_ref, *rest):
-        got, out, rows_scr = rest[:ctx], rest[ctx], rest[ctx + 1]
+        got, out, lines = rest[:ctx], rest[ctx], rest[ctx + 1]
         mine = where_ref[4]
-        if more:
-            rows_scr[ctx * rows :, :] = jnp.zeros((more, wide), jnp.float32)
+        lines[ctx * rows :, :] = jnp.zeros((16, wide), jnp.float32)
+        lines[ctx * out_rows :, split:] = jnp.zeros((tall - ctx * out_rows, wide - split), jnp.float32)
         for c in range(ctx):
 
             @pl.when(mine == c)
             def _(c=c):
                 for a in range(ctx):
                     piece = got[(c - a) % ctx]
-                    rows_scr[a * rows : (a + 1) * rows, :] = piece[:rows, :].astype(jnp.float32)
-                    if more:
-                        at = ctx * rows + a
-                        rows_scr[at : at + 1, :] = piece[rows : rows + 1, :].astype(jnp.float32)
-                out[...] = rows_scr[...].astype(jnp.bfloat16)
+                    lines[a * rows : (a + 1) * rows, :split] = piece[:rows, :split].astype(
+                        jnp.float32
+                    )
+                    lines[a * out_rows : (a + 1) * out_rows, split:] = piece[
+                        :out_rows, split:
+                    ].astype(jnp.float32)
+                    at = ctx * rows + a
+                    lines[at : at + 1, :split] = piece[rows : rows + 1, :split].astype(jnp.float32)
+                out[...] = lines[...].astype(jnp.bfloat16)
 
     return kernel_call(
         body,
-        [((ctx * rows + more, wide), jnp.bfloat16)],
+        [((tall, wide), jnp.bfloat16)],
         [where, *pieces],
         {0: "smem"},
-        [pltpu.VMEM((ctx * rows + more, wide), jnp.float32)],
+        [pltpu.VMEM((tall, wide), jnp.float32)],
     )[0]
-
-
-def plane_gather(value):
-    size = lax.axis_size("dp")
-
-    def across(item, mask):
-        return lax.ppermute(item, "dp", [(i, i ^ mask) for i in range(size)])
-
-    near = [value] + [across(value, m) for m in range(2, size, 2)]
-    far = [across(item, 1) for item in near]
-    return near + far, list(range(0, size, 2)) + list(range(1, size, 2))
 
 
 def plane_send(parts):
@@ -1333,6 +1444,14 @@
 
 def ctx_send(parts, sign):
     return [parts[0]] + [shift(parts[k], sign * k) for k in range(1, len(parts))]
+
+
+def stage(*values):
+    return lax.optimization_barrier(values)
+
+
+def gate(value, *conditions):
+    return lax.optimization_barrier((value, conditions))[0]
 
 
 def fused(
@@ -1366,69 +1485,100 @@
 
     gains = [gain_in, gain_query, gain_key, gain_attn, gain_pre, gain_post]
     sizes = [g.shape[0] for g in gains]
-    packed = pack(w_query, w_key, w_value, gains)
-    w_gate, w_up, w_down, packed = lax.optimization_barrier((w_gate, w_up, w_down, packed))
-    qkv_chunk = join_rows(where, ctx_gather(packed), w_query.shape[0])
-    out_chunk = join_rows(where, ctx_gather(w_out), w_out.shape[0])
-    qkv_pieces, masks = plane_gather(qkv_chunk)
-    out_pieces, _ = plane_gather(out_chunk)
-    per = dp // ctx
-    down = w_down.T.reshape(dp, width // dp, w_down.shape[0])
-    down = lax.all_to_all(down, "dp", split_axis=0, concat_axis=0, tiled=True)
-    down = ctx_exchange(down.reshape(ctx, per, width // dp, w_down.shape[0]))
-    pairs = ctx_send(split_columns(where, w_gate, w_up, ctx), 1)
-    shard = join_wide(where, pairs, down)
-    cosine, sine, valid, allowed = tables(where, lengths, count, stretch, ctx, head_dim)
-    shard_x, shard_y = swap(shard, 1), swap(shard, 2)
-
+    chunk, out_rows = width // dp, heads * head_dim // dp
+    packed = pack(w_query, w_key, w_value, w_out, gains)
+    split = packed.shape[1] - width
+    downs = gate(w_down, packed).T.reshape(dp, chunk, w_down.shape[0])
+    downs = lax.all_to_all(downs, "dp", split_axis=0, concat_axis=0, tiled=True)
+    packed = ctx_gather(packed)
+    aux = tables(where, lengths, count, stretch, ctx, head_dim)
+    packed, downs, aux = stage(packed, downs, aux)
+    cosine, sine, valid, allowed = aux
+
+    blocks = list(split_wide(where, w_gate, w_up, downs.reshape(dp, chunk, -1), ctx))
+    packed = gate(packed, blocks[0])
+    blocks = ctx_send(blocks, 1)
+    near = plane_near(join_rows(where, packed, w_query.shape[0], split, w_out.shape[0]))
+    shared = plane_whole(near)
+    shared, blocks = stage(shared, blocks)
+
+    shard = join_wide(where, blocks, w_down.shape[0])
     normed, query, both, raw, norm_in, norm_query, norm_key = project(
-        where, tokens, qkv_pieces, sizes[:3], cosine, sine, masks, heads, ctx
-    )
+        where, tokens, shared, sizes[:3], cosine, sine, heads, ctx
+    )
+    shard, normed, query, both = stage(shard, normed, query, both)
+
+    shard = plane_near(shard)
     norm_attn, norm_pre, norm_post = late_gains(
-        where, qkv_pieces, masks, width // dp, [384, 512, 640], sizes[3:], ctx, both
+        where, shared, [384, 512, 640], sizes[3:], ctx, both
     )
     both = ctx_gather(both)
-    probs, mixed, attn_raw, after, normed_two = attend(
-        where, tokens, query, both, allowed, valid, norm_attn, norm_pre, out_pieces, masks, heads
-    )
-    shard_x, shard_y, normed_two = lax.optimization_barrier((shard_x, shard_y, normed_two))
-    first = halves_of(width // dp)[0]
-    weights = [shard, shard_x, shard_y, swap(shard_x[:, :first], 2), swap(shard_y[:, first:], 1)]
-    weights = weights + [swap(w, 0) for w in weights]
-    group_two, act, one, two, *sums = feed_forward(where, ctx_gather(normed_two), weights)
-    output, ffn_grad, gain_post_grad = finish(
-        ctx_send(sums, -1), after, cotangent, valid, norm_post
-    )
-    group_two_far = swap(group_two, 0)
-    act_far = swap(act, 0)
-    group_ffn, gate_grad, upper_grad, *sums = feed_back(
-        where, ctx_gather(ffn_grad), weights, one, two
-    )
-    sums = ctx_send(sums, -1)
-    group_ffn_far, gate_far, upper_far = (
-        swap(group_ffn, 0),
-        swap(gate_grad, 0),
-        swap(upper_grad, 0),
-    )
+    probs, mixed, attn_raw, residual, normed_two = attend(
+        where,
+        tokens,
+        query,
+        both,
+        allowed,
+        valid,
+        norm_attn,
+        norm_pre,
+        shared,
+        out_rows,
+        heads,
+    )
+    far = [swap(gate(shard[0], both[2]), 0)]
+    shard, far, halves, normed_two, mixed = stage(shard, far, cut(shard), normed_two, mixed)
+
+    halves = diagonal(halves)
+    two_pieces = ctx_gather(normed_two)
+    two_pieces, halves, shard, normed = stage(two_pieces, halves, shard, normed)
+
+    weights = shard + halves
+    weights = weights + far + [swap(w, 0) for w in weights[1:]]
+    two_pieces, weights, normed = stage(two_pieces, weights, normed)
+
+    order = [0, 1, 3, 2]
+    normed_group = [normed, shift(normed, 1), None, shift(normed, 3)]
+    group_two, act, one, one_last, two, two_last, *sums = feed_forward(
+        where, [two_pieces[k] for k in order], weights
+    )
+    group_two, act, one, one_last, two, two_last, sums, near_group = stage(
+        group_two, act, one, one_last, two, two_last, sums, [normed_group[1], normed_group[3]]
+    )
+    normed_group[1], normed_group[3] = near_group
+
+    sums = [sums[0]] + [shift(sums[i], -order[i]) for i in range(1, ctx)]
+    group_two_far, act_far, mixed_far = swap(group_two, 0), swap(act, 0), swap(mixed, 0)
+    sums, group_two_far, act_far, mixed_far = stage(sums, group_two_far, act_far, mixed_far)
+
+    output, ffn_grad, gain_post_grad = finish(sums, residual, cotangent, valid, norm_post)
+    ffn_pieces = ctx_gather(ffn_grad)
+    ffn_early = [ffn_pieces[k] for k in order[:-1]]
+    group_ffn, grads, *sums = feed_back(where, ffn_early, weights, one, two, True)
+    ffn_last, group_ffn, grads, sums = stage(ffn_pieces[order[-1]], group_ffn, grads, sums)
+
+    ffn_last, grads_last, sum_last = feed_back(
+        where, [ffn_last], weights, one_last, two_last, False
+    )
+    sums[1] = shift(sums[1], -order[1])
+    ffn_last, grads_last, sum_last, group_ffn, grads, sums = stage(
+        ffn_last, grads_last, sum_last, group_ffn, grads, sums
+    )
+
+    sums[2] = shift(sums[2], -order[2])
+    sums.append(shift(sum_last, -order[-1]))
+    group_ffn, grads = [group_ffn, ffn_last], [grads, grads_last]
+    group_ffn_far, grads_far = [swap(g, 0) for g in group_ffn], [swap(g, 0) for g in grads]
     send_a, kept_a, send_b, kept_b = wide_grads(
-        where,
-        group_two,
-        group_two_far,
-        group_ffn,
-        group_ffn_far,
-        act,
-        act_far,
-        gate_grad,
-        gate_far,
-        upper_grad,
-        upper_far,
-    )
-    sums, send_a, send_b = lax.optimization_barrier((sums, send_a, send_b))
+        where, group_two, group_two_far, group_ffn, group_ffn_far, act, act_far, grads, grads_far
+    )
+    sums, send_a, kept_a, send_b, kept_b = stage(sums, send_a, kept_a, send_b, kept_b)
+
     got_a, got_b = swap(send_a, 1), swap(send_b, 2)
     dx, attn_grad, query_grad, gain_pre_grad, gain_attn_grad, gain_query_grad, *parts = attend_back(
         where,
         sums,
-        after,
+        residual,
         cotangent,
         valid,
         attn_raw,
@@ -1439,23 +1589,19 @@
         query,
         raw,
         both,
-        out_pieces,
+        shared,
+        out_rows,
         cosine,
         sine,
-        masks,
         heads,
     )
     parts = ctx_send(parts, -1)
-    send_a, kept_a, send_b, kept_b = wide_middle(where, kept_a, got_a, kept_b, got_b)
-    out_blocks = plane_send(
-        narrow_grads(where, attn_grad, swap(attn_grad, 0), mixed, swap(mixed, 0))
-    )
-    out_blocks = ctx_send(narrow_middle(where, out_blocks, [mixed.shape[1]], ctx), 1)
-    parts, send_a, send_b, out_blocks = lax.optimization_barrier(
-        (parts, send_a, send_b, out_blocks)
-    )
-    got_a, got_b = swap(send_a, 2), swap(send_b, 1)
-    input_grad, qkv_grads, gain_rows = project_back(
+    normed_group[2] = shift(gate(normed, parts), 2)
+    out_blocks = narrow_grads(
+        where, [attn_grad, swap(attn_grad, 0)], [mixed, mixed_far], False
+    )
+    parts = gate(parts, out_blocks)
+    input_grad, *blocks = project_back(
         where,
         parts,
         raw,
@@ -1466,28 +1612,31 @@
         norm_key,
         cosine,
         sine,
-        qkv_pieces,
-        masks,
+        shared,
         heads,
         ctx,
         [gain_query_grad, gain_attn_grad, gain_pre_grad, gain_post_grad],
     )
-    blocks = plane_send(
-        narrow_grads(
-            where,
-            normed,
-            swap(normed, 0),
-            qkv_grads,
-            swap(qkv_grads, 0),
-            [gain_rows, swap(gain_rows, 0)],
-        )
-    )
-    blocks = ctx_send(
-        narrow_middle(where, blocks, [heads * head_dim, head_dim, head_dim], ctx), 1
-    )
+    out_blocks = plane_send(out_blocks)
+    got_a, got_b, blocks, out_blocks, normed_group = stage(
+        got_a, got_b, list(blocks), out_blocks, normed_group
+    )
+
+    blocks = ctx_send(blocks, 1)
+    send_a, kept_a, send_b, kept_b = wide_middle(where, kept_a, got_a, kept_b, got_b)
+    got_a, got_b = swap(send_a, 2), swap(send_b, 1)
+    out_blocks = narrow_middle(where, out_blocks, [mixed.shape[1]], ctx)
+    normed_far = [swap(n, 0) for n in normed_group]
+    blocks = narrow_grads(
+        where, normed_group + normed_far, blocks + [swap(b, 0) for b in blocks], True
+    )
+    got_a, got_b, out_blocks, blocks = stage(got_a, got_b, out_blocks, blocks)
+
+    blocks, out_blocks = plane_send(blocks), ctx_send(out_blocks, 1)
     grad_gate, grad_up, grad_down = wide_last(
         kept_a, got_a, kept_b, got_b, w_gate.shape[1] // ctx
     )
+    blocks, out_blocks, grad_gate = stage(blocks, out_blocks, grad_gate)
 
     def total(pieces):
         result = pieces[0].astype(jnp.float32)

time: 445 us -> 404 us (0.908)
  waiting for transfers between devices: 210 us -> 153 us
  starting transfers between devices: 95.4 us -> 112 us
  Pallas kernels: 105 us -> 112 us
  local copies, waits for them, and re-layouts: 23.2 us -> 18.1 us
    ppermute x6, waiting for transfers between devices: 58.6 us -> 5.41 us  [plane_send(): lax.ppermute(parts[m], 'dp', [(i, i ^ 2 * m) for i in range(size)])]
    ppermute x36 -> x33, starting transfers between devices: 61.4 us -> 83.4 us  [shift(): lax.ppermute(value, 'ctx', [(i, (i + step) % size) for i in range(size)])]
    ppermute x14 -> x0, waiting for transfers between devices: 13 us -> none  [across(): return lax.ppermute(item, 'dp', [(i, i ^ mask) for i in range(size)])]
    ppermute x23 -> x38, waiting for transfers between devices: 27.9 us -> 40.1 us  [swap(): return lax.ppermute(value, 'dp', [(i, i ^ 1 << bit) for i in range(size)])]
    ppermute x14 -> x0, starting transfers between devices: 9.25 us -> none  [across(): return lax.ppermute(item, 'dp', [(i, i ^ mask) for i in range(size)])]
    pallas_call x21 -> x20, Pallas kernels: 105 us -> 112 us  [kernel_call(): pl.pallas_call(body, out_shape=[jax.ShapeDtypeStruct(s, t) for s, t in ou...]
    ppermute x23 -> x38, starting transfers between devices: 12.6 us -> 17.7 us  [swap(): return lax.ppermute(value, 'dp', [(i, i ^ 1 << bit) for i in range(size)])]
    unnamed x162 -> x138, local copies, waits for them, and re-layouts: 15.5 us -> 12 us
  transfers between devices with their start and end apart: 80 -> 78, of which waited for: 34 -> 34; matrix products, arithmetic and copies ran while one was open for 1% -> 1% of each run, Pallas kernels for 18% -> 22%
where the time goes in v1:
time: 404 us; the launch traced here: 397 us
  waiting for transfers between devices  153 us (38%)
  Pallas kernels  112 us (28%)
  starting transfers between devices  112 us (28%)
  local copies, waits for them, and re-layouts  18.1 us (4%)
    pallas_call x20, Pallas kernels, kernel_call(): pl.pallas_call(body, out_shape=[jax.ShapeDtypeStruct(s, t) for s, t in ou...  112 us
    ppermute x33, waiting for transfers between devices, shift(): lax.ppermute(value, 'ctx', [(i, (i + step) % size) for i in range(size)])  107 us
    ppermute x33, starting transfers between devices, shift(): lax.ppermute(value, 'ctx', [(i, (i + step) % size) for i in range(size)])  83.4 us
    ppermute x38, waiting for transfers between devices, swap(): return lax.ppermute(value, 'dp', [(i, i ^ 1 << bit) for i in range(size)])  40.1 us
    ppermute x38, starting transfers between devices, swap(): return lax.ppermute(value, 'dp', [(i, i ^ 1 << bit) for i in range(size)])  17.7 us
    unnamed x138, local copies, waits for them, and re-layouts  12 us
  transfers between devices with their start and end apart: 78, of which 34 were waited for; matrix products, arithmetic and copies ran while one was open for 1% of the time, Pallas kernels for 22%

profile of v1, /device:TPU:0, one launch (start us, length us, event | category | flops | bytes accessed | tf_op | source)
XLA Modules:
  0.0 397.3 jit_solution(101767234602775915)
XLA Ops:
  4.5 5.2 %all-to-all-start = ((bf16[8,144,216]{2,1,0:T(8,128)(2,1)}), bf16[8,144,216]{2,1,0:T(8,128)(2,1)S(1)}, u32[]{:S(2)}, u32[]{:S(2)}) async-start(bf16[8,144,216]{2,1,0:T(8,128)(2,1)} %bitcast.12), calls=%async_computation | async-start | bytes 1179648 | tf_op jit(solution)/shard_map/all_to_all | solution.py:1492
  19.7 8.8 %collective-permute-done.1.rest_2_ = bf16[40,2688]{1,0:T(8,128)(2,1)S(1)} collective-permute-done((bf16[40,2688]{1,0:T(8,128)(2,1)S(1)}, bf16[40,2688]{1,0:T(8,128)(2,1)S(1)}, u32[]{:S(2)}, u32[]{:S(2)}) %collective-permute-start.1) | collective-permute-done | bytes 215072 | tf_op jit(solution)/shard_map/ppermute | solution.py:65
  45.5 10.6 %collective-permute-done.3.rest_1_.rest_5_ = bf16[160,2688]{1,0:T(8,128)(2,1)S(1)} collective-permute-done((bf16[160,2688]{1,0:T(8,128)(2,1)}, bf16[160,2688]{1,0:T(8,128)(2,1)S(1)}, u32[]{:S(2)}, u32[]{:S(2)}) %collective-permute-start.3) | collective-permute-done | bytes 860192 | tf_op jit(solution)/shard_map/ppermute | solution.py:60
  59.6 12.2 %collective-permute-done.13.rest_2_ = bf16[3,36,1728]{2,1,0:T(8,128)(2,1)S(1)} collective-permute-done((bf16[3,36,1728]{2,1,0:T(8,128)(2,1)}, bf16[3,36,1728]{2,1,0:T(8,128)(2,1)S(1)}, u32[]{:S(2)}, u32[]{:S(2)}) %collective-permute-start.13) | collective-permute-done | bytes 373280 | tf_op jit(solution)/shard_map/ppermute | solution.py:65
  81.5 5.1 %shard_map.285 = (bf16[128,1152]{1,0:T(8,128)(2,1)}, bf16[128,1024]{1,0:T(8,128)(2,1)}, bf16[128,512]{1,0:T(8,128)(2,1)}, f32[128,1280]{1,0:T(8,128)}, f32[1,115...) custom-call(s32[5]{0:T(128)} %stack.23.where_ref, bf16[128,1152]{1,0:T(8,128)(2,1)} %x_ref.5, ...), custom_call_target="tpu_custom_call" | custom-call | tf_op jit(solution)/shard_map/pallas_call | solution.py:426
  86.7 7.5 %collective-permute-start.16 = (bf16[128,512]{1,0:T(8,128)(2,1)}, bf16[128,512]{1,0:T(8,128)(2,1)S(1)}, u32[]{:S(2)}, u32[]{:S(2)}) collective-permute-start(bf16[128,512]{1,0:T(8,128)(2,1)} %get-tuple-element.282.behind_ref.rest_0_.rest_14_), channel_id=1, source_target_pairs={{0,2},{1,3},{2,0},{3,1},{4,6},{5,7},{6,4},{7,5},{8,10},{9,11},{10,... | collective-permute-start | bytes 393224 | tf_op jit(solution)/shard_map/ppermute | solution.py:65
  116.4 13.4 %collective-permute-done.18.rest_1_ = bf16[3,144,1728]{2,1,0:T(8,128)(2,1)S(1)} collective-permute-done((bf16[3,144,1728]{2,1,0:T(8,128)(2,1)S(1)}, bf16[3,144,1728]{2,1,0:T(8,128)(2,1)S(1)}, u32[]{:S(2)}, u32[]{:S(2)}) %collective-permute-start.18) | collective-permute-done | bytes 1493024 | tf_op jit(solution)/shard_map/ppermute | solution.py:60
  140.0 5.5 %collective-permute-done.21.rest_11_ = bf16[128,1152]{1,0:T(8,128)(2,1)S(1)} collective-permute-done((bf16[128,1152]{1,0:T(8,128)(2,1)S(1)}, bf16[128,1152]{1,0:T(8,128)(2,1)S(1)}, u32[]{:S(2)}, u32[]{:S(2)}) %collective-permute-start.21) | collective-permute-done | bytes 294944 | tf_op jit(solution)/shard_map/ppermute | solution.py:65
  145.5 10.3 %collective-permute-done.22.rest_13_ = bf16[128,1152]{1,0:T(8,128)(2,1)S(1)} collective-permute-done((bf16[128,1152]{1,0:T(8,128)(2,1)S(1)}, bf16[128,1152]{1,0:T(8,128)(2,1)S(1)}, u32[]{:S(2)}, u32[]{:S(2)}) %collective-permute-start.22) | collective-permute-done | bytes 294944 | tf_op jit(solution)/shard_map/ppermute | solution.py:65
  157.0 6.8 %collective-permute-done.29.rest_9_ = bf16[3,64,1728]{2,1,0:T(8,128)(2,1)S(1)} collective-permute-done((bf16[3,64,1728]{2,1,0:T(8,128)(2,1)S(1)}, bf16[3,64,1728]{2,1,0:T(8,128)(2,1)S(1)}, u32[]{:S(2)}, u32[]{:S(2)}) %collective-permute-start.29) | collective-permute-done | bytes 663584 | tf_op jit(solution)/shard_map/ppermute | solution.py:60
  164.7 6.8 %collective-permute-start.30 = (bf16[128,1152]{1,0:T(8,128)(2,1)S(1)}, bf16[128,1152]{1,0:T(8,128)(2,1)S(1)}, u32[]{:S(2)}, u32[]{:S(2)}) collective-permute-start(bf16[128,1152]{1,0:T(8,128)(2,1)S(1)} %copy-done.30), channel_id=1, source_target_pairs={{0,1},{1,2},{2,3},{3,0},{4,5},{5,6},{6,7},{7,4},{8,9},{9,10},{10,1... | collective-permute-start | bytes 884744 | tf_op jit(solution)/shard_map/ppermute | solution.py:65
  173.6 15.3 %shard_map.288 = (bf16[512,1152]{1,0:T(8,128)(2,1)}, bf16[512,1792]{1,0:T(8,128)(2,1)}, bf16[384,1728]{1,0:T(8,128)(2,1)}, bf16[128,1728]{1,0:T(8,128)(2,1)}, bf...) custom-call(s32[5]{0:T(128)} %stack.23.where_ref, ...), custom_call_target="tpu_custom_call" | custom-call | tf_op jit(solution)/shard_map/pallas_call | solution.py:426
  194.2 11.8 %collective-permute-done.32.rest_1_ = bf16[128,1152]{1,0:T(8,128)(2,1)S(1)} collective-permute-done((bf16[128,1152]{1,0:T(8,128)(2,1)}, bf16[128,1152]{1,0:T(8,128)(2,1)S(1)}, u32[]{:S(2)}, u32[]{:S(2)}) %collective-permute-start.32) | collective-permute-done | bytes 294944 | tf_op jit(solution)/shard_map/ppermute | solution.py:65
  206.0 11.8 %collective-permute-done.34.rest_3_ = bf16[128,1152]{1,0:T(8,128)(2,1)S(1)} collective-permute-done((bf16[128,1152]{1,0:T(8,128)(2,1)}, bf16[128,1152]{1,0:T(8,128)(2,1)S(1)}, u32[]{:S(2)}, u32[]{:S(2)}) %collective-permute-start.34) | collective-permute-done | bytes 294944 | tf_op jit(solution)/shard_map/ppermute | solution.py:65
  225.2 8.1 %collective-permute-done.39.rest_11_ = bf16[128,1152]{1,0:T(8,128)(2,1)S(1)} collective-permute-done((bf16[128,1152]{1,0:T(8,128)(2,1)}, bf16[128,1152]{1,0:T(8,128)(2,1)S(1)}, u32[]{:S(2)}, u32[]{:S(2)}) %collective-permute-start.39) | collective-permute-done | bytes 294944 | tf_op jit(solution)/shard_map/ppermute | solution.py:65
  237.3 12.3 %shard_map.290 = (bf16[384,1152]{1,0:T(8,128)(2,1)}, bf16[2,384,1792]{2,1,0:T(8,128)(2,1)}, f32[128,1152]{1,0:T(8,128)}, bf16[128,1152]{1,0:T(8,128)(2,1)}, bf16[128,1152]{1,0:T(8,128)(2,1)}) custom-call(s32[5]{0:T(128)} %stack.23.where_ref, bf16[384,1728]{1,0:T(8,128)(2,1)} %get-tuple-element.353.one_ref, bf16[384,1728]{1,0:T(8,128)(2,1)} %get-tuple-element.354.two_ref, ...), custom_call_target="tpu_custom_call" | custom-call | tf_op jit(solution)/shard_map/pallas_call | solution.py:426
  254.4 9.5 %shard_map.291 = (bf16[128,1152]{1,0:T(8,128)(2,1)}, bf16[2,128,1792]{2,1,0:T(8,128)(2,1)}, bf16[128,1152]{1,0:T(8,128)(2,1)}) custom-call(s32[5]{0:T(128)} %stack.23.where_ref, bf16[128,1728]{1,0:T(8,128)(2,1)} %get-tuple-element.350.one_ref, bf16[128,1728]{1,0:T(8,128)(2,1)} %get-tuple-element.351.two_ref, bf16[3,144,1728]{2,1,0:T(8,128)(2,1)} %shard_map.284.rest_0_, ...), custom_call_target="tpu_custom_call" | custom-call | tf_op jit(solution)/shard_map/pallas_call | solution.py:426
  265.0 13.4 %collective-permute-start.42 = (bf16[128,1152]{1,0:T(8,128)(2,1)}, bf16[128,1152]{1,0:T(8,128)(2,1)S(1)}, u32[]{:S(2)}, u32[]{:S(2)}) collective-permute-start(bf16[128,1152]{1,0:T(8,128)(2,1)} %get-tuple-element.371), channel_id=1, source_target_pairs={{0,1},{1,2},{2,3},{3,0},{4,5},{5,6},{6,7},{7,4},{8,9},{9,10},{10,1... | collective-permute-start | bytes 884744 | tf_op jit(solution)/shard_map/ppermute | solution.py:65
  279.1 15.4 %shard_map.292 = (bf16[3,160,1792]{2,1,0:T(8,128)(2,1)}, bf16[3,160,1792]{2,1,0:T(8,128)(2,1)}, bf16[3,128,1792]{2,1,0:T(8,128)(2,1)}, bf16[3,128,1792]{2,1,0:T(8,128)(2,1)}) custom-call(s32[5]{0:T(128)} %stack.23.where_ref, bf16[512,1152]{1,0:T(8,128)(2,1)} %get-tuple-element.338.rest_0_, bf16[512,1152]{1,0:T(8,128)(2,1)} %collective-permute-done.35.rest_1_, ...), custom_call_target="tpu_custom_call" | custom-call | tf_op jit(solution)/shard_map/pallas_call | solution.py:426
  299.8 7.0 %shard_map.293 = (f32[128,1152]{1,0:T(8,128)}, bf16[128,1152]{1,0:T(8,128)(2,1)}, bf16[128,1024]{1,0:T(8,128)(2,1)}, f32[1,1152]{1,0:T(1,128)}, f32[1,1152]{1,0:...) custom-call(s32[5]{0:T(128)} %stack.23.where_ref, ...), custom_call_target="tpu_custom_call" | custom-call | tf_op jit(solution)/shard_map/pallas_call | solution.py:426
  315.8 5.9 %collective-permute-done.49.rest_2_ = bf16[128,512]{1,0:T(8,128)(2,1)S(1)} collective-permute-done((bf16[128,512]{1,0:T(8,128)(2,1)}, bf16[128,512]{1,0:T(8,128)(2,1)S(1)}, u32[]{:S(2)}, u32[]{:S(2)}) %collective-permute-start.49) | collective-permute-done | bytes 131104 | tf_op jit(solution)/shard_map/ppermute | solution.py:65
  329.3 8.7 %collective-permute-done.57.rest_2_ = bf16[128,1152]{1,0:T(8,128)(2,1)} collective-permute-done((bf16[128,1152]{1,0:T(8,128)(2,1)S(1)}, bf16[128,1152]{1,0:T(8,128)(2,1)}, u32[]{:S(2)}, u32[]{:S(2)}) %collective-permute-start.57) | collective-permute-done | bytes 294944 | tf_op jit(solution)/shard_map/ppermute | solution.py:65
  338.9 6.2 %shard_map.295 = (bf16[128,1152]{1,0:T(8,128)(2,1)}, bf16[144,384]{1,0:T(8,128)(2,1)}, bf16[144,384]{1,0:T(8,128)(2,1)}, bf16[144,384]{1,0:T(8,128)(2,1)}, bf16[144,384]{1,0:T(8,128)(2,1)}) custom-call(s32[5]{0:T(128)} %stack.23.where_ref, f32[128,1280]{1,0:T(8,128)} %get-tuple-element.346.raw_ref, bf16[128,1024]{1,0:T(8,128)(2,1)} %get-tuple-element.387.query_ref, ...), custom_call_target="tpu_custom_call" | custom-call | tf_op jit(solution)/shard_map/pallas_call | solution.py:426
  345.1 5.4 %collective-permute-done.56.rest_3_ = bf16[144,1024]{1,0:T(8,128)(2,1)} collective-permute-done((bf16[144,1024]{1,0:T(8,128)(2,1)}, bf16[144,1024]{1,0:T(8,128)(2,1)}, u32[]{:S(2)}, u32[]{:S(2)}) %collective-permute-start.56) | collective-permute-done | bytes 294944 | tf_op jit(solution)/shard_map/ppermute | solution.py:1440
  (302 shorter events, 172.8 us)
Async XLA Ops:
  4.5 24.1 %all-to-all-start = ((bf16[8,144,216]{2,1,0:T(8,128)(2,1)}), bf16[8,144,216]{2,1,0:T(8,128)(2,1)S(1)}, u32[]{:S(2)}, u32[]{:S(2)}) async-start(bf16[8,144,216]{2,1,0:T(8,128)(2,1)} %bitcast.12), calls=%async_computation | async-start | bytes 1179648 | tf_op jit(solution)/shard_map/all_to_all | solution.py:1492
  34.9 21.2 %collective-permute-start.3 = (bf16[160,2688]{1,0:T(8,128)(2,1)}, bf16[160,2688]{1,0:T(8,128)(2,1)S(1)}, u32[]{:S(2)}, u32[]{:S(2)}) collective-permute-start(bf16[160,2688]{1,0:T(8,128)(2,1)} %shard_map.283.rest_0_.rest_4_), channel_id=1, source_target_pairs={{0,8},{4,12},{8,0},{12,4},{16,24},{20,28},{24,16},{28,20},{1,9},{5... | collective-permute-start | bytes 2580488 | tf_op jit(solution)/shard_map/ppermute | solution.py:60
  36.6 20.9 %collective-permute-start.4 = (bf16[160,2688]{1,0:T(8,128)(2,1)}, bf16[160,2688]{1,0:T(8,128)(2,1)S(1)}, u32[]{:S(2)}, u32[]{:S(2)}) collective-permute-start(bf16[160,2688]{1,0:T(8,128)(2,1)} %shard_map.283.rest_0_.rest_4_), channel_id=1, source_target_pairs={{0,16},{4,20},{8,24},{12,28},{16,0},{20,4},{24,8},{28,12},{1,17},{... | collective-permute-start | bytes 2580488 | tf_op jit(solution)/shard_map/ppermute | solution.py:60
  38.1 20.9 %collective-permute-start.12 = (bf16[3,36,1728]{2,1,0:T(8,128)(2,1)}, bf16[3,36,1728]{2,1,0:T(8,128)(2,1)S(1)}, u32[]{:S(2)}, u32[]{:S(2)}) collective-permute-start(bf16[3,36,1728]{2,1,0:T(8,128)(2,1)} %get-tuple-element.257), channel_id=1, source_target_pairs={{0,1},{1,2},{2,3},{3,0},{4,5},{5,6},{6,7},{7,4},{8,9},{9,10},{10,1... | collective-permute-start | bytes 1119752 | tf_op jit(solution)/shard_map/ppermute | solution.py:65
  43.2 28.6 %collective-permute-start.13 = (bf16[3,36,1728]{2,1,0:T(8,128)(2,1)}, bf16[3,36,1728]{2,1,0:T(8,128)(2,1)S(1)}, u32[]{:S(2)}, u32[]{:S(2)}) collective-permute-start(bf16[3,36,1728]{2,1,0:T(8,128)(2,1)} %get-tuple-element.258), channel_id=1, source_target_pairs={{0,2},{1,3},{2,0},{3,1},{4,6},{5,7},{6,4},{7,5},{8,10},{9,11},{10,... | collective-permute-start | bytes 1119752 | tf_op jit(solution)/shard_map/ppermute | solution.py:65
  44.8 27.0 %collective-permute-start.14 = (bf16[3,36,1728]{2,1,0:T(8,128)(2,1)S(1)}, bf16[3,36,1728]{2,1,0:T(8,128)(2,1)S(1)}, u32[]{:S(2)}, u32[]{:S(2)}) collective-permute-start(bf16[3,36,1728]{2,1,0:T(8,128)(2,1)S(1)} %copy-done.64), channel_id=1, source_target_pairs={{0,3},{1,0},{2,1},{3,2},{4,7},{5,4},{6,5},{7,6},{8,11},{9,8},{10,9... | collective-permute-start | bytes 1119752 | tf_op jit(solution)/shard_map/ppermute | solution.py:65
  94.2 35.6 %collective-permute-start.18 = (bf16[3,144,1728]{2,1,0:T(8,128)(2,1)S(1)}, bf16[3,144,1728]{2,1,0:T(8,128)(2,1)S(1)}, u32[]{:S(2)}, u32[]{:S(2)}) collective-permute-start(bf16[3,144,1728]{2,1,0:T(8,128)(2,1)S(1)} %copy-done.2), channel_id=1, source_target_pairs={{0,8},{4,12},{8,0},{12,4},{16,24},{20,28},{24,16},{28,20},{1,9},{5... | collective-permute-start | bytes 4478984 | tf_op jit(solution)/shard_map/ppermute | solution.py:60
  94.7 35.5 %collective-permute-start.19 = (bf16[3,144,1728]{2,1,0:T(8,128)(2,1)S(1)}, bf16[3,144,1728]{2,1,0:T(8,128)(2,1)}, u32[]{:S(2)}, u32[]{:S(2)}) collective-permute-start(bf16[3,144,1728]{2,1,0:T(8,128)(2,1)S(1)} %copy-done.2), channel_id=1, source_target_pairs={{0,16},{4,20},{8,24},{12,28},{16,0},{20,4},{24,8},{28,12},{1,17},{... | collective-permute-start | bytes 4478984 | tf_op jit(solution)/shard_map/ppermute | solution.py:60
  98.2 33.3 %collective-permute-start.20 = (bf16[3,144,1728]{2,1,0:T(8,128)(2,1)S(1)}, bf16[3,144,1728]{2,1,0:T(8,128)(2,1)}, u32[]{:S(2)}, u32[]{:S(2)}) collective-permute-start(bf16[3,144,1728]{2,1,0:T(8,128)(2,1)S(1)} %copy-done.2), channel_id=1, source_target_pairs={{0,4},{4,0},{8,12},{12,8},{16,20},{20,16},{24,28},{28,24},{1,5},{5... | collective-permute-start | bytes 4478984 | tf_op jit(solution)/shard_map/ppermute | solution.py:60
  131.5 24.3 %collective-permute-start.24 = (bf16[3,80,1728]{2,1,0:T(8,128)(2,1)S(1)}, bf16[3,80,1728]{2,1,0:T(8,128)(2,1)S(1)}, u32[]{:S(2)}, u32[]{:S(2)}) collective-permute-start(bf16[3,80,1728]{2,1,0:T(8,128)(2,1)S(1)} %slice.58), channel_id=1, source_target_pairs={{0,16},{4,20},{8,24},{12,28},{16,0},{20,4},{24,8},{28,12},{1,17},{... | collective-permute-start | bytes 2488328 | tf_op jit(solution)/shard_map/ppermute | solution.py:60
  132.1 23.7 %collective-permute-start.25 = (bf16[3,64,1728]{2,1,0:T(8,128)(2,1)S(1)}, bf16[3,64,1728]{2,1,0:T(8,128)(2,1)S(1)}, u32[]{:S(2)}, u32[]{:S(2)}) collective-permute-start(bf16[3,64,1728]{2,1,0:T(8,128)(2,1)S(1)} %slice.59), channel_id=1, source_target_pairs={{0,8},{4,12},{8,0},{12,4},{16,24},{20,28},{24,16},{28,20},{1,9},{5... | collective-permute-start | bytes 1990664 | tf_op jit(solution)/shard_map/ppermute | solution.py:60
  137.7 18.2 %collective-permute-start.22 = (bf16[128,1152]{1,0:T(8,128)(2,1)S(1)}, bf16[128,1152]{1,0:T(8,128)(2,1)S(1)}, u32[]{:S(2)}, u32[]{:S(2)}) collective-permute-start(bf16[128,1152]{1,0:T(8,128)(2,1)S(1)} %copy-done.41), channel_id=1, source_target_pairs={{0,2},{1,3},{2,0},{3,1},{4,6},{5,7},{6,4},{7,5},{8,10},{9,11},{10,... | collective-permute-start | bytes 884744 | tf_op jit(solution)/shard_map/ppermute | solution.py:65
  138.0 17.8 %collective-permute-start.23 = (bf16[128,1152]{1,0:T(8,128)(2,1)S(1)}, bf16[128,1152]{1,0:T(8,128)(2,1)S(1)}, u32[]{:S(2)}, u32[]{:S(2)}) collective-permute-start(bf16[128,1152]{1,0:T(8,128)(2,1)S(1)} %copy-done.41), channel_id=1, source_target_pairs={{0,3},{1,0},{2,1},{3,2},{4,7},{5,4},{6,5},{7,6},{8,11},{9,8},{10,9... | collective-permute-start | bytes 884744 | tf_op jit(solution)/shard_map/ppermute | solution.py:65
  164.7 24.1 %collective-permute-start.30 = (bf16[128,1152]{1,0:T(8,128)(2,1)S(1)}, bf16[128,1152]{1,0:T(8,128)(2,1)S(1)}, u32[]{:S(2)}, u32[]{:S(2)}) collective-permute-start(bf16[128,1152]{1,0:T(8,128)(2,1)S(1)} %copy-done.30), channel_id=1, source_target_pairs={{0,1},{1,2},{2,3},{3,0},{4,5},{5,6},{6,7},{7,4},{8,9},{9,10},{10,1... | collective-permute-start | bytes 884744 | tf_op jit(solution)/shard_map/ppermute | solution.py:65
  188.9 28.9 %collective-permute-start.36 = (bf16[512,1792]{1,0:T(8,128)(2,1)}, bf16[512,1792]{1,0:T(8,128)(2,1)}, u32[]{:S(2)}, u32[]{:S(2)}) collective-permute-start(bf16[512,1792]{1,0:T(8,128)(2,1)} %get-tuple-element.339.rest_6_), channel_id=1, source_target_pairs={{0,4},{4,0},{8,12},{12,8},{16,20},{20,16},{24,28},{28,24},{1,5},{5... | collective-permute-start | bytes 5505032 | tf_op jit(solution)/shard_map/ppermute | solution.py:60
  189.0 28.8 %collective-permute-start.35 = (bf16[512,1152]{1,0:T(8,128)(2,1)}, bf16[512,1152]{1,0:T(8,128)(2,1)}, u32[]{:S(2)}, u32[]{:S(2)}) collective-permute-start(bf16[512,1152]{1,0:T(8,128)(2,1)} %get-tuple-element.338.rest_0_), channel_id=1, source_target_pairs={{0,4},{4,0},{8,12},{12,8},{16,20},{20,16},{24,28},{28,24},{1,5},{5... | collective-permute-start | bytes 3538952 | tf_op jit(solution)/shard_map/ppermute | solution.py:60
  193.7 24.1 %collective-permute-start.34 = (bf16[128,1152]{1,0:T(8,128)(2,1)}, bf16[128,1152]{1,0:T(8,128)(2,1)S(1)}, u32[]{:S(2)}, u32[]{:S(2)}) collective-permute-start(bf16[128,1152]{1,0:T(8,128)(2,1)} %get-tuple-element.337), channel_id=1, source_target_pairs={{0,2},{1,3},{2,0},{3,1},{4,6},{5,7},{6,4},{7,5},{8,10},{9,11},{10,... | collective-permute-start | bytes 884744 | tf_op jit(solution)/shard_map/ppermute | solution.py:65
  225.2 24.8 %collective-permute-start.38 = (bf16[128,1152]{1,0:T(8,128)(2,1)}, bf16[128,1152]{1,0:T(8,128)(2,1)S(1)}, u32[]{:S(2)}, u32[]{:S(2)}) collective-permute-start(bf16[128,1152]{1,0:T(8,128)(2,1)} %get-tuple-element.352.rest_10_), channel_id=1, source_target_pairs={{0,2},{1,3},{2,0},{3,1},{4,6},{5,7},{6,4},{7,5},{8,10},{9,11},{10,... | collective-permute-start | bytes 884744 | tf_op jit(solution)/shard_map/ppermute | solution.py:65
  265.0 29.5 %collective-permute-start.42 = (bf16[128,1152]{1,0:T(8,128)(2,1)}, bf16[128,1152]{1,0:T(8,128)(2,1)S(1)}, u32[]{:S(2)}, u32[]{:S(2)}) collective-permute-start(bf16[128,1152]{1,0:T(8,128)(2,1)} %get-tuple-element.371), channel_id=1, source_target_pairs={{0,1},{1,2},{2,3},{3,0},{4,5},{5,6},{6,7},{7,4},{8,9},{9,10},{10,1... | collective-permute-start | bytes 884744 | tf_op jit(solution)/shard_map/ppermute | solution.py:65
  278.4 18.7 %collective-permute-start.43 = (bf16[128,1152]{1,0:T(8,128)(2,1)}, bf16[128,1152]{1,0:T(8,128)(2,1)}, u32[]{:S(2)}, u32[]{:S(2)}) collective-permute-start(bf16[128,1152]{1,0:T(8,128)(2,1)} %get-tuple-element.372), channel_id=1, source_target_pairs={{0,2},{1,3},{2,0},{3,1},{4,6},{5,7},{6,4},{7,5},{8,10},{9,11},{10,... | collective-permute-start | bytes 884744 | tf_op jit(solution)/shard_map/ppermute | solution.py:65
  297.1 53.4 %collective-permute-start.52 = (bf16[3,160,1792]{2,1,0:T(8,128)(2,1)}, bf16[3,160,1792]{2,1,0:T(8,128)(2,1)S(1)}, u32[]{:S(2)}, u32[]{:S(2)}) collective-permute-start(bf16[3,160,1792]{2,1,0:T(8,128)(2,1)} %get-tuple-element.411), channel_id=1, source_target_pairs={{0,8},{4,12},{8,0},{12,4},{16,24},{20,28},{24,16},{28,20},{1,9},{5... | collective-permute-start | bytes 5160968 | tf_op jit(solution)/shard_map/ppermute | solution.py:60
  298.3 52.2 %collective-permute-start.53 = (bf16[3,128,1792]{2,1,0:T(8,128)(2,1)}, bf16[3,128,1792]{2,1,0:T(8,128)(2,1)S(1)}, u32[]{:S(2)}, u32[]{:S(2)}) collective-permute-start(bf16[3,128,1792]{2,1,0:T(8,128)(2,1)} %get-tuple-element.412), channel_id=1, source_target_pairs={{0,16},{4,20},{8,24},{12,28},{16,0},{20,4},{24,8},{28,12},{1,17},{... | collective-permute-start | bytes 4128776 | tf_op jit(solution)/shard_map/ppermute | solution.py:60
  357.2 23.9 %collective-permute-start.58 = (bf16[3,80,1792]{2,1,0:T(8,128)(2,1)}, bf16[3,80,1792]{2,1,0:T(8,128)(2,1)S(1)}, u32[]{:S(2)}, u32[]{:S(2)}) collective-permute-start(bf16[3,80,1792]{2,1,0:T(8,128)(2,1)} %get-tuple-element.423), channel_id=1, source_target_pairs={{0,16},{4,20},{8,24},{12,28},{16,0},{20,4},{24,8},{28,12},{1,17},{... | collective-permute-start | bytes 2580488 | tf_op jit(solution)/shard_map/ppermute | solution.py:60
  359.1 22.0 %collective-permute-start.59 = (bf16[3,64,1792]{2,1,0:T(8,128)(2,1)}, bf16[3,64,1792]{2,1,0:T(8,128)(2,1)S(1)}, u32[]{:S(2)}, u32[]{:S(2)}) collective-permute-start(bf16[3,64,1792]{2,1,0:T(8,128)(2,1)} %get-tuple-element.424), channel_id=1, source_target_pairs={{0,8},{4,12},{8,0},{12,4},{16,24},{20,28},{24,16},{28,20},{1,9},{5... | collective-permute-start | bytes 2064392 | tf_op jit(solution)/shard_map/ppermute | solution.py:60
  (122 other events, 1250.4 us)

commit v2 on v1

--- a/solution.py
+++ b/solution.py
@@ -421,16 +421,16 @@
     return {"vmem": pl.BlockSpec(memory_space=pltpu.VMEM), "smem": pl.BlockSpec(memory_space=pltpu.SMEM), "any": pl.BlockSpec(memory_space=pl.ANY)}[name]
 
 
-def kernel_call(body, outs, args, where=None, scratch=(), flops=0, size=0):
-    where = where or {}
+def kernel_call(body, outs, args, where=None, scratch=(), out_where=None):
+    where, out_where = where or {}, out_where or {}
     return pl.pallas_call(
         body,
         out_shape=[jax.ShapeDtypeStruct(s, t) for s, t in outs],
         in_specs=[place(where.get(i, "vmem")) for i in range(len(args))],
-        out_specs=[place("vmem") for _ in outs],
+        out_specs=[place(out_where.get(i, "vmem")) for i in range(len(outs))],
         scratch_shapes=list(scratch),
         compiler_params=pltpu.CompilerParams(vmem_limit_bytes=121 * mega // 2),
-        cost_estimate=pl.CostEstimate(flops=flops, bytes_accessed=size, transcendentals=0),
+        cost_estimate=pl.CostEstimate(flops=0, bytes_accessed=0, transcendentals=0),
     )(*args)
 
 
@@ -711,13 +711,15 @@
     ]
 
 
-def load_weights(index, refs, chunk, target, sems):
+def load_weights(index, pair, last, chunk, target, sems):
     def copies(m):
         result = []
-        for i, (ref, mask, at, rows) in enumerate(pieces_of(refs, chunk)):
+        for i, (ref, mask, at, rows) in enumerate(pieces_of(last if m == 2 else pair, chunk)):
             start = pl.multiple_of((index ^ mask) * chunk + at, 16)
             result.append(
-                pltpu.make_async_copy(ref.at[m], target.at[m, pl.ds(start, rows)], sems.at[m, i])
+                pltpu.make_async_copy(
+                    ref if m == 2 else ref.at[m], target.at[m, pl.ds(start, rows)], sems.at[m, i]
+                )
             )
         return result
 
@@ -748,64 +750,79 @@
     ]
 
 
-def feed_forward(where, pieces, weights):
+def feed_forward(where, pieces, weights, with_own):
     count, width = pieces[0].shape
-    kinds, chunk, inner = weights[0].shape
+    (pair, last), kinds = weights, 3
+    _, chunk, inner = pair[0].shape
     lanes = -(-inner // 128) * 128
-    near, spots = len(pieces), len(weights)
-    total, early = near * count, (near - 1) * count
+    near, spots = len(pieces), len(pair)
+    total = near * count
     slope = (2.0 / np.pi) ** 0.5
 
     def body(where_ref, *rest):
-        shards, rest = rest[:spots], rest[spots:]
-        parts = rest[:near]
-        group_out, act_out, *slopes = rest[near : near + 6]
-        sums = rest[near + 6 : near + 6 + near]
-        weight, sems = rest[near + 6 + near :]
-        copies = load_weights(where_ref[0], shards, chunk, weight, sems)
+        pair_refs, last_refs, rest = rest[:spots], rest[spots : 2 * spots], rest[2 * spots :]
+        parts, outs, sums = rest[:near], rest[near : near + 3], rest[near + 3 : near + 3 + near]
+        weight, group, act, slopes, gates, sems, out_sems = rest[near + 3 + near :]
+        copies = load_weights(where_ref[0], pair_refs, last_refs, chunk, weight, sems)
         for kind in copies:
             for copy in kind:
                 copy.start()
         for k in range(near):
-            group_out[k * count : (k + 1) * count, :] = parts[k][...]
-        for kind in copies[:2]:
-            for copy in kind:
-                copy.wait()
+            group[k * count : (k + 1) * count, :] = parts[k][...]
+        stores = [
+            pltpu.make_async_copy(source, out, out_sems.at[i])
+            for i, (source, out) in enumerate(zip((group, act, slopes), outs))
+        ]
+        stores[0].start()
+        for copy in copies[0]:
+            copy.wait()
         for low, high in column_steps(inner, 256):
-            gate = dot(group_out[...], weight[0, :, low:high], 1, 0)
-            upper = dot(group_out[...], weight[1, :, low:high], 1, 0)
-            bent = jnp.tanh(slope * (gate + 0.044715 * (gate * gate * gate)))
-            half = 0.5 * (1.0 + bent)
+            gates[:, low:high] = dot(group[...], weight[0, :, low:high], 1, 0)
+        for copy in copies[1]:
+            copy.wait()
+        for low, high in column_steps(inner, 256):
+            gate = gates[:, low:high]
+            upper = dot(group[...], weight[1, :, low:high], 1, 0)
+            square = 0.044715 * slope * gate * gate
+            half = 0.5 + 0.5 * jnp.tanh(gate * (slope + square))
             gelu = gate * half
-            steep = half + 0.5 * gate * (1.0 - bent * bent) * (
-                slope * (1.0 + 3.0 * 0.044715 * gate * gate)
-            )
-            act_out[:, low:high] = (gelu * upper).astype(jnp.bfloat16)
-            for value, outs in ((steep * upper, slopes[:2]), (gelu, slopes[2:])):
-                outs[0][:, low:high] = value[:early].astype(jnp.bfloat16)
-                outs[1][:, low:high] = value[early:].astype(jnp.bfloat16)
+            steep = half * (1.0 + 2.0 * (gate - gelu) * (slope + 3.0 * square))
+            act[:, low:high] = (gelu * upper).astype(jnp.bfloat16)
+            slopes[0, :, low:high] = (steep * upper).astype(jnp.bfloat16)
+            slopes[1, :, low:high] = gelu.astype(jnp.bfloat16)
         if lanes > inner:
-            act_out[:, inner:] = jnp.zeros((total, lanes - inner), jnp.bfloat16)
+            act[:, inner:] = jnp.zeros((total, lanes - inner), jnp.bfloat16)
+        for store in stores[1:]:
+            store.start()
         for copy in copies[2]:
             copy.wait()
-        for low, high in column_steps(width, 384):
-            part = dot(act_out[:, :inner], weight[2, low:high, :], 1, 1)
+        for low, high in column_steps(width, 256):
+            part = dot(act[:, :inner], weight[2, low:high, :], 1, 1)
             for k in range(near):
                 sums[k][:, low:high] = part[k * count : (k + 1) * count].astype(sums[k].dtype)
-
-    return kernel_call(
-        body,
-        [((total, width), jnp.bfloat16)]
-        + [((total, lanes), jnp.bfloat16)]
-        + [((early, inner), jnp.bfloat16), ((count, inner), jnp.bfloat16)] * 2
-        + [((count, width), jnp.float32)]
-        + [((count, width), jnp.bfloat16)] * (near - 1),
-        [where, *weights, *pieces],
-        {0: "smem", **{1 + i: "any" for i in range(spots)}},
+        for store in stores:
+            store.wait()
+
+    return kernel_call(
+        body,
+        [
+            ((total, width), jnp.bfloat16),
+            ((total, lanes), jnp.bfloat16),
+            ((2, total, inner), jnp.bfloat16),
+        ]
+        + [((count, width), jnp.float32 if with_own and k == 0 else jnp.bfloat16) for k in range(near)],
+        [where, *pair, *last, *pieces],
+        {0: "smem", **{1 + i: "any" for i in range(2 * spots)}},
         [
             pltpu.VMEM((kinds, width, inner), jnp.bfloat16),
+            pltpu.VMEM((total, width), jnp.bfloat16),
+            pltpu.VMEM((total, lanes), jnp.bfloat16),
+            pltpu.VMEM((2, total, inner), jnp.bfloat16),
+            pltpu.VMEM((total, inner), jnp.float32),
             pltpu.SemaphoreType.DMA((kinds, spots)),
+            pltpu.SemaphoreType.DMA((3,)),
         ],
+        {i: "any" for i in range(3)},
     )
 
 
@@ -836,20 +853,21 @@
     )
 
 
-def feed_back(where, pieces, weights, one, two, with_own):
+def feed_back(where, pieces, weights, slopes, with_own):
     count, width = pieces[0].shape
-    kinds, chunk, inner = weights[0].shape
+    (pair, last), kinds = weights, 3
+    _, chunk, inner = pair[0].shape
     lanes = -(-inner // 128) * 128
-    near, spots = len(pieces), len(weights)
+    near, spots = len(pieces), len(pair)
     total = near * count
 
-    def body(where_ref, one_ref, two_ref, *rest):
-        shards, rest = rest[:spots], rest[spots:]
+    def body(where_ref, slopes_ref, *rest):
+        pair_refs, last_refs, rest = rest[:spots], rest[spots : 2 * spots], rest[2 * spots :]
         parts = rest[:near]
         group_out, both_out = rest[near : near + 2]
         sums = rest[near + 2 : near + 2 + near]
         weight, sems = rest[near + 2 + near :]
-        copies = load_weights(where_ref[0], shards, chunk, weight, sems)
+        copies = load_weights(where_ref[0], pair_refs, last_refs, chunk, weight, sems)
         for kind in (copies[2], copies[0], copies[1]):
             for copy in kind:
                 copy.start()
@@ -859,16 +877,15 @@
             copy.wait()
         for low, high in column_steps(inner, 256):
             grad = dot(group_out[...], weight[2, :, low:high], 1, 0)
-            for i, ref in enumerate((one_ref, two_ref)):
-                both_out[i, :, low:high] = (grad * ref[:, low:high].astype(jnp.float32)).astype(
-                    jnp.bfloat16
-                )
+            for i in range(2):
+                slope = slopes_ref[i, :, low:high].astype(jnp.float32)
+                both_out[i, :, low:high] = (grad * slope).astype(jnp.bfloat16)
         if lanes > inner:
             both_out[:, :, inner:] = jnp.zeros((2, total, lanes - inner), jnp.bfloat16)
         for kind in copies[:2]:
             for copy in kind:
                 copy.wait()
-        for low, high in column_steps(width, 384):
+        for low, high in column_steps(width, 256):
             part = dot(both_out[0, :, :inner], weight[0, low:high, :], 1, 1)
             part = part + dot(both_out[1, :, :inner], weight[1, low:high, :], 1, 1)
             for k in range(near):
@@ -879,8 +896,8 @@
         [((total, width), jnp.bfloat16)]
         + [((2, total, lanes), jnp.bfloat16)]
         + [((count, width), jnp.float32 if with_own and k == 0 else jnp.bfloat16) for k in range(near)],
-        [where, one, two, *weights, *pieces],
-        {0: "smem", **{3 + i: "any" for i in range(spots)}},
+        [where, slopes, *pair, *last, *pieces],
+        {0: "smem", **{2 + i: "any" for i in range(2 * spots)}},
         [
             pltpu.VMEM((kinds, width, inner), jnp.bfloat16),
             pltpu.SemaphoreType.DMA((kinds, spots)),
@@ -888,105 +905,126 @@
     )
 
 
-def wide_grads(where, two, two_far, back, back_far, act, act_far, both, both_far):
-    total, width = two.shape
-    inner = act.shape[1]
+def wide_grads(where, lefts, rights):
+    width = lefts[0].shape[1]
+    total = sum(left.shape[0] for left in lefts)
+    lanes = rights[0][0][0].shape[-1]
+    kinds = len(rights)
     chunk = width // 8
     first, second = halves_of(chunk)
-
-    cuts = [(0, back[0].shape[0]), (back[0].shape[0], total)]
+    arrays = []
+    for array in [r for right in rights for r, _ in right]:
+        if all(array is not other for other in arrays):
+            arrays.append(array)
+    spots = [[[array is other for other in arrays].index(True) for array, _ in right] for right in rights]
+    most = max(len(right) for right in rights)
 
     def body(where_ref, *rest):
-        twos, backs, acts, boths = rest[0:2], rest[2:6], rest[6:8], rest[8:12]
-        outs = rest[12:16]
-        turned, left = rest[16:]
+        left_refs, right_refs = rest[: len(lefts)], rest[len(lefts) : len(lefts) + len(arrays)]
+        outs = rest[len(lefts) + len(arrays) : len(lefts) + len(arrays) + 4]
+        turned, left, values, sems = rest[len(lefts) + len(arrays) + 4 :]
+        copies = []
+        for m, right in enumerate(rights):
+            at, row = [], 0
+            for i, (array, index) in enumerate(right):
+                ref = right_refs[spots[m][i]]
+                size = array.shape[-2]
+                at.append(
+                    pltpu.make_async_copy(
+                        ref if index is None else ref.at[index],
+                        values.at[m, pl.ds(row, size)],
+                        sems.at[m, i],
+                    )
+                )
+                row += size
+            copies.append(at)
+        for part in copies:
+            for copy in part:
+                copy.start()
         core, x, y = where_ref[1], where_ref[2], where_ref[3]
         order = []
         for flip in (1, 0):
             order.append([(j * 2 + jnp.bitwise_xor(x, flip), 0, first) for j in range(2)])
         for flip in (1, 0):
             order.append([(jnp.bitwise_xor(y, flip) * 2 + j, first, second) for j in range(2)])
-        for index, kinds in ((0, (0, 1)), (1, (2,))):
-            for side in range(2):
-                if index == 0:
-                    turned[:, side * total : (side + 1) * total] = twos[side][...].T
-                else:
-                    for i, (start, end) in enumerate(cuts):
-                        turned[:, side * total + start : side * total + end] = backs[
-                            2 * side + i
-                        ][...].T
-            at = 0
-            for block in order:
-                for plane, offset, size in block:
-                    start = pl.multiple_of((plane * 2 + core) * chunk + offset, 16)
-                    left[at : at + size, :] = turned[pl.ds(start, size), :]
+        row = 0
+        for ref in left_refs:
+            turned[:, row : row + ref.shape[0]] = ref[...].T
+            row += ref.shape[0]
+        at = 0
+        for block in order:
+            for plane, offset, size in block:
+                start = pl.multiple_of((plane * 2 + core) * chunk + offset, 16)
+                left[at : at + size, :] = turned[pl.ds(start, size), :]
+                at += size
+        for m in range(kinds):
+            for copy in copies[m]:
+                copy.wait()
+            for low, high in column_steps(lanes, 256):
+                part = dot(left[...], values[m, :, low:high], 1, 0).astype(jnp.bfloat16)
+                at = 0
+                for out, block in zip(outs, order):
+                    size = 2 * block[0][2]
+                    out[m, :, low:high] = part[at : at + size]
                     at += size
-            for m in kinds:
-                for low, high in column_steps(inner, 256):
-                    if m == 2:
-                        rights = [acts[0][:, low:high], acts[1][:, low:high]]
-                    else:
-                        rights = [b[m, :, low:high] for b in boths]
-                    right = jnp.concatenate(rights, axis=0)
-                    part = dot(left[...], right, 1, 0)
-                    part = part.astype(jnp.bfloat16)
-                    at = 0
-                    for out, block in zip(outs, order):
-                        size = 2 * block[0][2]
-                        out[m, :, low:high] = part[at : at + size]
-                        at += size
-
-    return kernel_call(
-        body,
-        [
-            ((3, 2 * first, inner), jnp.bfloat16),
-            ((3, 2 * first, inner), jnp.bfloat16),
-            ((3, 2 * second, inner), jnp.bfloat16),
-            ((3, 2 * second, inner), jnp.bfloat16),
+
+    return kernel_call(
+        body,
+        [
+            ((kinds, 2 * first, lanes), jnp.bfloat16),
+            ((kinds, 2 * first, lanes), jnp.bfloat16),
+            ((kinds, 2 * second, lanes), jnp.bfloat16),
+            ((kinds, 2 * second, lanes), jnp.bfloat16),
         ],
-        [where, two, two_far, *back, *back_far, act, act_far, *both, *both_far],
+        [where, *lefts, *arrays],
+        {0: "smem", **{1 + len(lefts) + i: "any" for i in range(len(arrays))}},
+        [
+            pltpu.VMEM((width, total), jnp.bfloat16),
+            pltpu.VMEM((width // 2, total), jnp.bfloat16),
+            pltpu.VMEM((kinds, total, lanes), jnp.bfloat16),
+            pltpu.SemaphoreType.DMA((kinds, most)),
+        ],
+    )
+
+
+def wide_middle(where, wides, gots):
+    sizes = [wide[0].shape[0] for wide in wides]
+    kinds = sum(sizes)
+    first, second = wides[0][1].shape[1] // 2, wides[0][3].shape[1] // 2
+    lanes = wides[0][1].shape[2]
+    args = [a for wide, got in zip(wides, gots) for a in (wide[1], got[0], wide[3], got[1])]
+
+    def body(where_ref, *rest):
+        refs, outs = rest[: len(args)], rest[len(args) :]
+        x, y = where_ref[2], where_ref[3]
+        at = 0
+        for i, size in enumerate(sizes):
+            kept_a, got_a, kept_b, got_b = refs[4 * i : 4 * i + 4]
+            for m in range(size):
+                for kept, got, place, rows, pair in (
+                    (kept_a, got_a, y, first, outs[:2]),
+                    (kept_b, got_b, x, second, outs[2:]),
+                ):
+                    for flip, out in ((1, pair[0]), (0, pair[1])):
+                        spot = pl.ds(
+                            pl.multiple_of(jnp.bitwise_xor(place, flip) * rows, 16), rows
+                        )
+                        total = kept[m, spot, :].astype(jnp.float32) + got[m, spot, :].astype(
+                            jnp.float32
+                        )
+                        out[at] = total.astype(jnp.bfloat16)
+                at += 1
+
+    return kernel_call(
+        body,
+        [((kinds, first, lanes), jnp.bfloat16)] * 2 + [((kinds, second, lanes), jnp.bfloat16)] * 2,
+        [where, *args],
         {0: "smem"},
-        [
-            pltpu.VMEM((width, 2 * total), jnp.bfloat16),
-            pltpu.VMEM((width // 2, 2 * total), jnp.bfloat16),
-        ],
-    )
-
-
-def wide_middle(where, kept_a, got_a, kept_b, got_b):
-    kinds, twice_a, inner = kept_a.shape
-    first, second = twice_a // 2, kept_b.shape[1] // 2
-
-    def body(where_ref, kept_a_ref, got_a_ref, kept_b_ref, got_b_ref, *outs):
-        x, y = where_ref[2], where_ref[3]
-        for m in range(kinds):
-            for flip, out in ((1, outs[0]), (0, outs[1])):
-                rows = pl.ds(pl.multiple_of(jnp.bitwise_xor(y, flip) * first, 16), first)
-                total = kept_a_ref[m, rows, :].astype(jnp.float32) + got_a_ref[m, rows, :].astype(
-                    jnp.float32
-                )
-                out[m] = total.astype(jnp.bfloat16)
-            for flip, out in ((1, outs[2]), (0, outs[3])):
-                rows = pl.ds(pl.multiple_of(jnp.bitwise_xor(x, flip) * second, 16), second)
-                total = kept_b_ref[m, rows, :].astype(jnp.float32) + got_b_ref[m, rows, :].astype(
-                    jnp.float32
-                )
-                out[m] = total.astype(jnp.bfloat16)
-
-    return kernel_call(
-        body,
-        [
-            ((kinds, first, inner), jnp.bfloat16),
-            ((kinds, first, inner), jnp.bfloat16),
-            ((kinds, second, inner), jnp.bfloat16),
-            ((kinds, second, inner), jnp.bfloat16),
-        ],
-        [where, kept_a, got_a, kept_b, got_b],
-        {0: "smem"},
-    )
-
-
-def wide_last(kept_a, got_a, kept_b, got_b, inner):
+    )
+
+
+def wide_last(wide, got, inner):
+    (_, kept_a, _, kept_b), (got_a, got_b) = wide, got
     kinds, first, _ = kept_a.shape
     second = kept_b.shape[1]
 
@@ -1329,14 +1367,47 @@
     )
 
 
-def split_wide(where, gate, up, down, ctx):
+def narrow_last(blocks, out_blocks, sizes, cols):
+    rows = out_blocks[0].shape[0]
+    near = len(blocks)
+    q, k, v = cols
+
+    def body(*rest):
+        outs = rest[2 * near :]
+        total = rest[0][...]
+        for r in rest[1:near]:
+            total = total + r[...].astype(jnp.float32)
+        outs[0][...] = total[:rows, :q]
+        turned = total[:rows, q:].T
+        outs[1][...] = turned[:k]
+        outs[2][...] = turned[k:]
+        out = rest[near][...]
+        for r in rest[near + 1 : 2 * near]:
+            out = out + r[...].astype(jnp.float32)
+        outs[3][...] = out
+        start = 0
+        for ref, size in zip(outs[4:], sizes):
+            ref[...] = total[rows : rows + 1, start : start + size]
+            start += size
+
+    return kernel_call(
+        body,
+        [
+            ((rows, q), jnp.float32),
+            ((k, rows), jnp.float32),
+            ((v, rows), jnp.float32),
+            ((rows, out_blocks[0].shape[1]), jnp.float32),
+        ]
+        + [((1, size), jnp.float32) for size in sizes],
+        [*blocks, *out_blocks],
+    )
+
+
+def split_pair(where, gate, up, ctx):
     rows, whole = gate.shape
     inner = whole // ctx
-    groups, chunk, part = down.shape
-    per, steps = groups // ctx, chunk // rows
-
-    def body(where_ref, gate_ref, up_ref, down_ref, *rest):
-        outs, wide = rest[:ctx], rest[ctx]
+
+    def body(where_ref, gate_ref, up_ref, *outs):
         mine = where_ref[4]
         for c in range(ctx):
 
@@ -1346,26 +1417,15 @@
                     j = (c + k) % ctx
                     outs[k][0] = gate_ref[:, j * inner : (j + 1) * inner]
                     outs[k][1] = up_ref[:, j * inner : (j + 1) * inner]
-                    for b in range(groups):
-                        first = b % steps * rows
-                        wide[:, b * part : (b + 1) * part] = down_ref[
-                            j * per + b // steps, first : first + rows, :
-                        ].astype(jnp.float32)
-                    outs[k][2] = wide[...].astype(jnp.bfloat16)
-
-    return kernel_call(
-        body,
-        [((3, rows, inner), jnp.bfloat16)] * ctx,
-        [where, gate, up, down],
-        {0: "smem"},
-        [pltpu.VMEM((rows, inner), jnp.float32)],
-    )
-
-
-def join_wide(where, pieces, part):
+
+    return kernel_call(
+        body, [((2, rows, inner), jnp.bfloat16)] * ctx, [where, gate, up], {0: "smem"}
+    )
+
+
+def join_pair(where, pieces):
     ctx = len(pieces)
     _, rows, inner = pieces[0].shape
-    chunk, groups = ctx * rows, inner // part
 
     def body(where_ref, *rest):
         got, out, wide = rest[:ctx], rest[ctx], rest[ctx + 1]
@@ -1380,19 +1440,95 @@
                             jnp.float32
                         )
                     out[m] = wide[...].astype(jnp.bfloat16)
+
+    return kernel_call(
+        body,
+        [((2, ctx * rows, inner), jnp.bfloat16)],
+        [where, *pieces],
+        {0: "smem"},
+        [pltpu.VMEM((ctx * rows, inner), jnp.float32)],
+    )[0]
+
+
+def share_down(where, down):
+    width, part = down.shape
+    chunk = width // 8
+
+    def body(where_ref, down_ref, *outs):
+        plane, core = where_ref[0] // 2, where_ref[1]
+        for flip, out in enumerate(outs):
+            for m in range(4):
+                group = jnp.bitwise_xor(plane, m) * 2 + jnp.bitwise_xor(core, flip)
+                out[m] = down_ref[pl.ds(pl.multiple_of(group * chunk, 16), chunk), :]
+
+    return kernel_call(
+        body, [((4, chunk, part), jnp.bfloat16)] * 2, [where, down], {0: "smem"}
+    )
+
+
+def split_down(where, pieces, rows, ctx):
+    groups = 2 * len(pieces)
+    _, chunk, part = pieces[0].shape
+    per, steps = groups // ctx, chunk // rows
+
+    def body(where_ref, *rest):
+        got, outs, (wide, down_ref) = rest[:4], rest[4 : 4 + ctx], rest[4 + ctx :]
+        mine = where_ref[4]
+        plane, core = where_ref[0] // 2, where_ref[1]
+        for m in range(4):
+            for flip in range(2):
+                group = jnp.bitwise_xor(plane, m) * 2 + jnp.bitwise_xor(core, flip)
+                down_ref[pl.ds(group, 1)] = got[m][flip][None]
+        for c in range(ctx):
+
+            @pl.when(mine == c)
+            def _(c=c):
+                for k in range(ctx):
+                    j = (c + k) % ctx
+                    for b in range(groups):
+                        first = b % steps * rows
+                        wide[:, b * part : (b + 1) * part] = down_ref[
+                            j * per + b // steps, first : first + rows, :
+                        ].astype(jnp.float32)
+                    outs[k][...] = wide[...].astype(jnp.bfloat16)
+
+    return kernel_call(
+        body,
+        [((rows, groups * part), jnp.bfloat16)] * ctx,
+        [where, *pieces],
+        {0: "smem"},
+        [
+            pltpu.VMEM((rows, groups * part), jnp.float32),
+            pltpu.VMEM((groups, chunk, part), jnp.bfloat16),
+        ],
+    )
+
+
+def join_down(where, pieces, part):
+    ctx = len(pieces)
+    rows, inner = pieces[0].shape
+    chunk, groups = ctx * rows, inner // part
+
+    def body(where_ref, *rest):
+        got, out, wide = rest[:ctx], rest[ctx], rest[ctx + 1]
+        mine = where_ref[4]
+        for c in range(ctx):
+
+            @pl.when(mine == c)
+            def _(c=c):
                 for a in range(ctx):
-                    piece = got[(c - a) % ctx][2].astype(jnp.float32)
+                    piece = got[(c - a) % ctx][...].astype(jnp.float32)
                     for b in range(groups):
                         first = b % ctx * rows
                         at = (b // ctx * ctx + a) * part
                         wide[first : first + rows, at : at + part] = piece[
                             :, b * part : (b + 1) * part
                         ]
-                out[2] = wide[...].astype(jnp.bfloat16)
-
-    return kernel_call(
-        body,
-        [((3, chunk, inner), jnp.bfloat16)],
+                out[...] = wide[...].astype(jnp.bfloat16)
+
+    return kernel_call(
+        body,
+        [((chunk, inner), jnp.bfloat16)],
         [where, *pieces],
         {0: "smem"},
         [pltpu.VMEM((chunk, inner), jnp.float32)],
@@ -1486,33 +1622,37 @@
     gains = [gain_in, gain_query, gain_key, gain_attn, gain_pre, gain_post]
     sizes = [g.shape[0] for g in gains]
     chunk, out_rows = width // dp, heads * head_dim // dp
+    order = [0, 1, 3, 2]
     packed = pack(w_query, w_key, w_value, w_out, gains)
     split = packed.shape[1] - width
-    downs = gate(w_down, packed).T.reshape(dp, chunk, w_down.shape[0])
-    downs = lax.all_to_all(downs, "dp", split_axis=0, concat_axis=0, tiled=True)
+    kept, sent = share_down(where, gate(w_down, packed).T)
     packed = ctx_gather(packed)
+    got = swap(sent, 0)
+    downs = plane_send([jnp.stack([kept[m], got[m]]) for m in range(4)])
     aux = tables(where, lengths, count, stretch, ctx, head_dim)
     packed, downs, aux = stage(packed, downs, aux)
     cosine, sine, valid, allowed = aux
 
-    blocks = list(split_wide(where, w_gate, w_up, downs.reshape(dp, chunk, -1), ctx))
+    blocks = list(split_pair(where, w_gate, w_up, ctx))
     packed = gate(packed, blocks[0])
     blocks = ctx_send(blocks, 1)
     near = plane_near(join_rows(where, packed, w_query.shape[0], split, w_out.shape[0]))
     shared = plane_whole(near)
-    shared, blocks = stage(shared, blocks)
-
-    shard = join_wide(where, blocks, w_down.shape[0])
+    pair = join_pair(where, blocks)
+    shared, pair, downs = stage(shared, pair, downs)
+
     normed, query, both, raw, norm_in, norm_query, norm_key = project(
         where, tokens, shared, sizes[:3], cosine, sine, heads, ctx
     )
-    shard, normed, query, both = stage(shard, normed, query, both)
-
-    shard = plane_near(shard)
+    pair, normed, query, both, downs = stage(pair, normed, query, both, downs)
+
+    pair = plane_near(pair)
+    downs = list(split_down(where, downs, w_gate.shape[0], ctx))
     norm_attn, norm_pre, norm_post = late_gains(
         where, shared, [384, 512, 640], sizes[3:], ctx, both
     )
     both = ctx_gather(both)
+    downs = ctx_send(gate(downs, both), 1)
     probs, mixed, attn_raw, residual, normed_two = attend(
         where,
         tokens,
@@ -1526,55 +1666,80 @@
         out_rows,
         heads,
     )
-    far = [swap(gate(shard[0], both[2]), 0)]
-    shard, far, halves, normed_two, mixed = stage(shard, far, cut(shard), normed_two, mixed)
-
-    halves = diagonal(halves)
-    two_pieces = ctx_gather(normed_two)
-    two_pieces, halves, shard, normed = stage(two_pieces, halves, shard, normed)
-
-    weights = shard + halves
-    weights = weights + far + [swap(w, 0) for w in weights[1:]]
-    two_pieces, weights, normed = stage(two_pieces, weights, normed)
-
-    order = [0, 1, 3, 2]
+    pair, pair_cut, downs, normed_two, mixed = stage(pair, cut(pair), downs, normed_two, mixed)
+
+    last = plane_near(join_down(where, downs, w_down.shape[0]))
+    two_pieces = [normed_two] + [shift(normed_two, k) for k in order[1:-1]]
+    pair_far = [swap(pair[0], 0)]
+    two_pieces, pair, pair_far, last, last_cut, normed = stage(
+        two_pieces, pair, pair_far, last, cut(last), normed
+    )
+
+    two_pieces.append(shift(two_pieces[0], order[-1]))
+    pair = pair + diagonal(pair_cut)
+    pair_far = pair_far + [swap(p, 0) for p in pair[1:3]]
+    two_pieces, pair, pair_far, last, last_cut, normed = stage(
+        two_pieces, pair, pair_far, last, last_cut, normed
+    )
+
+    last = last + diagonal(last_cut)
+    pair_far = pair_far + [swap(p, 0) for p in pair[3:]]
+    pair, last = pair + pair_far, last + [swap(p, 0) for p in last]
+    two_pieces, pair, last, normed = stage(two_pieces, pair, last, normed)
+
+    weights = (pair, last)
     normed_group = [normed, shift(normed, 1), None, shift(normed, 3)]
-    group_two, act, one, one_last, two, two_last, *sums = feed_forward(
-        where, [two_pieces[k] for k in order], weights
-    )
-    group_two, act, one, one_last, two, two_last, sums, near_group = stage(
-        group_two, act, one, one_last, two, two_last, sums, [normed_group[1], normed_group[3]]
+    group_two, act, slopes, *sums = feed_forward(where, two_pieces[:-1], weights, True)
+    group_two, act, slopes, sums, near_group = stage(
+        group_two, act, slopes, sums, [normed_group[1], normed_group[3]]
     )
     normed_group[1], normed_group[3] = near_group
 
-    sums = [sums[0]] + [shift(sums[i], -order[i]) for i in range(1, ctx)]
-    group_two_far, act_far, mixed_far = swap(group_two, 0), swap(act, 0), swap(mixed, 0)
+    sums = [sums[0]] + [shift(sums[i], -order[i]) for i in range(1, ctx - 1)]
+    two_last, act_last, slopes_last, sum_last = feed_forward(
+        where, two_pieces[-1:], weights, False
+    )
+    sums, two_last, act_last, slopes_last, sum_last, group_two, act, mixed = stage(
+        sums, two_last, act_last, slopes_last, sum_last, group_two, act, mixed
+    )
+
+    sums.append(shift(sum_last, -order[-1]))
+    group_two, act = [group_two, two_last], [act, act_last]
+    group_two_far, act_far = [swap(g, 0) for g in group_two], [swap(a, 0) for a in act]
+    mixed_far = swap(mixed, 0)
     sums, group_two_far, act_far, mixed_far = stage(sums, group_two_far, act_far, mixed_far)
 
     output, ffn_grad, gain_post_grad = finish(sums, residual, cotangent, valid, norm_post)
-    ffn_pieces = ctx_gather(ffn_grad)
-    ffn_early = [ffn_pieces[k] for k in order[:-1]]
-    group_ffn, grads, *sums = feed_back(where, ffn_early, weights, one, two, True)
-    ffn_last, group_ffn, grads, sums = stage(ffn_pieces[order[-1]], group_ffn, grads, sums)
-
-    ffn_last, grads_last, sum_last = feed_back(
-        where, [ffn_last], weights, one_last, two_last, False
-    )
-    sums[1] = shift(sums[1], -order[1])
-    ffn_last, grads_last, sum_last, group_ffn, grads, sums = stage(
-        ffn_last, grads_last, sum_last, group_ffn, grads, sums
-    )
-
-    sums[2] = shift(sums[2], -order[2])
+    ffn_early = [ffn_grad] + [shift(ffn_grad, k) for k in order[1:-1]]
+    ffn_early, ffn_grad = stage(ffn_early, ffn_grad)
+
+    ffn_last = shift(ffn_grad, order[-1])
+    group_ffn, grads, *sums = feed_back(where, ffn_early, weights, slopes, True)
+    ffn_last, group_ffn, grads, sums = stage(ffn_last, group_ffn, grads, sums)
+
+    ffn_parts = [group_ffn, ffn_last]
+    ffn_far = [swap(f, 0) for f in ffn_parts]
+    grads_far = swap(grads, 0)
+    _, grads_last, sum_last = feed_back(
+        where, [ffn_last], weights, slopes_last, False
+    )
+    sums[1], sums[2] = shift(sums[1], -order[1]), shift(sums[2], -order[2])
+    down_wide = wide_grads(
+        where, gate(ffn_parts, grads_last) + ffn_far, [[(a, None) for a in act + act_far]]
+    )
+    grads_last, sum_last, grads, grads_far, sums, down_wide = stage(
+        grads_last, sum_last, grads, grads_far, sums, down_wide
+    )
+
     sums.append(shift(sum_last, -order[-1]))
-    group_ffn, grads = [group_ffn, ffn_last], [grads, grads_last]
-    group_ffn_far, grads_far = [swap(g, 0) for g in group_ffn], [swap(g, 0) for g in grads]
-    send_a, kept_a, send_b, kept_b = wide_grads(
-        where, group_two, group_two_far, group_ffn, group_ffn_far, act, act_far, grads, grads_far
-    )
-    sums, send_a, kept_a, send_b, kept_b = stage(sums, send_a, kept_a, send_b, kept_b)
-
-    got_a, got_b = swap(send_a, 1), swap(send_b, 2)
+    down_got = [swap(down_wide[0], 1), swap(down_wide[2], 2)]
+    all_grads = [grads, grads_last, grads_far, swap(grads_last, 0)]
+    pair_wide = wide_grads(
+        where, group_two + group_two_far, [[(g, m) for g in all_grads] for m in range(2)]
+    )
+    sums, down_wide, down_got, pair_wide = stage(sums, down_wide, down_got, pair_wide)
+
+    pair_got = [swap(pair_wide[0], 1), swap(pair_wide[2], 2)]
     dx, attn_grad, query_grad, gain_pre_grad, gain_attn_grad, gain_query_grad, *parts = attend_back(
         where,
         sums,
@@ -1596,11 +1761,13 @@
         heads,
     )
     parts = ctx_send(parts, -1)
-    normed_group[2] = shift(gate(normed, parts), 2)
     out_blocks = narrow_grads(
         where, [attn_grad, swap(attn_grad, 0)], [mixed, mixed_far], False
     )
-    parts = gate(parts, out_blocks)
+    parts, pair_got, out_blocks, query_grad, dx, normed = stage(
+        parts, pair_got, out_blocks, query_grad, dx, normed
+    )
+
     input_grad, *blocks = project_back(
         where,
         parts,
@@ -1617,53 +1784,39 @@
         ctx,
         [gain_query_grad, gain_attn_grad, gain_pre_grad, gain_post_grad],
     )
+    normed_group[2] = shift(normed, 2)
     out_blocks = plane_send(out_blocks)
-    got_a, got_b, blocks, out_blocks, normed_group = stage(
-        got_a, got_b, list(blocks), out_blocks, normed_group
-    )
+    wide = wide_middle(where, [pair_wide, down_wide], [pair_got, down_got])
+    blocks, out_blocks, wide, normed_group = stage(list(blocks), out_blocks, wide, normed_group)
 
     blocks = ctx_send(blocks, 1)
-    send_a, kept_a, send_b, kept_b = wide_middle(where, kept_a, got_a, kept_b, got_b)
-    got_a, got_b = swap(send_a, 2), swap(send_b, 1)
-    out_blocks = narrow_middle(where, out_blocks, [mixed.shape[1]], ctx)
+    wide_got = [swap(wide[0], 2), swap(wide[2], 1)]
     normed_far = [swap(n, 0) for n in normed_group]
     blocks = narrow_grads(
         where, normed_group + normed_far, blocks + [swap(b, 0) for b in blocks], True
     )
-    got_a, got_b, out_blocks, blocks = stage(got_a, got_b, out_blocks, blocks)
+    out_blocks = narrow_middle(where, out_blocks, [mixed.shape[1]], ctx)
+    wide_got, out_blocks, blocks = stage(wide_got, out_blocks, blocks)
 
     blocks, out_blocks = plane_send(blocks), ctx_send(out_blocks, 1)
-    grad_gate, grad_up, grad_down = wide_last(
-        kept_a, got_a, kept_b, got_b, w_gate.shape[1] // ctx
-    )
+    grad_gate, grad_up, grad_down = wide_last(wide, wide_got, w_gate.shape[1] // ctx)
     blocks, out_blocks, grad_gate = stage(blocks, out_blocks, grad_gate)
 
-    def total(pieces):
-        result = pieces[0].astype(jnp.float32)
-        for p in pieces[1:]:
-            result = result + p.astype(jnp.float32)
-        return result
-
-    grad_out = total(out_blocks).T
-    grad_qkv = total(blocks)
-
-    outs, start = [], 0
-    for size in sizes:
-        outs.append(grad_qkv[width // dp, start : start + size])
-        start += size
-    grad_qkv = grad_qkv[: width // dp]
     q_cols, k_cols = heads * head_dim // ctx, head_dim // ctx
+    grad_query, grad_key, grad_value, grad_out, *gain_outs = narrow_last(
+        blocks, out_blocks, sizes, (q_cols, k_cols, k_cols)
+    )
     return (
         output,
         input_grad,
-        grad_qkv[:, :q_cols],
-        grad_qkv[:, q_cols : q_cols + k_cols],
-        grad_qkv[:, q_cols + k_cols :],
-        grad_out,
+        grad_query,
+        grad_key.T,
+        grad_value.T,
+        grad_out.T,
         grad_gate,
         grad_up,
         grad_down.T,
-        *outs,
+        *[g.reshape(-1) for g in gain_outs],
     )
 
 

time: 404 us -> 379 us (0.938)
  waiting for transfers between devices: 153 us -> 125 us
  Pallas kernels: 112 us -> 127 us
  starting transfers between devices: 112 us -> 106 us
  local copies, waits for them, and re-layouts: 18.1 us -> 12.8 us
    ppermute x33 -> x36, waiting for transfers between devices: 107 us -> 70.7 us  [shift(): lax.ppermute(value, 'ctx', [(i, (i + step) % size) for i in range(size)])]
    ppermute x33 -> x36, starting transfers between devices: 83.4 us -> 68 us  [shift(): lax.ppermute(value, 'ctx', [(i, (i + step) % size) for i in range(size)])]
    pallas_call x20 -> x26, Pallas kernels: 112 us -> 127 us  [kernel_call(): pl.pallas_call(body, out_shape=[jax.ShapeDtypeStruct(s, t) for s, t in ou...]
    ppermute x38 -> x52, waiting for transfers between devices: 40.1 us -> 54.6 us  [swap(): return lax.ppermute(value, 'dp', [(i, i ^ 1 << bit) for i in range(size)])]
    ppermute x38 -> x52, starting transfers between devices: 17.7 us -> 26.6 us  [swap(): return lax.ppermute(value, 'dp', [(i, i ^ 1 << bit) for i in range(size)])]
    ppermute x6 -> x9, starting transfers between devices: 5.71 us -> 11.7 us  [plane_send(): lax.ppermute(parts[m], 'dp', [(i, i ^ 2 * m) for i in range(size)])]
    unnamed x138 -> x172, local copies, waits for them, and re-layouts: 12 us -> 6.23 us
    ppermute x6 -> x9, waiting for transfers between devices: 5.41 us -> 0.02 us  [plane_send(): lax.ppermute(parts[m], 'dp', [(i, i ^ 2 * m) for i in range(size)])]
  transfers between devices with their start and end apart: 78 -> 97, of which waited for: 34 -> 39; matrix products, arithmetic and copies ran while one was open for 1% -> 1% of each run, Pallas kernels for 22% -> 30%
where the time goes in v2:
time: 379 us; the launch traced here: 374 us
  Pallas kernels  127 us (34%)
  waiting for transfers between devices  125 us (33%)
  starting transfers between devices  106 us (28%)
  local copies, waits for them, and re-layouts  12.8 us (3%)
    pallas_call x26, Pallas kernels, kernel_call(): pl.pallas_call(body, out_shape=[jax.ShapeDtypeStruct(s, t) for s, t in ou...  127 us
    ppermute x36, waiting for transfers between devices, shift(): lax.ppermute(value, 'ctx', [(i, (i + step) % size) for i in range(size)])  70.7 us
    ppermute x36, starting transfers between devices, shift(): lax.ppermute(value, 'ctx', [(i, (i + step) % size) for i in range(size)])  68 us
    ppermute x52, waiting for transfers between devices, swap(): return lax.ppermute(value, 'dp', [(i, i ^ 1 << bit) for i in range(size)])  54.6 us
    ppermute x52, starting transfers between devices, swap(): return lax.ppermute(value, 'dp', [(i, i ^ 1 << bit) for i in range(size)])  26.6 us
    ppermute x9, starting transfers between devices, plane_send(): lax.ppermute(parts[m], 'dp', [(i, i ^ 2 * m) for i in range(size)])  11.7 us
  transfers between devices with their start and end apart: 97, of which 39 were waited for; matrix products, arithmetic and copies ran while one was open for 1% of the time, Pallas kernels for 30%

profile of v2, /device:TPU:0, one launch (start us, length us, event | category | flops | bytes accessed | tf_op | source)
XLA Modules:
  0.0 374.2 jit_solution(4637061694776889328)
XLA Ops:
  33.7 5.0 %collective-permute-start.16 = (bf16[2,36,1728]{2,1,0:T(8,128)(2,1)}, bf16[2,36,1728]{2,1,0:T(8,128)(2,1)S(1)}, u32[]{:S(2)}, u32[]{:S(2)}) collective-permute-start(bf16[2,36,1728]{2,1,0:T(8,128)(2,1)} %get-tuple-element.353), channel_id=1, source_target_pairs={{0,1},{1,2},{2,3},{3,0},{4,5},{5,6},{6,7},{7,4},{8,9},{9,10},{10,1... | collective-permute-start | bytes 746504 | tf_op jit(solution)/shard_map/ppermute | solution.py:65
  42.9 9.0 %collective-permute-done.7.rest_1_.rest_5_ = bf16[160,2688]{1,0:T(8,128)(2,1)S(1)} collective-permute-done((bf16[160,2688]{1,0:T(8,128)(2,1)}, bf16[160,2688]{1,0:T(8,128)(2,1)S(1)}, u32[]{:S(2)}, u32[]{:S(2)}) %collective-permute-start.7) | collective-permute-done | bytes 860192 | tf_op jit(solution)/shard_map/ppermute | solution.py:60
  59.1 5.2 %collective-permute-done.9.rest_3_.rest_7_ = bf16[80,2688]{1,0:T(8,128)(2,1)S(1)} collective-permute-done((bf16[80,2688]{1,0:T(8,128)(2,1)S(1)}, bf16[80,2688]{1,0:T(8,128)(2,1)S(1)}, u32[]{:S(2)}, u32[]{:S(2)}) %collective-permute-start.9) | collective-permute-done | bytes 430112 | tf_op jit(solution)/shard_map/ppermute | solution.py:60
  68.4 5.2 %shard_map.286 = (bf16[128,1152]{1,0:T(8,128)(2,1)}, bf16[128,1024]{1,0:T(8,128)(2,1)}, bf16[128,512]{1,0:T(8,128)(2,1)}, f32[128,1280]{1,0:T(8,128)}, f32[1,115...) custom-call(s32[5]{0:T(128)} %stack.35.where_ref, bf16[128,1152]{1,0:T(8,128)(2,1)} %x_ref.5, ...), custom_call_target="tpu_custom_call" | custom-call | tf_op jit(solution)/shard_map/pallas_call | solution.py:426
  75.7 5.1 %collective-permute-start.19 = (bf16[128,512]{1,0:T(8,128)(2,1)}, bf16[128,512]{1,0:T(8,128)(2,1)S(1)}, u32[]{:S(2)}, u32[]{:S(2)}) collective-permute-start(bf16[128,512]{1,0:T(8,128)(2,1)} %get-tuple-element.383.behind_ref.rest_0_.rest_14_), channel_id=1, source_target_pairs={{0,1},{1,2},{2,3},{3,0},{4,5},{5,6},{6,7},{7,4},{8,9},{9,10},{10,1... | collective-permute-start | bytes 393224 | tf_op jit(solution)/shard_map/ppermute | solution.py:65
  86.1 4.8 %collective-permute-done.20.rest_2_.rest_16_ = bf16[128,512]{1,0:T(8,128)(2,1)S(1)} collective-permute-done((bf16[128,512]{1,0:T(8,128)(2,1)}, bf16[128,512]{1,0:T(8,128)(2,1)S(1)}, u32[]{:S(2)}, u32[]{:S(2)}) %collective-permute-start.20) | collective-permute-done | bytes 131104 | tf_op jit(solution)/shard_map/ppermute | solution.py:65
  100.6 4.7 %shard_map.288 = (f32[2,256,256]{2,1,0:T(8,128)}, bf16[128,1024]{1,0:T(8,128)(2,1)}, f32[128,1152]{1,0:T(8,128)}, f32[128,1152]{1,0:T(8,128)}, bf16[128,1152]{1,0:T(8,128)(2,1)}) custom-call(s32[5]{0:T(128)} %stack.35.where_ref, bf16[128,1152]{1,0:T(8,128)(2,1)} %x_ref.5, bf16[128,1024]{1,0:T(8,128)(2,1)} %get-tuple-element.380.query_ref, ...), custom_call_target="tpu_custom_call" | custom-call | tf_op jit(solution)/shard_map/pallas_call | solution.py:426
  117.1 7.6 %collective-permute-done.30.rest_11_ = bf16[144,1728]{1,0:T(8,128)(2,1)S(1)} collective-permute-done((bf16[144,1728]{1,0:T(8,128)(2,1)}, bf16[144,1728]{1,0:T(8,128)(2,1)S(1)}, u32[]{:S(2)}, u32[]{:S(2)}) %collective-permute-start.30) | collective-permute-done | bytes 497696 | tf_op jit(solution)/shard_map/ppermute | solution.py:60
  132.6 9.8 %collective-permute-done.34.rest_4_ = bf16[2,64,1728]{2,1,0:T(8,128)(2,1)S(1)} collective-permute-done((bf16[2,64,1728]{2,1,0:T(8,128)(2,1)}, bf16[2,64,1728]{2,1,0:T(8,128)(2,1)S(1)}, u32[]{:S(2)}, u32[]{:S(2)}) %collective-permute-start.34) | collective-permute-done | bytes 442400 | tf_op jit(solution)/shard_map/ppermute | solution.py:60
  149.8 6.6 %collective-permute-done.40.rest_14_ = bf16[64,1728]{1,0:T(8,128)(2,1)S(1)} collective-permute-done((bf16[64,1728]{1,0:T(8,128)(2,1)S(1)}, bf16[64,1728]{1,0:T(8,128)(2,1)S(1)}, u32[]{:S(2)}, u32[]{:S(2)}) %collective-permute-start.40) | collective-permute-done | bytes 221216 | tf_op jit(solution)/shard_map/ppermute | solution.py:60
  164.7 12.1 %shard_map.291 = (bf16[384,1152]{1,0:T(8,128)(2,1)}, bf16[384,1792]{1,0:T(8,128)(2,1)}, bf16[2,384,1728]{2,1,0:T(8,128)(2,1)}, f32[128,1152]{1,0:T(8,128)}, bf16...) custom-call(s32[5]{0:T(128)} %stack.35.where_ref, bf16[2,144,1728]{2,1,0:T(8,128)(2,1)} %shard_map.285.rest_0_, ...), custom_call_target="tpu_custom_call" | custom-call | tf_op jit(solution)/shard_map/pallas_call | solution.py:426
  179.1 8.0 %shard_map.292 = (bf16[128,1152]{1,0:T(8,128)(2,1)}, bf16[128,1792]{1,0:T(8,128)(2,1)}, bf16[2,128,1728]{2,1,0:T(8,128)(2,1)}, bf16[128,1152]{1,0:T(8,128)(2,1)}) custom-call(s32[5]{0:T(128)} %stack.35.where_ref, bf16[2,144,1728]{2,1,0:T(8,128)(2,1)} %shard_map.285.rest_0_, bf16[2,144,1728]{2,1,0:T(8,128)(2,1)} %copy-done.3, ...), custom_call_target="tpu_custom_call" | custom-call | tf_op jit(solution)/shard_map/pallas_call | solution.py:426
  187.2 5.9 %collective-permute-done.49.rest_2_ = bf16[128,1152]{1,0:T(8,128)(2,1)S(1)} collective-permute-done((bf16[128,1152]{1,0:T(8,128)(2,1)}, bf16[128,1152]{1,0:T(8,128)(2,1)S(1)}, u32[]{:S(2)}, u32[]{:S(2)}) %collective-permute-start.49) | collective-permute-done | bytes 294944 | tf_op jit(solution)/shard_map/ppermute | solution.py:65
  197.3 13.2 %collective-permute-done.50.rest_3_ = bf16[128,1152]{1,0:T(8,128)(2,1)S(1)} collective-permute-done((bf16[128,1152]{1,0:T(8,128)(2,1)}, bf16[128,1152]{1,0:T(8,128)(2,1)S(1)}, u32[]{:S(2)}, u32[]{:S(2)}) %collective-permute-start.50) | collective-permute-done | bytes 294944 | tf_op jit(solution)/shard_map/ppermute | solution.py:65
  218.7 8.1 %collective-permute-done.56.rest_21_ = bf16[128,1152]{1,0:T(8,128)(2,1)S(1)} collective-permute-done((bf16[128,1152]{1,0:T(8,128)(2,1)}, bf16[128,1152]{1,0:T(8,128)(2,1)S(1)}, u32[]{:S(2)}, u32[]{:S(2)}) %collective-permute-start.56) | collective-permute-done | bytes 294944 | tf_op jit(solution)/shard_map/ppermute | solution.py:65
  232.7 12.5 %shard_map.294 = (bf16[384,1152]{1,0:T(8,128)(2,1)}, bf16[2,384,1792]{2,1,0:T(8,128)(2,1)}, f32[128,1152]{1,0:T(8,128)}, bf16[128,1152]{1,0:T(8,128)(2,1)}, bf16[128,1152]{1,0:T(8,128)(2,1)}) custom-call(s32[5]{0:T(128)} %stack.35.where_ref, bf16[2,384,1728]{2,1,0:T(8,128)(2,1)} %get-tuple-element.507.slopes_ref, bf16[2,144,1728]{2,1,0:T(8,128)(2,1)} %shard_map.285.rest_0_, ...), custom_call_target="tpu_custom_call" | custom-call | tf_op jit(solution)/shard_map/pallas_call | solution.py:426
  248.6 8.5 %collective-permute-start.61 = (bf16[128,1152]{1,0:T(8,128)(2,1)}, bf16[128,1152]{1,0:T(8,128)(2,1)}, u32[]{:S(2)}, u32[]{:S(2)}) collective-permute-start(bf16[128,1152]{1,0:T(8,128)(2,1)} %get-tuple-element.522), channel_id=1, source_target_pairs={{0,1},{1,2},{2,3},{3,0},{4,5},{5,6},{6,7},{7,4},{8,9},{9,10},{10,1... | collective-permute-start | bytes 884744 | tf_op jit(solution)/shard_map/ppermute | solution.py:65
  257.1 9.5 %shard_map.295 = (bf16[128,1152]{1,0:T(8,128)(2,1)}, bf16[2,128,1792]{2,1,0:T(8,128)(2,1)}, bf16[128,1152]{1,0:T(8,128)(2,1)}) custom-call(s32[5]{0:T(128)} %stack.35.where_ref, bf16[2,128,1728]{2,1,0:T(8,128)(2,1)} %get-tuple-element.504.slopes_ref, bf16[2,144,1728]{2,1,0:T(8,128)(2,1)} %shard_map.285.rest_0_, bf16[2,144,1728]{2,1,0:T(8,128)(2,1)} %copy-done.3, ...), custom_call_target="tpu_custom_call" | custom-call | tf_op jit(solution)/shard_map/pallas_call | solution.py:426
  266.7 7.1 %shard_map.296 = (bf16[1,160,1792]{2,1,0:T(8,128)(2,1)}, bf16[1,160,1792]{2,1,0:T(8,128)(2,1)}, bf16[1,128,1792]{2,1,0:T(8,128)(2,1)}, bf16[1,128,1792]{2,1,0:T(8,128)(2,1)}) custom-call(s32[5]{0:T(128)} %stack.35.where_ref, bf16[384,1152]{1,0:T(8,128)(2,1)} %get-tuple-element.524.rest_0_, bf16[128,1152]{1,0:T(8,128)(2,1)} %copy-done.22, ...), custom_call_target="tpu_custom_call" | custom-call | tf_op jit(solution)/shard_map/pallas_call | solution.py:426
  277.4 10.7 %shard_map.297 = (bf16[2,160,1792]{2,1,0:T(8,128)(2,1)}, bf16[2,160,1792]{2,1,0:T(8,128)(2,1)}, bf16[2,128,1792]{2,1,0:T(8,128)(2,1)}, bf16[2,128,1792]{2,1,0:T(8,128)(2,1)}) custom-call(s32[5]{0:T(128)} %stack.35.where_ref, bf16[384,1152]{1,0:T(8,128)(2,1)} %get-tuple-element.490.rest_0_, bf16[128,1152]{1,0:T(8,128)(2,1)} %get-tuple-element.491.rest_1_, ...), custom_call_target="tpu_custom_call" | custom-call | tf_op jit(solution)/shard_map/pallas_call | solution.py:426
  295.1 7.0 %shard_map.298 = (f32[128,1152]{1,0:T(8,128)}, bf16[128,1152]{1,0:T(8,128)(2,1)}, bf16[128,1024]{1,0:T(8,128)(2,1)}, f32[1,1152]{1,0:T(1,128)}, f32[1,1152]{1,0:...) custom-call(s32[5]{0:T(128)} %stack.35.where_ref, ...), custom_call_target="tpu_custom_call" | custom-call | tf_op jit(solution)/shard_map/pallas_call | solution.py:426
  308.9 7.1 %collective-permute-done.69.rest_2_ = bf16[128,512]{1,0:T(8,128)(2,1)S(1)} collective-permute-done((bf16[128,512]{1,0:T(8,128)(2,1)}, bf16[128,512]{1,0:T(8,128)(2,1)S(1)}, u32[]{:S(2)}, u32[]{:S(2)}) %collective-permute-start.69) | collective-permute-done | bytes 131104 | tf_op jit(solution)/shard_map/ppermute | solution.py:65
  322.6 5.1 %shard_map.301 = (bf16[3,80,1792]{2,1,0:T(8,128)(2,1)}, bf16[3,80,1792]{2,1,0:T(8,128)(2,1)}, bf16[3,64,1792]{2,1,0:T(8,128)(2,1)}, bf16[3,64,1792]{2,1,0:T(8,128)(2,1)}) custom-call(s32[5]{0:T(128)} %stack.35.where_ref, bf16[2,160,1792]{2,1,0:T(8,128)(2,1)} %get-tuple-element.588.rest_0_, bf16[2,160,1792]{2,1,0:T(8,128)(2,1)} %copy-done.23, ...), custom_call_target="tpu_custom_call" | custom-call | tf_op jit(solution)/shard_map/pallas_call | solution.py:426
  327.6 6.2 %shard_map.300 = (bf16[128,1152]{1,0:T(8,128)(2,1)}, bf16[144,384]{1,0:T(8,128)(2,1)}, bf16[144,384]{1,0:T(8,128)(2,1)}, bf16[144,384]{1,0:T(8,128)(2,1)}, bf16[144,384]{1,0:T(8,128)(2,1)}) custom-call(s32[5]{0:T(128)} %stack.35.where_ref, f32[128,1280]{1,0:T(8,128)} %get-tuple-element.500.raw_ref, bf16[128,1024]{1,0:T(8,128)(2,1)} %get-tuple-element.567.query_ref, ...), custom_call_target="tpu_custom_call" | custom-call | tf_op jit(solution)/shard_map/pallas_call | solution.py:426
  (382 shorter events, 188.1 us)
Async XLA Ops:
  10.1 17.3 %collective-permute-start.1 = (bf16[40,2688]{1,0:T(8,128)(2,1)S(1)}, bf16[40,2688]{1,0:T(8,128)(2,1)S(1)}, u32[]{:S(2)}, u32[]{:S(2)}) collective-permute-start(bf16[40,2688]{1,0:T(8,128)(2,1)S(1)} %copy-done.27), channel_id=1, source_target_pairs={{0,2},{1,3},{2,0},{3,1},{4,6},{5,7},{6,4},{7,5},{8,10},{9,11},{10,... | collective-permute-start | bytes 645128 | tf_op jit(solution)/shard_map/ppermute | solution.py:65
  30.7 21.2 %collective-permute-start.7 = (bf16[160,2688]{1,0:T(8,128)(2,1)}, bf16[160,2688]{1,0:T(8,128)(2,1)S(1)}, u32[]{:S(2)}, u32[]{:S(2)}) collective-permute-start(bf16[160,2688]{1,0:T(8,128)(2,1)} %shard_map.284.rest_0_.rest_4_), channel_id=1, source_target_pairs={{0,8},{4,12},{8,0},{12,4},{16,24},{20,28},{24,16},{28,20},{1,9},{5... | collective-permute-start | bytes 2580488 | tf_op jit(solution)/shard_map/ppermute | solution.py:60
  32.2 20.9 %collective-permute-start.8 = (bf16[160,2688]{1,0:T(8,128)(2,1)}, bf16[160,2688]{1,0:T(8,128)(2,1)S(1)}, u32[]{:S(2)}, u32[]{:S(2)}) collective-permute-start(bf16[160,2688]{1,0:T(8,128)(2,1)} %shard_map.284.rest_0_.rest_4_), channel_id=1, source_target_pairs={{0,16},{4,20},{8,24},{12,28},{16,0},{20,4},{24,8},{28,12},{1,17},{... | collective-permute-start | bytes 2580488 | tf_op jit(solution)/shard_map/ppermute | solution.py:60
  33.7 21.0 %collective-permute-start.16 = (bf16[2,36,1728]{2,1,0:T(8,128)(2,1)}, bf16[2,36,1728]{2,1,0:T(8,128)(2,1)S(1)}, u32[]{:S(2)}, u32[]{:S(2)}) collective-permute-start(bf16[2,36,1728]{2,1,0:T(8,128)(2,1)} %get-tuple-element.353), channel_id=1, source_target_pairs={{0,1},{1,2},{2,3},{3,0},{4,5},{5,6},{6,7},{7,4},{8,9},{9,10},{10,1... | collective-permute-start | bytes 746504 | tf_op jit(solution)/shard_map/ppermute | solution.py:65
  38.7 19.9 %collective-permute-start.17 = (bf16[2,36,1728]{2,1,0:T(8,128)(2,1)}, bf16[2,36,1728]{2,1,0:T(8,128)(2,1)S(1)}, u32[]{:S(2)}, u32[]{:S(2)}) collective-permute-start(bf16[2,36,1728]{2,1,0:T(8,128)(2,1)} %get-tuple-element.354), channel_id=1, source_target_pairs={{0,2},{1,3},{2,0},{3,1},{4,6},{5,7},{6,4},{7,5},{8,10},{9,11},{10,... | collective-permute-start | bytes 746504 | tf_op jit(solution)/shard_map/ppermute | solution.py:65
  40.4 18.2 %collective-permute-start.18 = (bf16[2,36,1728]{2,1,0:T(8,128)(2,1)}, bf16[2,36,1728]{2,1,0:T(8,128)(2,1)S(1)}, u32[]{:S(2)}, u32[]{:S(2)}) collective-permute-start(bf16[2,36,1728]{2,1,0:T(8,128)(2,1)} %get-tuple-element.355), channel_id=1, source_target_pairs={{0,3},{1,0},{2,1},{3,2},{4,7},{5,4},{6,5},{7,6},{8,11},{9,8},{10,9... | collective-permute-start | bytes 746504 | tf_op jit(solution)/shard_map/ppermute | solution.py:65
  73.5 31.8 %collective-permute-start.22 = (bf16[2,144,1728]{2,1,0:T(8,128)(2,1)S(1)}, bf16[2,144,1728]{2,1,0:T(8,128)(2,1)S(1)}, u32[]{:S(2)}, u32[]{:S(2)}) collective-permute-start(bf16[2,144,1728]{2,1,0:T(8,128)(2,1)S(1)} %copy-done.2), channel_id=1, source_target_pairs={{0,8},{4,12},{8,0},{12,4},{16,24},{20,28},{24,16},{28,20},{1,9},{5... | collective-permute-start | bytes 2985992 | tf_op jit(solution)/shard_map/ppermute | solution.py:60
  75.1 31.1 %collective-permute-start.23 = (bf16[2,144,1728]{2,1,0:T(8,128)(2,1)S(1)}, bf16[2,144,1728]{2,1,0:T(8,128)(2,1)}, u32[]{:S(2)}, u32[]{:S(2)}) collective-permute-start(bf16[2,144,1728]{2,1,0:T(8,128)(2,1)S(1)} %copy-done.2), channel_id=1, source_target_pairs={{0,16},{4,20},{8,24},{12,28},{16,0},{20,4},{24,8},{28,12},{1,17},{... | collective-permute-start | bytes 2985992 | tf_op jit(solution)/shard_map/ppermute | solution.py:60
  108.0 20.8 %collective-permute-start.29 = (bf16[2,144,1728]{2,1,0:T(8,128)(2,1)S(1)}, bf16[2,144,1728]{2,1,0:T(8,128)(2,1)}, u32[]{:S(2)}, u32[]{:S(2)}) collective-permute-start(bf16[2,144,1728]{2,1,0:T(8,128)(2,1)S(1)} %copy-done.2), channel_id=1, source_target_pairs={{0,4},{4,0},{8,12},{12,8},{16,20},{20,16},{24,28},{28,24},{1,5},{5... | collective-permute-start | bytes 2985992 | tf_op jit(solution)/shard_map/ppermute | solution.py:60
  128.9 18.2 %collective-permute-start.35 = (bf16[2,144,1728]{2,1,0:T(8,128)(2,1)S(1)}, bf16[2,144,1728]{2,1,0:T(8,128)(2,1)S(1)}, u32[]{:S(2)}, u32[]{:S(2)}) collective-permute-start(bf16[2,144,1728]{2,1,0:T(8,128)(2,1)S(1)} %collective-permute-done.22.rest_1_), channel_id=1, source_target_pairs={{0,4},{4,0},{8,12},{12,8},{16,20},{20,16},{24,28},{28,24},{1,5},{5... | collective-permute-start | bytes 2985992 | tf_op jit(solution)/shard_map/ppermute | solution.py:60
  129.0 18.1 %collective-permute-start.36 = (bf16[2,144,1728]{2,1,0:T(8,128)(2,1)}, bf16[2,144,1728]{2,1,0:T(8,128)(2,1)S(1)}, u32[]{:S(2)}, u32[]{:S(2)}) collective-permute-start(bf16[2,144,1728]{2,1,0:T(8,128)(2,1)} %collective-permute-done.23.rest_2_), channel_id=1, source_target_pairs={{0,4},{4,0},{8,12},{12,8},{16,20},{20,16},{24,28},{28,24},{1,5},{5... | collective-permute-start | bytes 2985992 | tf_op jit(solution)/shard_map/ppermute | solution.py:60
  193.0 17.5 %collective-permute-start.53 = (bf16[384,1792]{1,0:T(8,128)(2,1)S(1)}, bf16[384,1792]{1,0:T(8,128)(2,1)S(1)}, u32[]{:S(2)}, u32[]{:S(2)}) collective-permute-start(bf16[384,1792]{1,0:T(8,128)(2,1)S(1)} %copy-done.20), channel_id=1, source_target_pairs={{0,4},{4,0},{8,12},{12,8},{16,20},{20,16},{24,28},{28,24},{1,5},{5... | collective-permute-start | bytes 4128776 | tf_op jit(solution)/shard_map/ppermute | solution.py:60
  193.1 17.5 %collective-permute-start.51 = (bf16[384,1152]{1,0:T(8,128)(2,1)S(1)}, bf16[384,1152]{1,0:T(8,128)(2,1)S(1)}, u32[]{:S(2)}, u32[]{:S(2)}) collective-permute-start(bf16[384,1152]{1,0:T(8,128)(2,1)S(1)} %copy-done.25), channel_id=1, source_target_pairs={{0,4},{4,0},{8,12},{12,8},{16,20},{20,16},{24,28},{28,24},{1,5},{5... | collective-permute-start | bytes 2654216 | tf_op jit(solution)/shard_map/ppermute | solution.py:60
  245.7 28.1 %collective-permute-start.59 = (bf16[2,384,1792]{2,1,0:T(8,128)(2,1)}, bf16[2,384,1792]{2,1,0:T(8,128)(2,1)S(1)}, u32[]{:S(2)}, u32[]{:S(2)}) collective-permute-start(bf16[2,384,1792]{2,1,0:T(8,128)(2,1)} %get-tuple-element.542.rest_4_), channel_id=1, source_target_pairs={{0,4},{4,0},{8,12},{12,8},{16,20},{20,16},{24,28},{28,24},{1,5},{5... | collective-permute-start | bytes 8257544 | tf_op jit(solution)/shard_map/ppermute | solution.py:60
  245.7 21.0 %collective-permute-start.62 = (bf16[384,1152]{1,0:T(8,128)(2,1)}, bf16[384,1152]{1,0:T(8,128)(2,1)}, u32[]{:S(2)}, u32[]{:S(2)}) collective-permute-start(bf16[384,1152]{1,0:T(8,128)(2,1)} %get-tuple-element.524.rest_0_), channel_id=1, source_target_pairs={{0,4},{4,0},{8,12},{12,8},{16,20},{20,16},{24,28},{28,24},{1,5},{5... | collective-permute-start | bytes 2654216 | tf_op jit(solution)/shard_map/ppermute | solution.py:60
  246.2 20.5 %collective-permute-start.63 = (bf16[128,1152]{1,0:T(8,128)(2,1)S(1)}, bf16[128,1152]{1,0:T(8,128)(2,1)}, u32[]{:S(2)}, u32[]{:S(2)}) collective-permute-start(bf16[128,1152]{1,0:T(8,128)(2,1)S(1)} %collective-permute-done.58.rest_20_.rest_1_), channel_id=1, source_target_pairs={{0,4},{4,0},{8,12},{12,8},{16,20},{20,16},{24,28},{28,24},{1,5},{5... | collective-permute-start | bytes 884744 | tf_op jit(solution)/shard_map/ppermute | solution.py:60
  246.2 27.6 %collective-permute-start.60 = (bf16[128,1152]{1,0:T(8,128)(2,1)}, bf16[128,1152]{1,0:T(8,128)(2,1)S(1)}, u32[]{:S(2)}, u32[]{:S(2)}) collective-permute-start(bf16[128,1152]{1,0:T(8,128)(2,1)} %get-tuple-element.521), channel_id=1, source_target_pairs={{0,3},{1,0},{2,1},{3,2},{4,7},{5,4},{6,5},{7,6},{8,11},{9,8},{10,9... | collective-permute-start | bytes 884744 | tf_op jit(solution)/shard_map/ppermute | solution.py:65
  248.6 25.2 %collective-permute-start.61 = (bf16[128,1152]{1,0:T(8,128)(2,1)}, bf16[128,1152]{1,0:T(8,128)(2,1)}, u32[]{:S(2)}, u32[]{:S(2)}) collective-permute-start(bf16[128,1152]{1,0:T(8,128)(2,1)} %get-tuple-element.522), channel_id=1, source_target_pairs={{0,1},{1,2},{2,3},{3,0},{4,5},{5,6},{6,7},{7,4},{8,9},{9,10},{10,1... | collective-permute-start | bytes 884744 | tf_op jit(solution)/shard_map/ppermute | solution.py:65
  274.8 17.9 %collective-permute-start.65 = (bf16[1,160,1792]{2,1,0:T(8,128)(2,1)}, bf16[1,160,1792]{2,1,0:T(8,128)(2,1)S(1)}, u32[]{:S(2)}, u32[]{:S(2)}) collective-permute-start(bf16[1,160,1792]{2,1,0:T(8,128)(2,1)} %get-tuple-element.536), channel_id=1, source_target_pairs={{0,8},{4,12},{8,0},{12,4},{16,24},{20,28},{24,16},{28,20},{1,9},{5... | collective-permute-start | bytes 1720328 | tf_op jit(solution)/shard_map/ppermute | solution.py:60
  275.3 17.4 %collective-permute-start.66 = (bf16[1,128,1792]{2,1,0:T(8,128)(2,1)}, bf16[1,128,1792]{2,1,0:T(8,128)(2,1)}, u32[]{:S(2)}, u32[]{:S(2)}) collective-permute-start(bf16[1,128,1792]{2,1,0:T(8,128)(2,1)} %get-tuple-element.538), channel_id=1, source_target_pairs={{0,16},{4,20},{8,24},{12,28},{16,0},{20,4},{24,8},{28,12},{1,17},{... | collective-permute-start | bytes 1376264 | tf_op jit(solution)/shard_map/ppermute | solution.py:60
  292.7 26.3 %collective-permute-start.71 = (bf16[2,160,1792]{2,1,0:T(8,128)(2,1)}, bf16[2,160,1792]{2,1,0:T(8,128)(2,1)S(1)}, u32[]{:S(2)}, u32[]{:S(2)}) collective-permute-start(bf16[2,160,1792]{2,1,0:T(8,128)(2,1)} %get-tuple-element.557), channel_id=1, source_target_pairs={{0,8},{4,12},{8,0},{12,4},{16,24},{20,28},{24,16},{28,20},{1,9},{5... | collective-permute-start | bytes 3440648 | tf_op jit(solution)/shard_map/ppermute | solution.py:60
  294.2 21.8 %collective-permute-start.72 = (bf16[2,128,1792]{2,1,0:T(8,128)(2,1)}, bf16[2,128,1792]{2,1,0:T(8,128)(2,1)S(1)}, u32[]{:S(2)}, u32[]{:S(2)}) collective-permute-start(bf16[2,128,1792]{2,1,0:T(8,128)(2,1)} %get-tuple-element.558), channel_id=1, source_target_pairs={{0,16},{4,20},{8,24},{12,28},{16,0},{20,4},{24,8},{28,12},{1,17},{... | collective-permute-start | bytes 2752520 | tf_op jit(solution)/shard_map/ppermute | solution.py:60
  335.8 23.5 %collective-permute-start.78 = (bf16[3,80,1792]{2,1,0:T(8,128)(2,1)}, bf16[3,80,1792]{2,1,0:T(8,128)(2,1)S(1)}, u32[]{:S(2)}, u32[]{:S(2)}) collective-permute-start(bf16[3,80,1792]{2,1,0:T(8,128)(2,1)} %get-tuple-element.603), channel_id=1, source_target_pairs={{0,16},{4,20},{8,24},{12,28},{16,0},{20,4},{24,8},{28,12},{1,17},{... | collective-permute-start | bytes 2580488 | tf_op jit(solution)/shard_map/ppermute | solution.py:60
  338.0 21.3 %collective-permute-start.79 = (bf16[3,64,1792]{2,1,0:T(8,128)(2,1)}, bf16[3,64,1792]{2,1,0:T(8,128)(2,1)S(1)}, u32[]{:S(2)}, u32[]{:S(2)}) collective-permute-start(bf16[3,64,1792]{2,1,0:T(8,128)(2,1)} %get-tuple-element.604), channel_id=1, source_target_pairs={{0,8},{4,12},{8,0},{12,4},{16,24},{20,28},{24,16},{28,20},{1,9},{5... | collective-permute-start | bytes 2064392 | tf_op jit(solution)/shard_map/ppermute | solution.py:60
  (159 other events, 1463.3 us)
